TPU v7x, 32 devices: a whole 2x2x4 slice. The times are simulated.
32 devices in a mesh: dp: 16 (over z, y, core), fsdp: 2 (over x).
Axes of the slice: x: 2, y: 2, z: 4, core: 2. Of those that a mesh axis runs over, the one named last changes fastest.
Arguments:
- tokens: bfloat16 [32, 2048, 1024], P('dp', 'fsdp'), may hold values from -6 to 6
- lengths: int32 [32], P('dp'), may hold values from 256 to 2048, as said below
- w_query: bfloat16 [1024, 1024], P(('dp', 'fsdp')), may hold values from -0.1875 to 0.1875
- w_key: bfloat16 [1024, 1024], P(('dp', 'fsdp')), may hold values from -0.1875 to 0.1875
- w_value: bfloat16 [1024, 1024], P(('dp', 'fsdp')), may hold values from -0.1875 to 0.1875
- w_gate: bfloat16 [1024, 1024], P(('dp', 'fsdp')), may hold values from -0.1875 to 0.1875
- out_gain: bfloat16 [1024], P(('dp', 'fsdp')), may hold values from 0.5 to 1.5
- w_out: bfloat16 [1024, 1024], P(('dp', 'fsdp')), may hold values from -0.1875 to 0.1875
- w_one: bfloat16 [1024, 2816], P(('dp', 'fsdp')), may hold values from -0.1875 to 0.1875
- w_two: bfloat16 [1024, 2816], P(('dp', 'fsdp')), may hold values from -0.1875 to 0.1875
- w_three: bfloat16 [2816, 1024], P(('dp', 'fsdp')), may hold values from -0.109375 to 0.109375
- cotangent: bfloat16 [32, 2048, 1024], P('dp', 'fsdp'), may hold values from -6 to 6
Outputs:
- layer_out: bfloat16 [32, 2048, 1024], P('dp', 'fsdp')
- input_grad: float32 [32, 2048, 1024], P('dp', 'fsdp')
- grad_query: float32 [1024, 1024], P(('dp', 'fsdp'))
- grad_key: float32 [1024, 1024], P(('dp', 'fsdp'))
- grad_value: float32 [1024, 1024], P(('dp', 'fsdp'))
- grad_gate: float32 [1024, 1024], P(('dp', 'fsdp'))
- grad_gain: float32 [1024], P(('dp', 'fsdp'))
- grad_out: float32 [1024, 1024], P(('dp', 'fsdp'))
- grad_one: float32 [1024, 2816], P(('dp', 'fsdp'))
- grad_two: float32 [1024, 2816], P(('dp', 'fsdp'))
- grad_three: float32 [2816, 1024], P(('dp', 'fsdp'))
Inputs may be any that keep to these rules, and one draw needn't show every extreme that they name: `lengths`: the 2 sequences on one index of dp include at least one whose length is the full 2048.
All inputs are finite; a program needn't handle non-finite values.
Results may differ from a plain program's by a relative error of at most 0.014.
Values may be sent and summed in bfloat16 or wider, within the bound.
A program may use at most 232 MiB of HBM per device.

v0:
```python
import jax
import jax.numpy as jnp
from jax import lax
from jax.sharding import PartitionSpec as P

HD = 64
H = 16
BLOCK = 256


norm_epsilon = 1e-06


def carried_in(x, axis, combine, identity, reverse):
    length, position = (lax.axis_size(axis), lax.axis_index(axis))
    everything = lax.all_gather(x.astype(jnp.bfloat16), axis)
    start = jnp.broadcast_to(jnp.asarray(identity, x.dtype), x.shape)

    def hop(k, before):
        at = length - 1 - k if reverse else k
        reached = at > position if reverse else at < position
        new = combine(before, everything[at].astype(x.dtype))
        return jnp.where(reached, new, before)

    return lax.fori_loop(0, length, hop, start)


def add_states(earlier, later):
    return earlier + later


def simple_norm(values):
    rms_scale = lax.rsqrt(jnp.mean(values * values, axis=-1, keepdims=True) + norm_epsilon)
    return (values * rms_scale, rms_scale)


def norm_back(values, rms_scale, upstream):
    inner_mean = jnp.mean(upstream * values, axis=-1, keepdims=True)
    return rms_scale * (upstream - values * (rms_scale * rms_scale) * inner_mean)


def project(left_side, right_side):
    return jnp.dot(left_side, right_side, preferred_element_type=jnp.float32)


def project_back(left_side, right_side):
    return lax.dot_general(
        left_side, right_side, (((1,), (1,)), ((), ())), preferred_element_type=jnp.float32
    )


def weight_term(left_side, right_side):
    return lax.dot_general(
        left_side, right_side, (((0,), (0,)), ((), ())), preferred_element_type=jnp.float32
    )


def einsum_wide(pattern, left_side, right_side):
    return jnp.einsum(pattern, left_side, right_side, preferred_element_type=jnp.float32)


def silu_slope(pre_rows):
    logistic = jax.nn.sigmoid(pre_rows)
    return logistic * (1.0 + pre_rows * (1.0 - logistic))


def local_prefix(states):
    leading = jnp.zeros_like(states[:, :1])
    return jnp.concatenate([leading, jnp.cumsum(states[:, :-1], axis=1)], axis=1)


def local_suffix(states):
    trailing = jnp.zeros_like(states[:, :1])
    later_sum = jnp.flip(jnp.cumsum(jnp.flip(states[:, 1:], axis=1), axis=1), axis=1)
    return jnp.concatenate([later_sum, trailing], axis=1)


def to_tiles(rows, seq_count):
    return rows.reshape(seq_count, -1, BLOCK, H, HD)


def column_term(left_side, right_side):
    return weight_term(left_side, right_side)


def shards(
    tokens,
    lengths,
    w_query,
    w_key,
    w_value,
    w_gate,
    out_gain,
    w_out,
    w_one,
    w_two,
    w_three,
    cotangent,
):
    seq_count, local_length, model_width = tokens.shape
    row_count = seq_count * local_length
    hidden_width = w_one.shape[1]
    causal = (jnp.arange(BLOCK)[:, None] >= jnp.arange(BLOCK)[None, :]).astype(jnp.float32)
    positions = lax.axis_index("fsdp") * local_length + jnp.arange(local_length, dtype=jnp.int32)
    valid_rows = (positions[None, :] < lengths[:, None]).astype(jnp.float32).reshape(row_count, 1)
    inputs = tokens.reshape(row_count, model_width).astype(jnp.float32)
    full_query, full_key, full_value, full_gate, full_gain, full_out = (
        lax.all_gather(w_query, ("dp", "fsdp"), axis=0, tiled=True),
        lax.all_gather(w_key, ("dp", "fsdp"), axis=0, tiled=True),
        lax.all_gather(w_value, ("dp", "fsdp"), axis=0, tiled=True),
        lax.all_gather(w_gate, ("dp", "fsdp"), axis=0, tiled=True),
        lax.all_gather(out_gain, ("dp", "fsdp"), axis=0, tiled=True),
        lax.all_gather(w_out, ("dp", "fsdp"), axis=0, tiled=True),
    )
    normed_one, scale_one = simple_norm(inputs)
    normed_low = normed_one.astype(jnp.bfloat16)
    pre_query = project(normed_low, full_query)
    pre_key = project(normed_low, full_key)
    pre_value = project(normed_low, full_value)
    pre_gate = project(normed_low, full_gate)
    query_tiles = to_tiles(jax.nn.silu(pre_query).astype(jnp.bfloat16), seq_count)
    key_tiles = to_tiles(jax.nn.silu(pre_key).astype(jnp.bfloat16), seq_count)
    value_tiles = to_tiles(pre_value.astype(jnp.bfloat16), seq_count)
    gate_rows = jax.nn.sigmoid(pre_gate)
    states = einsum_wide("bnjhd,bnjhe->bnhde", key_tiles, value_tiles)
    incoming = carried_in(
        jnp.sum(states, axis=1), "fsdp", add_states, jnp.zeros_like(states[:, 0]), False
    )
    prefix_low = (local_prefix(states) + incoming[:, None]).astype(jnp.bfloat16)
    scores_low = (einsum_wide("bnihd,bnjhd->bnhij", query_tiles, key_tiles) * causal).astype(
        jnp.bfloat16
    )
    within = einsum_wide("bnhij,bnjhe->bnihe", scores_low, value_tiles)
    carried = einsum_wide("bnihd,bnhde->bnihe", query_tiles, prefix_low)
    attended = (within + carried).reshape(row_count, model_width)
    attn_hat, scale_attn = simple_norm(attended)
    mixed_low = (attn_hat * full_gain * gate_rows).astype(jnp.bfloat16)
    residual = inputs + project(mixed_low, full_out)
    full_one, full_two, full_three = (
        lax.all_gather(w_one, ("dp", "fsdp"), axis=0, tiled=True),
        lax.all_gather(w_two, ("dp", "fsdp"), axis=0, tiled=True),
        lax.all_gather(w_three, ("dp", "fsdp"), axis=0, tiled=True),
    )
    normed_two, scale_two = simple_norm(residual)
    normed_two_low = normed_two.astype(jnp.bfloat16)
    up_one = project(normed_two_low, full_one)
    up_two = project(normed_two_low, full_two)
    glu_rows = (up_one * up_two).astype(jnp.bfloat16)
    block_out = valid_rows * (residual + project(glu_rows, full_three))
    layer_out = block_out.astype(jnp.bfloat16).reshape(seq_count, local_length, model_width)
    back_one, back_two, back_three = (
        lax.all_gather(w_one, ("dp", "fsdp"), axis=0, tiled=True),
        lax.all_gather(w_two, ("dp", "fsdp"), axis=0, tiled=True),
        lax.all_gather(w_three, ("dp", "fsdp"), axis=0, tiled=True),
    )
    again_rows, again_one, again_two = lax.optimization_barrier(
        (normed_two_low, back_one, back_two)
    )
    up_one = project(again_rows, again_one)
    up_two = project(again_rows, again_two)
    upstream = cotangent.reshape(row_count, model_width).astype(jnp.float32) * valid_rows
    upstream_low = upstream.astype(jnp.bfloat16)
    grad_glu = project_back(upstream_low, back_three)
    grad_up_one = (grad_glu * up_two).astype(jnp.bfloat16)
    grad_up_two = (grad_glu * up_one).astype(jnp.bfloat16)
    grad_up_both = jnp.concatenate([grad_up_one, grad_up_two], axis=1)
    grad_normed_two = project_back(grad_up_one, back_one) + project_back(grad_up_two, back_two)
    grad_up_rows = lax.psum_scatter(
        column_term(normed_two_low, grad_up_both), ("dp", "fsdp"), scatter_dimension=0, tiled=True
    )
    grad_three = lax.psum_scatter(
        column_term(glu_rows, upstream_low), ("dp", "fsdp"), scatter_dimension=0, tiled=True
    )
    grad_one = grad_up_rows[:, :hidden_width]
    grad_two = grad_up_rows[:, hidden_width:]
    grad_residual = upstream + norm_back(residual, scale_two, grad_normed_two)
    back_query, back_key, back_value, back_gate, back_gain, back_out = (
        lax.all_gather(w_query, ("dp", "fsdp"), axis=0, tiled=True),
        lax.all_gather(w_key, ("dp", "fsdp"), axis=0, tiled=True),
        lax.all_gather(w_value, ("dp", "fsdp"), axis=0, tiled=True),
        lax.all_gather(w_gate, ("dp", "fsdp"), axis=0, tiled=True),
        lax.all_gather(out_gain, ("dp", "fsdp"), axis=0, tiled=True),
        lax.all_gather(w_out, ("dp", "fsdp"), axis=0, tiled=True),
    )
    again_keys, again_values = lax.optimization_barrier((key_tiles, value_tiles))
    states = einsum_wide("bnjhd,bnjhe->bnhde", again_keys, again_values)
    incoming = carried_in(
        jnp.sum(states, axis=1), "fsdp", add_states, jnp.zeros_like(states[:, 0]), False
    )
    prefix_low = (local_prefix(states) + incoming[:, None]).astype(jnp.bfloat16)
    grad_residual_low = grad_residual.astype(jnp.bfloat16)
    grad_mixed = project_back(grad_residual_low, back_out)
    grad_norm_out = grad_mixed * gate_rows
    grad_gain_term = jnp.sum(grad_norm_out * attn_hat, axis=0)
    grad_pre_gate = (grad_mixed * attn_hat * back_gain * gate_rows * (1.0 - gate_rows)).astype(
        jnp.bfloat16
    )
    grad_attended = norm_back(attended, scale_attn, grad_norm_out * back_gain).astype(jnp.bfloat16)
    grad_tiles = to_tiles(grad_attended, seq_count)
    scores_low = (einsum_wide("bnihd,bnjhd->bnhij", query_tiles, key_tiles) * causal).astype(
        jnp.bfloat16
    )
    grad_scores = (einsum_wide("bnihe,bnjhe->bnhij", grad_tiles, value_tiles) * causal).astype(
        jnp.bfloat16
    )
    grad_prefix = einsum_wide("bnihd,bnihe->bnhde", query_tiles, grad_tiles)
    outgoing = carried_in(
        jnp.sum(grad_prefix, axis=1), "fsdp", add_states, jnp.zeros_like(grad_prefix[:, 0]), True
    )
    grad_states = (local_suffix(grad_prefix) + outgoing[:, None]).astype(jnp.bfloat16)
    grad_queries = einsum_wide("bnhij,bnjhd->bnihd", grad_scores, key_tiles) + einsum_wide(
        "bnihe,bnhde->bnihd", grad_tiles, prefix_low
    )
    grad_keys = einsum_wide("bnhij,bnihd->bnjhd", grad_scores, query_tiles) + einsum_wide(
        "bnjhe,bnhde->bnjhd", value_tiles, grad_states
    )
    grad_values = einsum_wide("bnhij,bnihe->bnjhe", scores_low, grad_tiles) + einsum_wide(
        "bnjhd,bnhde->bnjhe", key_tiles, grad_states
    )
    grad_pre_query = (grad_queries.reshape(row_count, model_width) * silu_slope(pre_query)).astype(
        jnp.bfloat16
    )
    grad_pre_key = (grad_keys.reshape(row_count, model_width) * silu_slope(pre_key)).astype(
        jnp.bfloat16
    )
    grad_pre_value = grad_values.reshape(row_count, model_width).astype(jnp.bfloat16)
    grad_pre_four = jnp.concatenate(
        [grad_pre_query, grad_pre_key, grad_pre_value, grad_pre_gate], axis=1
    )
    grad_normed_one = project_back(grad_pre_query, back_query) + project_back(
        grad_pre_key, back_key
    )
    grad_normed_one = (
        grad_normed_one
        + project_back(grad_pre_value, back_value)
        + project_back(grad_pre_gate, back_gate)
    )
    input_grad = grad_residual + norm_back(inputs, scale_one, grad_normed_one)
    inner = column_term(normed_low, grad_pre_four)
    outer = column_term(mixed_low, grad_residual_low)
    grad_attn_rows = lax.psum_scatter(
        jnp.concatenate([inner, outer], axis=1), ("dp", "fsdp"), scatter_dimension=0, tiled=True
    )
    grad_gain = lax.psum_scatter(grad_gain_term, ("dp", "fsdp"), scatter_dimension=0, tiled=True)
    grad_query = grad_attn_rows[:, :model_width]
    grad_key = grad_attn_rows[:, model_width : 2 * model_width]
    grad_value = grad_attn_rows[:, 2 * model_width : 3 * model_width]
    grad_gate = grad_attn_rows[:, 3 * model_width : 4 * model_width]
    grad_out = grad_attn_rows[:, 4 * model_width :]
    return (
        layer_out,
        input_grad.reshape(seq_count, local_length, model_width),
        grad_query,
        grad_key,
        grad_value,
        grad_gate,
        grad_gain,
        grad_out,
        grad_one,
        grad_two,
        grad_three,
    )


def solution(mesh):
    in_specs = (
        P("dp", "fsdp", None),
        P("dp"),
        P(("dp", "fsdp"), None),
        P(("dp", "fsdp"), None),
        P(("dp", "fsdp"), None),
        P(("dp", "fsdp"), None),
        P(("dp", "fsdp")),
        P(("dp", "fsdp"), None),
        P(("dp", "fsdp"), None),
        P(("dp", "fsdp"), None),
        P(("dp", "fsdp"), None),
        P("dp", "fsdp", None),
    )
    out_specs = (
        P("dp", "fsdp", None),
        P("dp", "fsdp", None),
        P(("dp", "fsdp"), None),
        P(("dp", "fsdp"), None),
        P(("dp", "fsdp"), None),
        P(("dp", "fsdp"), None),
        P(("dp", "fsdp")),
        P(("dp", "fsdp"), None),
        P(("dp", "fsdp"), None),
        P(("dp", "fsdp"), None),
        P(("dp", "fsdp"), None),
    )
    return jax.shard_map(shards, mesh=mesh, in_specs=in_specs, out_specs=out_specs, check_vma=False)
```

profile of v0, /device:TPU:0, one launch (start us, length us, event | category | flops | bytes accessed | tf_op | source)
XLA Modules:
  0.0 2096.6 jit_solution(5051450028700467300)
XLA Ops:
  20.2 42.7 %all-reduce.3 = bf16[1024]{0:T(1024)(128)(2,1)S(1)} all-reduce(bf16[1024]{0:T(1024)(128)(2,1)S(1)} %dynamic-update-slice), channel_id=1, replica_groups=mesh['dp'=16,'fsdp'=2] {'dp','fsdp'}, use_global_device_ids=true, to_apply=%add.3 | all-reduce | flops 1024 | bytes 4096
  70.7 13.2 multiply_convert_fusion.12
  91.8 37.4 %all-gather.12.cloned.1.call-done = bf16[1024,1024]{1,0:T(8,128)(2,1)} async-done(((bf16[32,1024]{1,0:T(8,128)(2,1)}), bf16[1024,1024]{1,0:T(8,128)(2,1)}) %all-gather.12.cloned.1.call-update) | async-done | bytes 2097168 | tf_op jit(solution)/shard_map/all_gather | solution.py:110
  161.5 26.1 %all-gather.14.cloned.1.call-done = bf16[1024,1024]{1,0:T(8,128)(2,1)} async-done(((bf16[32,1024]{1,0:T(8,128)(2,1)}), bf16[1024,1024]{1,0:T(8,128)(2,1)}) %all-gather.14.cloned.1.call-update) | async-done | bytes 2097168 | tf_op jit(solution)/shard_map/all_gather | solution.py:108
  187.5 13.2 multiply_convert_fusion.13
  208.5 16.6 all-gather
  230.8 10.3 multiply_convert_fusion.1
  241.2 13.9 fusion.39
  255.1 11.7 multiply_reduce_fusion.4
  266.9 12.3 copy.82
  279.2 10.7 reshape.200
  298.9 14.1 all-gather.1
  313.0 13.1 multiply_convert_fusion.11
  326.1 12.5 multiply_reduce_fusion.3
  348.0 26.1 %all-gather.22.cloned.1.call-done = bf16[1024,2816]{1,0:T(8,128)(2,1)} async-done(((bf16[32,2816]{1,0:T(8,128)(2,1)}), bf16[1024,2816]{1,0:T(8,128)(2,1)}) %all-gather.22.cloned.1.call-update) | async-done | bytes 5767184 | tf_op jit(solution)/shard_map/all_gather | solution.py:140
  374.2 69.1 %all-gather.24.cloned.1.call-done = bf16[1024,2816]{1,0:T(8,128)(2,1)} async-done(((bf16[32,2816]{1,0:T(8,128)(2,1)}), bf16[1024,2816]{1,0:T(8,128)(2,1)}) %all-gather.24.cloned.1.call-update) | async-done | bytes 5767184 | tf_op jit(solution)/shard_map/all_gather | solution.py:141
  443.3 69.1 %all-gather.26.cloned.1.call-done = bf16[2816,1024]{1,0:T(8,128)(2,1)} async-done(((bf16[88,1024]{1,0:T(8,128)(2,1)}), bf16[2816,1024]{1,0:T(8,128)(2,1)}) %all-gather.26.cloned.1.call-update) | async-done | bytes 5767184 | tf_op jit(solution)/shard_map/all_gather | solution.py:142
  512.4 20.1 fusion.74
  532.5 21.3 %multiply_convert_fusion.2 = bf16[2048,2816]{1,0:T(8,128)(2,1)} fusion(f32[2048,2816]{1,0:T(8,128)} %fusion.74, bf16[2048,1024]{1,0:T(8,128)(2,1)} %multiply_convert_fusion.10, bf16[1024,2816]{1,0:T(8,128)(2,1)} %all-gather.22.cloned.1.call-done), kind=kOutput, calls=%fused_computation.9 | convolution fusion | flops 11822694400 | bytes 44564480 | tf_op jit(solution)/shard_map/dot_general | solution.py:43
  553.8 21.7 %multiply_convert_fusion.3 = bf16[2048,2816]{1,0:T(8,128)(2,1)} fusion(f32[2048,2816]{1,0:T(8,128)} %fusion.74, bf16[2048,1024]{1,0:T(8,128)(2,1)} %multiply_convert_fusion.10, bf16[1024,2816]{1,0:T(8,128)(2,1)} %all-gather.24.cloned.1.call-done), kind=kOutput, calls=%fused_computation.10 | convolution fusion | flops 11822694400 | bytes 44564480 | tf_op jit(solution)/shard_map/dot_general | solution.py:43
  575.5 17.9 fusion.75
  593.4 22.3 %multiply_reduce_fusion.2 = (f32[2048]{0:T(1024)S(1)}, f32[2048,1024]{1,0:T(8,128)}) fusion(f32[2048,1024]{1,0:T(8,128)} %get-tuple-element.385, f32[2048,1024]{1,0:T(8,128)} %fusion.75, bf16[2048,2816]{1,0:T(8,128)(2,1)} %multiply_convert_fusion.2, bf16[1024,2816]{1,0:T(8,128)(2,1)} %all-gather.24.cloned.1.call-done), kind=kOutput, calls=%fused_computation.46 | convolution fusion | flops 11817449472 | bytes 42475520 | tf_op jit(solution)/shard_map/dot_general | solution.py:47
  615.7 11.7 fusion.12
  627.5 14.4 multiply_reduce_fusion
  659.9 11.3 multiply_convert_fusion
  671.2 13.6 fusion.42
  684.8 13.2 fusion.47
  703.8 11.9 fusion.29
  734.5 12.2 copy.89
  746.7 10.8 reshape.203
  769.6 14.8 all-gather.2
  785.7 11.1 add_bitcast_fusion
  796.7 12.3 copy.94
  809.0 10.9 reshape.204
  840.9 16.2 multiply_convert_fusion.6
  857.1 26.5 %fusion.4 = f32[1024,4096]{1,0:T(8,128)} fusion(bf16[2048,1024]{1,0:T(8,128)(2,1)} %fusion.15, bf16[2048,1024]{0,1:T(8,128)(2,1)} %get-tuple-element.363, bf16[2048,1024]{0,1:T(8,128)(2,1)} %convert_element_type.221, bf16[2048,1024]{0,1:T(8,128)(2,1)} %get-tuple-element.395, bf16[2048,1024]{0,1:T(8,128)(2,1)} %get-tuple-element.396), kind=kOutput, calls=%fused_computation.13 | convolution fusion | flops 17246978048 | bytes 37748736 | tf_op jit(solution)/shard_map/dot_general | solution.py:53
  883.6 15.9 pad_maximum_fusion
  899.6 34.3 %fusion = f32[1024,5632]{1,0:T(8,128)} fusion(bf16[2048,1024]{1,0:T(8,128)(2,1)} %multiply_convert_fusion.10, bf16[2048,2816]{1,0:T(8,128)(2,1)} %multiply_convert_fusion.2, bf16[2048,2816]{1,0:T(8,128)(2,1)} %multiply_convert_fusion.3), kind=kOutput, calls=%fused_computation.5 | convolution fusion | flops 23668457472 | bytes 50331648 | tf_op jit(solution)/shard_map/dot_general | solution.py:53
  933.9 20.1 fusion.73
  954.0 21.4 %multiply_convert_fusion.4 = bf16[2048,2816]{1,0:T(8,128)(2,1)} fusion(f32[2048,2816]{1,0:T(8,128)} %fusion.73, bf16[2048,1024]{1,0:T(8,128)(2,1)} %multiply_convert_fusion.10, bf16[1024,2816]{1,0:T(8,128)(2,1)} %all-gather.24.cloned.1.call-done), kind=kOutput, calls=%fused_computation.11 | convolution fusion | flops 11822694400 | bytes 44564480 | tf_op jit(solution)/shard_map/dot_general | solution.py:43
  975.4 19.0 fusion.79
  995.1 41.8 %all-reduce.4 = f32[1024]{0:T(1024)S(1)} all-reduce(f32[1024]{0:T(1024)S(1)} %copy-done.29), channel_id=6, replica_groups=mesh['dp'=16,'fsdp'=2] {'dp','fsdp'}, use_global_device_ids=true, to_apply=%region_20.21.clone | all-reduce | flops 1024 | bytes 8192
  1060.9 15.9 fusion.20
  1076.8 10.2 fusion.19
  1087.0 19.2 multiply_convert_fusion.9
  1106.2 238.4 %reduce-scatter.4.cloned.1.call-done = f32[32,5120]{1,0:T(8,128)} async-done(((f32[1024,5120]{1,0:T(8,128)}), f32[32,5120]{1,0:T(8,128)}) %reduce-scatter.4.cloned.1.call-update) | async-done | bytes 655376 | tf_op jit(solution)/shard_map/reduce_scatter | solution.py:241
  1346.5 490.1 %reduce-scatter.6.cloned.1.call-done = f32[32,5632]{1,0:T(8,128)} async-done(((f32[1024,5632]{1,0:T(8,128)}), f32[32,5632]{1,0:T(8,128)}) %reduce-scatter.6.cloned.1.call-update) | async-done | bytes 720912 | tf_op jit(solution)/shard_map/reduce_scatter | solution.py:168
  1838.6 251.1 %reduce-scatter.8.cloned.1.call-done = f32[88,1024]{1,0:T(8,128)} async-done(((f32[2816,1024]{1,0:T(8,128)}), f32[88,1024]{1,0:T(8,128)}) %reduce-scatter.8.cloned.1.call-update) | async-done | bytes 360464 | tf_op jit(solution)/shard_map/reduce_scatter | solution.py:171
  (165 shorter events, 201.7 us)
Async XLA Ops:
  7.2 63.6 %all-gather.16.cloned.1.call-start = ((), (), s32[]{:S(2)}) async-start(), calls=%async_computation.5 | async-start | bytes 2162688 | tf_op jit(solution)/shard_map/all_gather | solution.py:109
  7.9 121.3 %all-gather.12.cloned.1.call-start = ((), (), s32[]{:S(2)}) async-start(), calls=%async_computation.3 | async-start | bytes 2162688 | tf_op jit(solution)/shard_map/all_gather | solution.py:110
  8.7 178.9 %all-gather.14.cloned.1.call-start = ((), (), s32[]{:S(2)}) async-start(), calls=%async_computation.4 | async-start | bytes 2162688 | tf_op jit(solution)/shard_map/all_gather | solution.py:108
  9.4 303.6 %all-gather.18.cloned.1.call-start = ((), (), s32[]{:S(2)}) async-start(), calls=%async_computation.6 | async-start | bytes 2162688 | tf_op jit(solution)/shard_map/all_gather | solution.py:111
  10.0 316.1 %all-gather.20.cloned.1.call-start = ((), (), s32[]{:S(2)}) async-start(), calls=%async_computation.7 | async-start | bytes 2162688 | tf_op jit(solution)/shard_map/all_gather | solution.py:113
  10.6 363.6 %all-gather.22.cloned.1.call-start = ((), (), s32[]{:S(2)}) async-start(), calls=%async_computation.8 | async-start | bytes 5947392 | tf_op jit(solution)/shard_map/all_gather | solution.py:140
  11.1 432.1 %all-gather.24.cloned.1.call-start = ((), (), s32[]{:S(2)}) async-start(), calls=%async_computation.9 | async-start | bytes 5947392 | tf_op jit(solution)/shard_map/all_gather | solution.py:141
  11.9 500.5 %all-gather.26.cloned.1.call-start = ((), (), s32[]{:S(2)}) async-start(), calls=%async_computation.10 | async-start | bytes 5947392 | tf_op jit(solution)/shard_map/all_gather | solution.py:142
  12.6 1331.9 %reduce-scatter.4.cloned.1.call-start = ((), (), s32[]{:S(2)}) async-start(), calls=%async_computation.11 | async-start | bytes 21626880 | tf_op jit(solution)/shard_map/reduce_scatter | solution.py:241
  12.7 218.1 %copy-start.9 = (f32[256,256]{1,0:T(8,128)}, f32[256,256]{1,0:T(8,128)S(1)}, u32[]{:S(2)}) copy-start(f32[256,256]{1,0:T(8,128)S(1)} %fusion.57) | copy-start | bytes 786436
  12.8 4.5 copy-start.3
  12.8 7.2 copy-start.34
  12.8 50.1 %copy-start.30 = (s32[2]{0:T(128)S(1)}, s32[2]{0:T(128)}, u32[]{:S(2)}) copy-start(s32[2]{0:T(128)} %param.19) | copy-start | bytes 28
  16.0 0.6 copy-start.22
  62.9 250.1 %copy-start.26 = (f32[1024]{0:T(1024)}, f32[1024]{0:T(1024)S(1)}, u32[]{:S(2)}) copy-start(f32[1024]{0:T(1024)S(1)} %convert_element_type.198) | copy-start | bytes 12292
  226.4 4.4 copy-start
  266.8 46.1 %copy-start.17 = (f32[2,2,4,128]{3,1,2,0:T(2,128)}, f32[2,2,4,128]{3,1,2,0:T(2,128)S(1)}, u32[]{:S(2)}) copy-start(f32[2,2,4,128]{3,1,2,0:T(2,128)S(1)} %copy.105) | copy-start | bytes 24580
  326.1 12.5 copy-start.11
  338.6 2.1 copy-start.6
  341.8 6.3 copy-start.7
  593.4 22.3 %copy-start.20 = (f32[1,8,2,128]{3,1,2,0:T(8,128)S(1)}, f32[1,8,2,128]{3,1,2,0:T(8,128)}, u32[]{:S(2)}) copy-start(f32[1,8,2,128]{3,1,2,0:T(8,128)} %copy-done.19) | copy-start | bytes 24580
  615.7 11.7 copy-start.14
  615.7 11.7 copy-start.18
  615.7 11.7 copy-start.27
  627.4 14.5 slice-start
  627.4 14.4 slice-start.1
  627.4 14.4 copy-start.28
  652.0 7.9 copy-start.10
  684.8 13.2 copy-start.1
  684.8 13.2 copy-start.2
  698.0 17.7 slice-start.2
  703.8 11.9 slice-start.3
  715.7 8.7 copy-start.8
  761.5 8.1 copy-start.16
  761.5 22.9 %copy-start.5 = (f32[2,16,64,64]{3,2,1,0:T(8,128)S(1)}, f32[2,16,64,64]{3,2,1,0:T(8,128)}, u32[]{:S(2)}) copy-start(f32[2,16,64,64]{3,2,1,0:T(8,128)} %custom-call.2) | copy-start | bytes 1572868
  899.5 937.1 %reduce-scatter.6.cloned.1.call-start = ((), (), s32[]{:S(2)}) async-start(), calls=%async_computation.12 | async-start | bytes 23789568 | tf_op jit(solution)/shard_map/reduce_scatter | solution.py:168
  933.9 1155.9 %reduce-scatter.8.cloned.1.call-start = ((), (), s32[]{:S(2)}) async-start(), calls=%async_computation.13 | async-start | bytes 11894784 | tf_op jit(solution)/shard_map/reduce_scatter | solution.py:171
  994.4 0.7 copy-start.23
  994.4 0.7 copy-start.29
  994.4 43.1 %copy-start.31 = (bf16[1024,1024]{1,0:T(8,128)(2,1)S(1)}, bf16[1024,1024]{1,0:T(8,128)(2,1)}, u32[]{:S(2)}) copy-start(bf16[1024,1024]{1,0:T(8,128)(2,1)} %all-gather.16.cloned.1.call-done) | copy-start | bytes 6291460
  1037.5 9.3 copy-start.12
  1037.5 9.3 copy-start.33
  1046.8 7.1 copy-start.13
  1046.8 7.1 copy-start.32
  1053.9 7.0 copy-start.4
  1053.9 7.0 copy-start.15
  1060.9 15.9 copy-start.25
  1076.8 10.2 copy-start.21
  (2 other events, 1.2 us)
Sparse Core Ops, SparseCore 0:
  11.0 59.6 all-gather.15
  73.7 55.4 all-gather.11
  132.2 55.3 all-gather.13
  190.4 56.6 all-gather.17
  249.9 55.3 all-gather.19
  308.0 66.0 all-gather.21
  377.1 66.1 all-gather.23
  446.2 66.1 all-gather.25
  899.6 444.8 reduce-scatter.3
  1346.7 489.8 reduce-scatter.5
  1839.5 250.1 reduce-scatter.7
where the time goes:
time: 2100 us
  waiting for transfers between devices  1210 us (58%)
  matrix products  505 us (24%)
  local copies, waits for them, and re-layouts  136 us (6%)
  blocking collectives  130 us (6%)
  other arithmetic  96 us (5%)
    reduce_scatter x1, waiting for transfers between devices, shards(): lax.psum_scatter(column_term(normed_two_low, grad_up_both), ('dp', 'fsdp'...  490 us
    reduce_scatter x1, waiting for transfers between devices, shards(): lax.psum_scatter(column_term(glu_rows, upstream_low), ('dp', 'fsdp'), sca...  251 us
    reduce_scatter x1, waiting for transfers between devices, shards(): lax.psum_scatter(jnp.concatenate([inner, outer], axis=1), ('dp', 'fsdp'),...  238 us
    dot_general x10, matrix products, project(): return jnp.dot(left_side, right_side, preferred_element_type=jnp.float32)  165 us
    dot_general x13, matrix products, einsum_wide(): jnp.einsum(pattern, left_side, right_side, preferred_element_type=jnp.flo...  137 us
    dot_general x8, matrix products, project_back(): lax.dot_general(left_side, right_side, (((1,), (1,)), ((), ())), preferre...  114 us
    dot_general x4, matrix products, weight_term(): lax.dot_general(left_side, right_side, (((0,), (0,)), ((), ())), preferre...  88.5 us
    unnamed x2, blocking collectives  84.5 us
  transfers between devices with their start and end apart: 11, of which 9 were waited for; matrix products, arithmetic and copies ran while one was open for 17% of the time, Pallas kernels for 0%

commit v1 on v0

v1 whole, which is shorter than its diff:
```python
import jax
import jax.numpy as jnp
from jax import lax
from jax.experimental import pallas as pl
from jax.experimental.pallas import tpu as pltpu
from jax.sharding import PartitionSpec as P

HD = 64
H = 16
BLOCK = 256


GROUP = 256
HEADS = GROUP // HD
LOW = jnp.bfloat16
WIDE = jnp.float32

norm_epsilon = 1e-06


def bit_steps():
    steps = []
    for axis in ("dp", "fsdp"):
        size = lax.axis_size(axis)
        bit = 0
        while (1 << bit) < size:
            steps.append((axis, bit, [(i, i ^ (1 << bit)) for i in range(size)]))
            bit += 1
    return steps


def stream_orders():
    steps = bit_steps()
    dp = [s for s in steps if s[0] == "dp"]
    fs = [s for s in steps if s[0] == "fsdp"]
    core, rest = dp[0], fs[:1] + dp[1:3]
    tail = dp[3:] + fs[1:]
    return [[core] + rest[k:] + rest[:k] + tail for k in range(3)]


def own_bit(step):
    axis, bit, _ = step
    return lax.rem(lax.div(lax.axis_index(axis), 1 << bit), 2)


def bit_dims():
    steps = bit_steps()
    dp = sorted([s for s in steps if s[0] == "dp"], key=lambda s: -s[1])
    fs = sorted([s for s in steps if s[0] == "fsdp"], key=lambda s: -s[1])
    return [(s[0], s[1]) for s in dp + fs]


def gather_rows(shard, order):
    dims = bit_dims()
    held = []
    data = shard
    for step in reversed(order):
        axis, bit, perm = step
        other = lax.ppermute(data, axis, perm)
        mine = own_bit(step) == 0
        place = sum(1 for d in held if dims.index(d) < dims.index((axis, bit)))
        held.append((axis, bit))
        data = jnp.stack(
            [jnp.where(mine, data, other), jnp.where(mine, other, data)], axis=place
        )
    return data.reshape((-1,) + shard.shape[1:])


def scatter_rows(full, order):
    dims = bit_dims()
    rows = full.shape[0] >> len(dims)
    data = full.astype(jnp.bfloat16).reshape((2,) * len(dims) + (rows,) + full.shape[1:])
    left = list(dims)
    for at, step in enumerate(order):
        axis, bit, perm = step
        place = left.index((axis, bit))
        left.pop(place)
        own = own_bit(step)
        send = lax.dynamic_index_in_dim(data, 1 - own, place, keepdims=False)
        keep = lax.dynamic_index_in_dim(data, own, place, keepdims=False)
        come = lax.ppermute(send, axis, perm)
        data = keep.astype(jnp.float32) + come.astype(jnp.float32)
        if at < len(order) - 1:
            data = data.astype(jnp.bfloat16)
    return data


def shift_sum(x, axis, reverse):
    size = lax.axis_size(axis)
    total = jnp.zeros_like(x)
    low = x.astype(jnp.bfloat16)
    for s in range(1, size):
        pairs = [(i + s, i) if reverse else (i, i + s) for i in range(size - s)]
        total = total + lax.ppermute(low, axis, pairs).astype(x.dtype)
    return total


def dot_nn(a, b):
    return jnp.dot(a, b, preferred_element_type=WIDE)


def dot_nt(a, b):
    return lax.dot_general(a, b, (((1,), (1,)), ((), ())), preferred_element_type=WIDE)


def dot_tn(a, b):
    return lax.dot_general(a, b, (((0,), (0,)), ((), ())), preferred_element_type=WIDE)


def rms_scale(values):
    return lax.rsqrt(jnp.mean(values * values, axis=-1, keepdims=True) + norm_epsilon)


def norm_back(values, scale, upstream):
    inner_mean = jnp.mean(upstream * values, axis=-1, keepdims=True)
    return scale * (upstream - values * (scale * scale) * inner_mean)


def silu_slope(pre_rows):
    logistic = jax.nn.sigmoid(pre_rows)
    return logistic * (1.0 + pre_rows * (1.0 - logistic))


def head_square():
    row = lax.broadcasted_iota(jnp.int32, (GROUP, GROUP), 0) // HD
    col = lax.broadcasted_iota(jnp.int32, (GROUP, GROUP), 1) // HD
    return (row == col).astype(WIDE)


def head_rows():
    lane = lax.broadcasted_iota(jnp.int32, (1, GROUP), 1) // HD
    return [(lane == h).astype(WIDE).astype(LOW) for h in range(HEADS)]


def split_heads(rows, marks):
    return jnp.concatenate([rows * mark for mark in marks], axis=0)


def pack_state(square, same):
    return jnp.sum((square * same).reshape(HEADS, HD, GROUP), axis=0)


def open_state(packed, same):
    return (jnp.concatenate([packed] * HEADS, axis=0) * same).astype(LOW)


def causal_masks():
    i = lax.broadcasted_iota(jnp.int32, (BLOCK, HEADS * BLOCK), 0)
    j = lax.broadcasted_iota(jnp.int32, (BLOCK, HEADS * BLOCK), 1) % BLOCK
    return (i >= j).astype(WIDE), (j >= i).astype(WIDE)


def groups(width):
    return [slice(g * GROUP, (g + 1) * GROUP) for g in range(width // GROUP)]


def key_value_kernel(per_seq, tok, w_key, w_value, normed, pre_key, keys, values, totals):
    x = tok[...].astype(WIDE)
    rows = (x * rms_scale(x)).astype(LOW)
    normed[...] = rows
    pre = dot_nn(rows, w_key[...])
    pre_key[...] = pre.astype(LOW)
    k = jax.nn.silu(pre).astype(LOW)
    keys[...] = k
    v = dot_nn(rows, w_value[...]).astype(LOW)
    values[...] = v

    @pl.when(pl.program_id(0) % per_seq == 0)
    def _():
        totals[...] = jnp.zeros_like(totals)

    same = head_square()
    for g in groups(k.shape[1]):
        totals[0, :, g] += pack_state(dot_tn(k[:, g], v[:, g]), same)


def query_gate_kernel(normed, w_query, w_gate, pre_query, queries, pre_gate):
    rows = normed[...]
    pre = dot_nn(rows, w_query[...])
    pre_query[...] = pre.astype(LOW)
    queries[...] = jax.nn.silu(pre).astype(LOW)
    pre_gate[...] = dot_nn(rows, w_gate[...]).astype(LOW)


def attend_kernel(
    per_seq, queries, keys, values, pre_gate, tok, incoming, gain, w_out,
    attended, mixed, residual, prefix, carry,
):
    @pl.when(pl.program_id(0) % per_seq == 0)
    def _():
        carry[...] = incoming[0]

    same, marks = head_square(), head_rows()
    causal, _ = causal_masks()
    prefix[0] = carry[...].astype(LOW)
    for g in groups(queries.shape[1]):
        q, k, v = queries[:, g], keys[:, g], values[:, g]
        scores = (dot_nt(q, split_heads(k, marks)) * causal).astype(LOW)
        out = dot_nn(scores, split_heads(v, marks))
        out += dot_nn(q, open_state(carry[:, g], same))
        attended[:, g] = out.astype(LOW)
        carry[:, g] += pack_state(dot_tn(k, v), same)
    rows = attended[...].astype(WIDE)
    gate = jax.nn.sigmoid(pre_gate[...].astype(WIDE))
    rows = (rows * rms_scale(rows) * gain[...] * gate).astype(LOW)
    mixed[...] = rows
    residual[...] = tok[...].astype(WIDE) + dot_nn(rows, w_out[...])


def feed_kernel(
    per_seq, limits, residual, cotangent, w_one, w_two, w_three, w_out, gain, pre_gate,
    attended, queries,
    layer_out, normed, glu, grad_one, grad_two, upstream_low, grad_residual, grad_low,
    grad_gate, grad_attended, totals, grad_gain,
):
    step = pl.program_id(0)
    row_count = residual.shape[0]
    spot = lax.broadcasted_iota(jnp.int32, (row_count, 1), 0) + (step % per_seq) * row_count
    valid = (spot < limits[step // per_seq]).astype(WIDE)
    res = residual[...]
    scale = rms_scale(res)
    rows = (res * scale).astype(LOW)
    normed[...] = rows
    upstream = cotangent[...].astype(WIDE) * valid
    up_low = upstream.astype(LOW)
    upstream_low[...] = up_low
    for c in groups(w_one.shape[1]):
        one = dot_nn(rows, w_one[:, c])
        two = dot_nn(rows, w_two[:, c])
        back = dot_nt(up_low, w_three[c, :])
        glu[:, c] = (one * two).astype(LOW)
        grad_one[:, c] = (back * two).astype(LOW)
        grad_two[:, c] = (back * one).astype(LOW)
    layer_out[...] = (valid * (res + dot_nn(glu[...], w_three[...]))).astype(LOW)
    back = dot_nt(grad_one[...], w_one[...]) + dot_nt(grad_two[...], w_two[...])
    grad = upstream + norm_back(res, scale, back)
    grad_residual[...] = grad
    grad = grad.astype(LOW)
    grad_low[...] = grad
    grad = dot_nt(grad, w_out[...])
    gate = jax.nn.sigmoid(pre_gate[...].astype(WIDE))
    att = attended[...].astype(WIDE)
    scale = rms_scale(att)
    hat = att * scale
    gated = grad * gate

    @pl.when(step == 0)
    def _():
        grad_gain[...] = jnp.zeros_like(grad_gain)

    grad_gain[...] += jnp.sum(gated * hat, axis=0, keepdims=True)
    gated = gated * gain[...]
    grad_gate[...] = (gated * hat * (1.0 - gate)).astype(LOW)
    grad_att = norm_back(att, scale, gated).astype(LOW)
    grad_attended[...] = grad_att

    @pl.when(step % per_seq == 0)
    def _():
        totals[...] = jnp.zeros_like(totals)

    same = head_square()
    for g in groups(grad_att.shape[1]):
        totals[0, :, g] += pack_state(dot_tn(queries[:, g], grad_att[:, g]), same)


def attend_back_kernel(
    per_seq, queries, keys, values, grad_attended, pre_query, pre_key, prefix, incoming,
    grad_query, grad_key, grad_value, carry,
):
    @pl.when(pl.program_id(0) % per_seq == 0)
    def _():
        carry[...] = incoming[0]

    same, marks = head_square(), head_rows()
    causal, causal_t = causal_masks()
    for g in groups(queries.shape[1]):
        q, k, v, ga = queries[:, g], keys[:, g], values[:, g], grad_attended[:, g]
        qs, ks, vs, gs = (split_heads(rows, marks) for rows in (q, k, v, ga))
        state = open_state(prefix[0, :, g].astype(WIDE), same)
        grad_state = open_state(carry[:, g], same)
        grad_scores = (dot_nt(ga, vs) * causal).astype(LOW)
        gq = dot_nn(grad_scores, ks) + dot_nt(ga, state)
        grad_scores = (dot_nt(v, gs) * causal_t).astype(LOW)
        gk = dot_nn(grad_scores, qs) + dot_nt(v, grad_state)
        scores = (dot_nt(k, qs) * causal_t).astype(LOW)
        gv = dot_nn(scores, gs) + dot_nn(k, grad_state)
        grad_query[:, g] = (gq * silu_slope(pre_query[:, g].astype(WIDE))).astype(LOW)
        grad_key[:, g] = (gk * silu_slope(pre_key[:, g].astype(WIDE))).astype(LOW)
        grad_value[:, g] = gv.astype(LOW)
        carry[:, g] += pack_state(dot_tn(q, ga), same)


def input_kernel(
    grad_query, grad_key, grad_value, grad_gate, w_query, w_key, w_value, w_gate, tok,
    grad_residual, input_grad,
):
    grad = dot_nt(grad_query[...], w_query[...]) + dot_nt(grad_key[...], w_key[...])
    grad += dot_nt(grad_value[...], w_value[...]) + dot_nt(grad_gate[...], w_gate[...])
    x = tok[...].astype(WIDE)
    input_grad[...] = grad_residual[...] + norm_back(x, rms_scale(x), grad)


def rows_spec(width, block=BLOCK, order=lambda i: i):
    return pl.BlockSpec((block, width), lambda i: (order(i), 0))


def whole_spec(array):
    rank = array.ndim
    return pl.BlockSpec(array.shape, lambda i: (0,) * rank, pipeline_mode=pl.Buffered(1))


def call(kernel, steps, operands, results, scratch=(), flops=0, limit=56):
    moved = sum(a.size * a.dtype.itemsize for a, _ in operands)
    return pl.pallas_call(
        kernel,
        grid=(steps,),
        in_specs=[spec for _, spec in operands],
        out_specs=[spec for _, _, spec in results],
        out_shape=[jax.ShapeDtypeStruct(shape, dtype) for shape, dtype, _ in results],
        scratch_shapes=list(scratch),
        compiler_params=pltpu.CompilerParams(
            dimension_semantics=("arbitrary",), vmem_limit_bytes=limit << 20
        ),
        cost_estimate=pl.CostEstimate(flops=flops, bytes_accessed=moved, transcendentals=0),
    )(*[a for a, _ in operands])


def shards(
    tokens,
    lengths,
    w_query,
    w_key,
    w_value,
    w_gate,
    out_gain,
    w_out,
    w_one,
    w_two,
    w_three,
    cotangent,
):
    seq_count, local_length, width = tokens.shape
    row_count = seq_count * local_length
    hidden = w_one.shape[1]
    steps = row_count // BLOCK
    per_seq = local_length // BLOCK
    orders = stream_orders()
    tok = tokens.reshape(row_count, width)
    cot = cotangent.reshape(row_count, width)
    limits = lengths - lax.axis_index("fsdp") * local_length
    full_key = gather_rows(w_key, orders[0])
    full_value = gather_rows(w_value, orders[1])
    full_query = gather_rows(w_query, orders[2])
    full_gate = gather_rows(w_gate, orders[0])
    gain_columns = jnp.broadcast_to(out_gain[:, None], (out_gain.shape[0], 128))
    full_out = gather_rows(jnp.concatenate([w_out, gain_columns], axis=1), orders[1])
    full_one = gather_rows(w_one, orders[2])
    full_two = gather_rows(w_two, orders[0])
    full_three = gather_rows(w_three, orders[1])
    gain = full_out[:, width].astype(WIDE)[None, :]
    full_out = full_out[:, :width]

    rows = rows_spec(width)
    narrow = ((row_count, width), LOW, rows)
    wide = ((row_count, width), WIDE, rows)
    big = ((row_count, hidden), LOW, rows_spec(hidden))
    state_spec = pl.BlockSpec((1, HD, width), lambda i: (i // per_seq, 0, 0))
    state = ((seq_count, HD, width), WIDE, state_spec)
    square = 2 * row_count * width * width

    normed_low, pre_key, keys, values, totals = call(
        lambda *refs: key_value_kernel(per_seq, *refs),
        steps,
        [(tok, rows), (full_key, whole_spec(full_key)), (full_value, whole_spec(full_value))],
        [narrow, narrow, narrow, narrow, state],
        flops=2 * square,
    )
    incoming = shift_sum(totals, "fsdp", False)
    pre_query, queries, pre_gate = call(
        query_gate_kernel,
        steps,
        [(normed_low, rows), (full_query, whole_spec(full_query)), (full_gate, whole_spec(full_gate))],
        [narrow, narrow, narrow],
        flops=2 * square,
    )
    prefix_spec = pl.BlockSpec((1, HD, width), lambda i: (i, 0, 0))
    attended, mixed, residual, prefix = call(
        lambda *refs: attend_kernel(per_seq, *refs),
        steps,
        [(queries, rows), (keys, rows), (values, rows), (pre_gate, rows), (tok, rows),
         (incoming, state_spec), (gain, whole_spec(gain)), (full_out, whole_spec(full_out))],
        [narrow, narrow, wide, ((steps, HD, width), LOW, prefix_spec)],
        scratch=[pltpu.VMEM((HD, width), WIDE)],
        flops=3 * square,
    )
    (
        layer_out, normed_two, glu, grad_up_one, grad_up_two, upstream_low, grad_residual,
        grad_residual_low, grad_pre_gate, grad_attended, grad_totals, grad_gain_term,
    ) = call(
        lambda *refs: feed_kernel(per_seq, *refs),
        steps,
        [(limits, pl.BlockSpec(memory_space=pltpu.SMEM)), (residual, rows), (cot, rows),
         (full_one, whole_spec(full_one)), (full_two, whole_spec(full_two)),
         (full_three, whole_spec(full_three)), (full_out, whole_spec(full_out)),
         (gain, whole_spec(gain)), (pre_gate, rows), (attended, rows), (queries, rows)],
        [narrow, narrow, big, big, big, narrow, wide, narrow, narrow, narrow, state,
         ((1, width), WIDE, pl.BlockSpec((1, width), lambda i: (0, 0)))],
        flops=12 * row_count * width * hidden + square,
    )
    outgoing = shift_sum(grad_totals, "fsdp", True)
    grad_one = scatter_rows(dot_tn(normed_two, grad_up_one), orders[1])
    grad_two = scatter_rows(dot_tn(normed_two, grad_up_two), orders[2])
    grad_three = scatter_rows(dot_tn(glu, upstream_low), orders[0])
    gain_term = jnp.broadcast_to(grad_gain_term.reshape(width, 1), (width, 128))
    grad_out = scatter_rows(
        jnp.concatenate([dot_tn(mixed, grad_residual_low), gain_term], axis=1), orders[1]
    )
    grad_gain = grad_out[:, width]
    grad_out = grad_out[:, :width]

    def back(i):
        return (i // per_seq) * per_seq + per_seq - 1 - i % per_seq

    back_rows = rows_spec(width, order=back)
    back_narrow = ((row_count, width), LOW, back_rows)
    grad_pre_query, grad_pre_key, grad_pre_value = call(
        lambda *refs: attend_back_kernel(per_seq, *refs),
        steps,
        [(queries, back_rows), (keys, back_rows), (values, back_rows),
         (grad_attended, back_rows), (pre_query, back_rows), (pre_key, back_rows),
         (prefix, pl.BlockSpec((1, HD, width), lambda i: (back(i), 0, 0))),
         (outgoing, state_spec)],
        [back_narrow, back_narrow, back_narrow],
        scratch=[pltpu.VMEM((HD, width), WIDE)],
        flops=6 * square,
    )
    grad_query = scatter_rows(dot_tn(normed_low, grad_pre_query), orders[0])
    grad_key = scatter_rows(dot_tn(normed_low, grad_pre_key), orders[1])
    grad_value = scatter_rows(dot_tn(normed_low, grad_pre_value), orders[2])
    grad_gate = scatter_rows(dot_tn(normed_low, grad_pre_gate), orders[0])
    (input_grad,) = call(
        input_kernel,
        steps,
        [(grad_pre_query, rows), (grad_pre_key, rows), (grad_pre_value, rows),
         (grad_pre_gate, rows), (full_query, whole_spec(full_query)),
         (full_key, whole_spec(full_key)), (full_value, whole_spec(full_value)),
         (full_gate, whole_spec(full_gate)), (tok, rows), (grad_residual, rows)],
        [wide],
        flops=4 * square,
    )
    return (
        layer_out.reshape(tokens.shape),
        input_grad.reshape(tokens.shape),
        grad_query,
        grad_key,
        grad_value,
        grad_gate,
        grad_gain,
        grad_out,
        grad_one,
        grad_two,
        grad_three,
    )


def solution(mesh):
    in_specs = (
        P("dp", "fsdp", None),
        P("dp"),
        P(("dp", "fsdp"), None),
        P(("dp", "fsdp"), None),
        P(("dp", "fsdp"), None),
        P(("dp", "fsdp"), None),
        P(("dp", "fsdp")),
        P(("dp", "fsdp"), None),
        P(("dp", "fsdp"), None),
        P(("dp", "fsdp"), None),
        P(("dp", "fsdp"), None),
        P("dp", "fsdp", None),
    )
    out_specs = (
        P("dp", "fsdp", None),
        P("dp", "fsdp", None),
        P(("dp", "fsdp"), None),
        P(("dp", "fsdp"), None),
        P(("dp", "fsdp"), None),
        P(("dp", "fsdp"), None),
        P(("dp", "fsdp")),
        P(("dp", "fsdp"), None),
        P(("dp", "fsdp"), None),
        P(("dp", "fsdp"), None),
        P(("dp", "fsdp"), None),
    )
    return jax.shard_map(shards, mesh=mesh, in_specs=in_specs, out_specs=out_specs, check_vma=False)
```

time: 2100 us -> 688 us (0.33)
  waiting for transfers between devices: 1210 us -> 193 us
  matrix products: 505 us -> 81.2 us
  Pallas kernels: 0 us -> 221 us
  blocking collectives: 130 us -> 0 us
  local copies, waits for them, and re-layouts: 136 us -> 40 us
  starting transfers between devices: 0.42 us -> 82.1 us
  other arithmetic: 96 us -> 60.1 us
    reduce_scatter x3 -> x0, waiting for transfers between devices: 980 us -> none  [the longest x1 490 us: shards(): lax.psum_scatter(column_term(normed_two_low, grad_up_both), ('dp', 'fsdp'...]
    dot_general x35 -> x8, matrix products: 505 us -> 81.2 us  [dot_tn(): lax.dot_general(a, b, (((0,), (0,)), ((), ())), preferred_element_type=WIDE)]
    all_gather x8 -> x0, waiting for transfers between devices: 230 us -> none  [the longest x1 69.1 us: shards(): lax.all_gather(w_two, ('dp', 'fsdp'), axis=0, tiled=True)]
    pallas_call x0 -> x6, Pallas kernels: none -> 221 us  [call(): pl.pallas_call(kernel, grid=(steps,), in_specs=[spec for _, spec in opera...]
    ppermute x0 -> x82, waiting for transfers between devices: none -> 193 us  [the longest x40 116 us: scatter_rows(): come = lax.ppermute(send, axis, perm)]
    unnamed x2 -> x0, blocking collectives: 84.5 us -> none
    ppermute x0 -> x82, starting transfers between devices: none -> 82.1 us  [the longest x40 41.6 us: scatter_rows(): come = lax.ppermute(send, axis, perm)]
    reshape x7 -> x0, local copies, waits for them, and re-layouts: 64 us -> none  [the longest x4 31.5 us: to_tiles(): return rows.reshape(seq_count, -1, BLOCK, H, HD)]
  transfers between devices with their start and end apart: 11 -> 82, of which waited for: 9 -> 39; matrix products, arithmetic and copies ran while one was open for 17% -> 22% of each run, Pallas kernels for 0% -> 17%
where the time goes in v1:
time: 688 us; the launch traced here: 680 us
  Pallas kernels  221 us (32%)
  waiting for transfers between devices  193 us (28%)
  starting transfers between devices  82.1 us (12%)
  matrix products  81.2 us (12%)
  other arithmetic  60.1 us (9%)
  local copies, waits for them, and re-layouts  40 us (6%)
    pallas_call x6, Pallas kernels, call(): pl.pallas_call(kernel, grid=(steps,), in_specs=[spec for _, spec in opera...  221 us
    ppermute x40, waiting for transfers between devices, scatter_rows(): come = lax.ppermute(send, axis, perm)  116 us
    dot_general x8, matrix products, dot_tn(): lax.dot_general(a, b, (((0,), (0,)), ((), ())), preferred_element_type=WIDE)  81.2 us
    ppermute x40, waiting for transfers between devices, gather_rows(): other = lax.ppermute(data, axis, perm)  74 us
    ppermute x40, starting transfers between devices, scatter_rows(): come = lax.ppermute(send, axis, perm)  41.6 us
    ppermute x40, starting transfers between devices, gather_rows(): other = lax.ppermute(data, axis, perm)  36.8 us
    another operation x77, other arithmetic, gather_rows(): jnp.stack([jnp.where(mine, data, other), jnp.where(mine, other, data)], a...  33.4 us
    convert_element_type x32, other arithmetic, scatter_rows(): data = data.astype(jnp.bfloat16)  15.9 us
  transfers between devices with their start and end apart: 82, of which 39 were waited for; matrix products, arithmetic and copies ran while one was open for 22% of the time, Pallas kernels for 17%

profile of v1, /device:TPU:0, one launch (start us, length us, event | category | flops | bytes accessed | tf_op | source)
XLA Modules:
  0.0 679.7 jit_solution(4735452428435630590)
XLA Ops:
  0.7 4.1 collective-permute-start.36
  4.8 2.8 collective-permute-start.31
  7.8 2.8 collective-permute-start.15
  13.4 20.4 %collective-permute-done.10 = bf16[32,1024]{1,0:T(8,128)(2,1)S(1)} collective-permute-done((bf16[32,1024]{1,0:T(8,128)(2,1)}, bf16[32,1024]{1,0:T(8,128)(2,1)S(1)}, u32[]{:S(2)}, u32[]{:S(2)}) %collective-permute-start.10) | collective-permute-done | bytes 65568 | tf_op jit(solution)/shard_map/ppermute | solution.py:59
  37.6 3.5 collective-permute-done
  41.1 2.9 collective-permute-done.5
  54.2 2.7 collective-permute-done.1
  61.2 9.2 %collective-permute-done.17 = bf16[2,2,32,1024]{3,2,0,1:T(8,128)(2,1)S(1)} collective-permute-done((bf16[2,2,32,1024]{3,2,0,1:T(8,128)(2,1)S(1)}, bf16[2,2,32,1024]{3,2,0,1:T(8,128)(2,1)S(1)}, u32[]{:S(2)}, u32[]{:S(2)}) %collective-permute-start.17) | collective-permute-done | bytes 262176 | tf_op jit(solution)/shard_map/ppermute | solution.py:59
  71.8 6.2 collective-permute-done.7
  80.4 7.6 %collective-permute-done.23 = bf16[2,2,32,1152]{3,2,0,1:T(8,128)(2,1)S(1)} collective-permute-done((bf16[2,2,32,1152]{3,2,0,1:T(8,128)(2,1)S(1)}, bf16[2,2,32,1152]{3,2,0,1:T(8,128)(2,1)S(1)}, u32[]{:S(2)}, u32[]{:S(2)}) %collective-permute-start.23) | collective-permute-done | bytes 294944 | tf_op jit(solution)/shard_map/ppermute | solution.py:59
  95.4 3.5 collective-permute-done.13
  99.4 3.7 collective-permute-done.8
  105.4 4.1 collective-permute-done.24
  110.8 6.4 collective-permute-done.33
  130.8 17.7 %shard_map.203 = (bf16[2048,1024]{1,0:T(8,128)(2,1)}, bf16[2048,1024]{1,0:T(8,128)(2,1)}, bf16[2048,1024]{1,0:T(8,128)(2,1)}, bf16[2048,1024]{1,0:T(8,128)(2,1)}, f32[2,64,1024]{2,1,0:T(8,128)}) custom-call(bf16[2048,1024]{1,0:T(8,128)(2,1)} %bitcast.452, bf16[1024,1024]{1,0:T(8,128)(2,1)} %bitcast.443, bf16[1024,1024]{1,0:T(8,128)(2,1)} %bitcast.441), custom_call_target="tpu_custom_call" | custom-call | flops 8589934592 | bytes 8388608 | tf_op jit(solution)/shard_map/pallas_call | solution.py:314
  154.1 13.6 %shard_map.204 = (bf16[2048,1024]{1,0:T(8,128)(2,1)}, bf16[2048,1024]{1,0:T(8,128)(2,1)}, bf16[2048,1024]{1,0:T(8,128)(2,1)}) custom-call(bf16[2048,1024]{1,0:T(8,128)(2,1)} %get-tuple-element.38.normed, bf16[1024,1024]{1,0:T(8,128)(2,1)} %bitcast.445, bf16[1024,1024]{1,0:T(8,128)(2,1)} %bitcast.439), custom_call_target="tpu_custom_call" | custom-call | flops 8589934592 | bytes 8388608 | tf_op jit(solution)/shard_map/pallas_call | solution.py:314
  183.9 23.3 %shard_map.205 = (bf16[2048,1024]{1,0:T(8,128)(2,1)}, bf16[2048,1024]{1,0:T(8,128)(2,1)}, f32[2048,1024]{1,0:T(8,128)}, bf16[8,64,1024]{2,1,0:T(8,128)(2,1)}) custom-call(bf16[2048,1024]{1,0:T(8,128)(2,1)} %get-tuple-element.39.refs_0_.refs_10_, bf16[2048,1024]{1,0:T(8,128)(2,1)} %get-tuple-element.40.refs_1_, bf16[2048,1024]{1,0:T(8,128)(2,1)} %get-tuple-element.41.refs_2_, ...), custom_call_target="tpu_custom_call" | custom-call | flops 12884901888 | bytes 23597056 | tf_op jit(solution)/shard_map/pallas_call | solution.py:314
  209.8 3.2 copy.62
  215.5 2.9 copy.61
  221.0 2.9 copy.60
  223.9 102.1 %shard_map.206 = (bf16[2048,1024]{1,0:T(8,128)(2,1)}, bf16[2048,1024]{1,0:T(8,128)(2,1)}, bf16[2048,2816]{1,0:T(8,128)(2,1)}, bf16[2048,2816]{1,0:T(8,128)(2,1)}...) custom-call(s32[2]{0:T(128)} %broadcast_subtract_fusion.refs_0_, ...), custom_call_target="tpu_custom_call" | custom-call | flops 75161927680 | bytes 44568584 | tf_op jit(solution)/shard_map/pallas_call | solution.py:314
  326.1 16.5 %convolution_convert_fusion = bf16[2816,1024]{1,0:T(8,128)(2,1)S(1)} fusion(bf16[2048,2816]{1,0:T(8,128)(2,1)} %get-tuple-element.63, bf16[2048,1024]{1,0:T(8,128)(2,1)} %get-tuple-element.64), kind=kOutput, calls=%fused_computation.9 | convolution fusion | flops 11814043648 | bytes 21495808 | tf_op jit(solution)/shard_map/dot_general | solution.py:107
  347.6 16.2 %convolution_convert_fusion.1 = bf16[1024,2816]{1,0:T(8,128)(2,1)S(1)} fusion(bf16[2048,1024]{1,0:T(8,128)(2,1)S(1)} %copy-done.19, bf16[2048,2816]{1,0:T(8,128)(2,1)} %get-tuple-element.62), kind=kOutput, calls=%fused_computation.10 | convolution fusion | flops 11814043648 | bytes 21495808 | tf_op jit(solution)/shard_map/dot_general | solution.py:107
  366.4 14.4 %convolution_convert_fusion.2 = bf16[1024,2816]{1,0:T(8,128)(2,1)S(1)} fusion(bf16[2048,1024]{1,0:T(8,128)(2,1)} %get-tuple-element.60, bf16[2048,2816]{1,0:T(8,128)(2,1)S(1)} %bitcast.458), kind=kOutput, calls=%fused_computation.11 | convolution fusion | flops 11814043648 | bytes 21495808 | tf_op jit(solution)/shard_map/dot_general | solution.py:107
  384.9 8.2 %convolution_convert_fusion.3 = bf16[1024,1024]{1,0:T(8,128)(2,1)S(1)} fusion(bf16[2048,1024]{1,0:T(8,128)(2,1)} %get-tuple-element.57, bf16[2048,1024]{1,0:T(8,128)(2,1)} %get-tuple-element.58), kind=kOutput, calls=%fused_computation.52 | convolution fusion | flops 4296015872 | bytes 10485760 | tf_op jit(solution)/shard_map/dot_general | solution.py:107
  396.2 4.9 convolution_convert_fusion.4
  406.0 37.4 %shard_map.207 = (bf16[2048,1024]{1,0:T(8,128)(2,1)}, bf16[2048,1024]{1,0:T(8,128)(2,1)}, bf16[2048,1024]{1,0:T(8,128)(2,1)}) custom-call(bf16[2048,1024]{1,0:T(8,128)(2,1)} %get-tuple-element.39.refs_0_.refs_10_, bf16[2048,1024]{1,0:T(8,128)(2,1)} %get-tuple-element.40.refs_1_, bf16[2048,1024]{1,0:T(8,128)(2,1)} %get-tuple-element.41.refs_2_, ...), custom_call_target="tpu_custom_call" | custom-call | flops 25769803776 | bytes 26738688 | tf_op jit(solution)/shard_map/pallas_call | solution.py:314
  443.4 8.2 %convolution_convert_fusion.5 = bf16[1024,1024]{1,0:T(8,128)(2,1)S(1)} fusion(bf16[2048,1024]{1,0:T(8,128)(2,1)} %get-tuple-element.38.normed, bf16[2048,1024]{1,0:T(8,128)(2,1)} %get-tuple-element.54.grad_value), kind=kOutput, calls=%fused_computation.54 | convolution fusion | flops 4296015872 | bytes 10485760 | tf_op jit(solution)/shard_map/dot_general | solution.py:107
  454.5 4.8 convolution_convert_fusion.6
  460.5 26.9 %shard_map.208 = f32[2048,1024]{1,0:T(8,128)} custom-call(bf16[2048,1024]{1,0:T(8,128)(2,1)} %get-tuple-element.52.grad_query, bf16[2048,1024]{1,0:T(8,128)(2,1)} %get-tuple-element.53.grad_key, bf16[2048,1024]{1,0:T(8,128)(2,1)} %get-tuple-element.54.grad_value, bf16[2048,1024]{1,0:T(8,128)(2,1)} %get-tuple-element.55.grad_gate, ...), custom_call_target="tpu_custom_call" | custom-call | flops 17179869184 | bytes 37748736 | tf_op jit(solution)/shard_map/pallas_call | solution.py:314
  487.4 8.0 %convolution_convert_fusion.7 = bf16[1024,1024]{1,0:T(8,128)(2,1)S(1)} fusion(bf16[2048,1024]{1,0:T(8,128)(2,1)} %get-tuple-element.38.normed, bf16[2048,1024]{1,0:T(8,128)(2,1)} %get-tuple-element.52.grad_query), kind=kOutput, calls=%fused_computation.56 | convolution fusion | flops 4296015872 | bytes 10485760 | tf_op jit(solution)/shard_map/dot_general | solution.py:107
  506.1 8.5 %collective-permute-done.58 = bf16[2,2,2,32,1024]{4,3,0,1,2:T(8,128)(2,1)S(1)} collective-permute-done((bf16[2,2,2,32,1024]{4,3,0,1,2:T(8,128)(2,1)S(1)}, bf16[2,2,2,32,1024]{4,3,0,1,2:T(8,128)(2,1)S(1)}, u32[]{:S(2)}, u32[]{:S(2)}) %collective-permute-start.58) | collective-permute-done | bytes 524320 | tf_op jit(solution)/shard_map/ppermute | solution.py:81
  520.5 14.3 %collective-permute-done.59 = bf16[2,2,32,1024]{3,2,0,1:T(8,128)(2,1)S(1)} collective-permute-done((bf16[2,2,32,1024]{3,2,0,1:T(8,128)(2,1)S(1)}, bf16[2,2,32,1024]{3,2,0,1:T(8,128)(2,1)S(1)}, u32[]{:S(2)}, u32[]{:S(2)}) %collective-permute-start.59) | collective-permute-done | bytes 262176 | tf_op jit(solution)/shard_map/ppermute | solution.py:81
  536.8 11.1 %collective-permute-done.43 = bf16[2,2,2,32,1024]{4,3,0,1,2:T(8,128)(2,1)S(1)} collective-permute-done((bf16[2,2,2,32,1024]{4,3,0,1,2:T(8,128)(2,1)S(1)}, bf16[2,2,2,32,1024]{4,3,0,1,2:T(8,128)(2,1)S(1)}, u32[]{:S(2)}, u32[]{:S(2)}) %collective-permute-start.43) | collective-permute-done | bytes 524320 | tf_op jit(solution)/shard_map/ppermute | solution.py:81
  550.5 7.5 %collective-permute-done.60 = bf16[2,32,1024]{2,1,0:T(8,128)(2,1)S(1)} collective-permute-done((bf16[2,32,1024]{2,1,0:T(8,128)(2,1)S(1)}, bf16[2,32,1024]{2,1,0:T(8,128)(2,1)S(1)}, u32[]{:S(2)}, u32[]{:S(2)}) %collective-permute-start.60) | collective-permute-done | bytes 131104 | tf_op jit(solution)/shard_map/ppermute | solution.py:81
  560.4 3.7 collective-permute-done.61
  566.0 5.8 collective-permute-done.54
  574.1 4.1 collective-permute-done.44
  580.5 2.7 collective-permute-done.55
  596.9 2.9 collective-permute-done.46
  600.5 3.2 fusion
  611.6 19.0 %collective-permute-done.78 = bf16[2,2,2,88,1024]{4,3,0,1,2:T(8,128)(2,1)S(1)} collective-permute-done((bf16[2,2,2,88,1024]{4,3,0,1,2:T(8,128)(2,1)S(1)}, bf16[2,2,2,88,1024]{4,3,0,1,2:T(8,128)(2,1)S(1)}, u32[]{:S(2)}, u32[]{:S(2)}) %collective-permute-start.78) | collective-permute-done | bytes 1441824 | tf_op jit(solution)/shard_map/ppermute | solution.py:81
  634.3 3.8 collective-permute-start.74
  638.1 3.2 collective-permute-done.68
  641.9 11.0 %collective-permute-done.79 = bf16[2,2,88,1024]{3,2,0,1:T(8,128)(2,1)S(1)} collective-permute-done((bf16[2,2,88,1024]{3,2,0,1:T(8,128)(2,1)S(1)}, bf16[2,2,88,1024]{3,2,0,1:T(8,128)(2,1)S(1)}, u32[]{:S(2)}, u32[]{:S(2)}) %collective-permute-start.79) | collective-permute-done | bytes 720928 | tf_op jit(solution)/shard_map/ppermute | solution.py:81
  657.2 3.1 collective-permute-start.70
  663.4 2.6 collective-permute-start.76
  666.6 10.0 %collective-permute-done.76 = bf16[32,2816]{1,0:T(8,128)(2,1)S(1)} collective-permute-done((bf16[32,2816]{1,0:T(8,128)(2,1)S(1)}, bf16[32,2816]{1,0:T(8,128)(2,1)S(1)}, u32[]{:S(2)}, u32[]{:S(2)}) %collective-permute-start.76) | collective-permute-done | bytes 180256 | tf_op jit(solution)/shard_map/ppermute | solution.py:81
  (364 shorter events, 169.4 us)
Async XLA Ops:
  0.7 51.3 %collective-permute-start.36 = (bf16[88,1024]{1,0:T(8,128)(2,1)}, bf16[88,1024]{1,0:T(8,128)(2,1)S(1)}, u32[]{:S(2)}, u32[]{:S(2)}) collective-permute-start(bf16[88,1024]{1,0:T(8,128)(2,1)} %param.22), channel_id=1, source_target_pairs={{0,16},{2,18},{4,20},{6,22},{8,24},{10,26},{12,28},{14,30},{16,0},... | collective-permute-start | bytes 540680 | tf_op jit(solution)/shard_map/ppermute | solution.py:59
  4.8 44.2 %collective-permute-start.26 = (bf16[32,2816]{1,0:T(8,128)(2,1)}, bf16[32,2816]{1,0:T(8,128)(2,1)S(1)}, u32[]{:S(2)}, u32[]{:S(2)}) collective-permute-start(bf16[32,2816]{1,0:T(8,128)(2,1)} %param.20), channel_id=1, source_target_pairs={{0,16},{2,18},{4,20},{6,22},{8,24},{10,26},{12,28},{14,30},{16,0},... | collective-permute-start | bytes 540680 | tf_op jit(solution)/shard_map/ppermute | solution.py:59
  4.8 45.7 %collective-permute-start.31 = (bf16[32,2816]{1,0:T(8,128)(2,1)}, bf16[32,2816]{1,0:T(8,128)(2,1)S(1)}, u32[]{:S(2)}, u32[]{:S(2)}) collective-permute-start(bf16[32,2816]{1,0:T(8,128)(2,1)} %param.21), channel_id=1, source_target_pairs={{0,16},{2,18},{4,20},{6,22},{8,24},{10,26},{12,28},{14,30},{16,0},... | collective-permute-start | bytes 540680 | tf_op jit(solution)/shard_map/ppermute | solution.py:59
  7.7 26.1 %collective-permute-start.10 = (bf16[32,1024]{1,0:T(8,128)(2,1)}, bf16[32,1024]{1,0:T(8,128)(2,1)S(1)}, u32[]{:S(2)}, u32[]{:S(2)}) collective-permute-start(bf16[32,1024]{1,0:T(8,128)(2,1)} %param.14), channel_id=1, source_target_pairs={{0,16},{2,18},{4,20},{6,22},{8,24},{10,26},{12,28},{14,30},{16,0},... | collective-permute-start | bytes 196616 | tf_op jit(solution)/shard_map/ppermute | solution.py:59
  7.8 26.7 %collective-permute-start.15 = (bf16[32,1024]{1,0:T(8,128)(2,1)}, bf16[32,1024]{1,0:T(8,128)(2,1)S(1)}, u32[]{:S(2)}, u32[]{:S(2)}) collective-permute-start(bf16[32,1024]{1,0:T(8,128)(2,1)} %param.17), channel_id=1, source_target_pairs={{0,16},{2,18},{4,20},{6,22},{8,24},{10,26},{12,28},{14,30},{16,0},... | collective-permute-start | bytes 196616 | tf_op jit(solution)/shard_map/ppermute | solution.py:59
  52.6 37.9 %collective-permute-start.37 = (bf16[2,88,1024]{2,1,0:T(8,128)(2,1)S(1)}, bf16[2,88,1024]{2,1,0:T(8,128)(2,1)S(1)}, u32[]{:S(2)}, u32[]{:S(2)}) collective-permute-start(bf16[2,88,1024]{2,1,0:T(8,128)(2,1)S(1)} %pad_maximum_fusion.29), channel_id=1, source_target_pairs={{0,1},{1,0},{2,3},{3,2},{4,5},{5,4},{6,7},{7,6},{8,9},{9,8},{10,11... | collective-permute-start | bytes 1081352 | tf_op jit(solution)/shard_map/ppermute | solution.py:59
  57.0 31.9 %collective-permute-start.32 = (bf16[2,32,2816]{2,1,0:T(8,128)(2,1)S(1)}, bf16[2,32,2816]{2,1,0:T(8,128)(2,1)S(1)}, u32[]{:S(2)}, u32[]{:S(2)}) collective-permute-start(bf16[2,32,2816]{2,1,0:T(8,128)(2,1)S(1)} %pad_maximum_fusion.28), channel_id=1, source_target_pairs={{0,8},{2,10},{4,12},{6,14},{8,0},{10,2},{12,4},{14,6},{16,24},{18,... | collective-permute-start | bytes 1081352 | tf_op jit(solution)/shard_map/ppermute | solution.py:59
  58.2 30.8 %collective-permute-start.27 = (bf16[2,32,2816]{2,1,0:T(8,128)(2,1)S(1)}, bf16[2,32,2816]{2,1,0:T(8,128)(2,1)S(1)}, u32[]{:S(2)}, u32[]{:S(2)}) collective-permute-start(bf16[2,32,2816]{2,1,0:T(8,128)(2,1)S(1)} %pad_maximum_fusion.27), channel_id=1, source_target_pairs={{0,4},{2,6},{4,0},{6,2},{8,12},{10,14},{12,8},{14,10},{16,20},{18,... | collective-permute-start | bytes 1081352 | tf_op jit(solution)/shard_map/ppermute | solution.py:59
  58.9 11.6 %collective-permute-start.17 = (bf16[2,2,32,1024]{3,2,0,1:T(8,128)(2,1)S(1)}, bf16[2,2,32,1024]{3,2,0,1:T(8,128)(2,1)S(1)}, u32[]{:S(2)}, u32[]{:S(2)}) collective-permute-start(bf16[2,2,32,1024]{3,2,0,1:T(8,128)(2,1)S(1)} %pad_maximum_fusion.34), channel_id=1, source_target_pairs={{0,4},{2,6},{4,0},{6,2},{8,12},{10,14},{12,8},{14,10},{16,20},{18,... | collective-permute-start | bytes 786440 | tf_op jit(solution)/shard_map/ppermute | solution.py:59
  79.1 14.9 %collective-permute-start.18 = (bf16[2,2,2,32,1024]{4,3,0,1,2:T(8,128)(2,1)S(1)}, bf16[2,2,2,32,1024]{4,3,0,1,2:T(8,128)(2,1)S(1)}, u32[]{:S(2)}, u32[]{:S(2)}) collective-permute-start(bf16[2,2,2,32,1024]{4,3,0,1,2:T(8,128)(2,1)S(1)} %pad_maximum_fusion.26), channel_id=1, source_target_pairs={{0,1},{1,0},{2,3},{3,2},{4,5},{5,4},{6,7},{7,6},{8,9},{9,8},{10,11... | collective-permute-start | bytes 1572872 | tf_op jit(solution)/shard_map/ppermute | solution.py:59
  88.9 14.3 %collective-permute-start.8 = (bf16[2,2,2,32,1024]{4,3,0,2,1:T(8,128)(2,1)S(1)}, bf16[2,2,2,32,1024]{4,3,0,2,1:T(8,128)(2,1)S(1)}, u32[]{:S(2)}, u32[]{:S(2)}) collective-permute-start(bf16[2,2,2,32,1024]{4,3,0,2,1:T(8,128)(2,1)S(1)} %pad_maximum_fusion.24), channel_id=1, source_target_pairs={{0,4},{2,6},{4,0},{6,2},{8,12},{10,14},{12,8},{14,10},{16,20},{18,... | collective-permute-start | bytes 1572872 | tf_op jit(solution)/shard_map/ppermute | solution.py:59
  89.1 16.0 %collective-permute-start.3 = (bf16[2,2,2,32,1024]{4,3,0,1,2:T(8,128)(2,1)S(1)}, bf16[2,2,2,32,1024]{4,3,0,1,2:T(8,128)(2,1)S(1)}, u32[]{:S(2)}, u32[]{:S(2)}) collective-permute-start(bf16[2,2,2,32,1024]{4,3,0,1,2:T(8,128)(2,1)S(1)} %pad_maximum_fusion.23), channel_id=1, source_target_pairs={{0,1},{1,0},{2,3},{3,2},{4,5},{5,4},{6,7},{7,6},{8,9},{9,8},{10,11... | collective-permute-start | bytes 1572872 | tf_op jit(solution)/shard_map/ppermute | solution.py:59
  90.5 19.0 %collective-permute-start.24 = (bf16[2,2,2,32,1152]{4,3,0,2,1:T(8,128)(2,1)S(1)}, bf16[2,2,2,32,1152]{4,3,0,2,1:T(8,128)(2,1)S(1)}, u32[]{:S(2)}, u32[]{:S(2)}) collective-permute-start(bf16[2,2,2,32,1152]{4,3,0,2,1:T(8,128)(2,1)S(1)} %pad_maximum_fusion.22), channel_id=1, source_target_pairs={{0,4},{2,6},{4,0},{6,2},{8,12},{10,14},{12,8},{14,10},{16,20},{18,... | collective-permute-start | bytes 1769480 | tf_op jit(solution)/shard_map/ppermute | solution.py:59
  94.0 25.4 %collective-permute-start.38 = (bf16[2,2,88,1024]{3,2,0,1:T(8,128)(2,1)S(1)}, bf16[2,2,88,1024]{3,2,0,1:T(8,128)(2,1)S(1)}, u32[]{:S(2)}, u32[]{:S(2)}) collective-permute-start(bf16[2,2,88,1024]{3,2,0,1:T(8,128)(2,1)S(1)} %pad_maximum_fusion.21), channel_id=1, source_target_pairs={{0,8},{2,10},{4,12},{6,14},{8,0},{10,2},{12,4},{14,6},{16,24},{18,... | collective-permute-start | bytes 2162696 | tf_op jit(solution)/shard_map/ppermute | solution.py:59
  98.9 18.3 %collective-permute-start.33 = (bf16[2,2,32,2816]{3,2,0,1:T(8,128)(2,1)S(1)}, bf16[2,2,32,2816]{3,2,0,1:T(8,128)(2,1)S(1)}, u32[]{:S(2)}, u32[]{:S(2)}) collective-permute-start(bf16[2,2,32,2816]{3,2,0,1:T(8,128)(2,1)S(1)} %pad_maximum_fusion.20), channel_id=1, source_target_pairs={{0,4},{2,6},{4,0},{6,2},{8,12},{10,14},{12,8},{14,10},{16,20},{18,... | collective-permute-start | bytes 2162696 | tf_op jit(solution)/shard_map/ppermute | solution.py:59
  103.2 14.2 %collective-permute-start.28 = (bf16[2,2,32,2816]{3,2,0,1:T(8,128)(2,1)S(1)}, bf16[2,2,32,2816]{3,2,0,1:T(8,128)(2,1)S(1)}, u32[]{:S(2)}, u32[]{:S(2)}) collective-permute-start(bf16[2,2,32,2816]{3,2,0,1:T(8,128)(2,1)S(1)} %pad_maximum_fusion.19), channel_id=1, source_target_pairs={{0,1},{1,0},{2,3},{3,2},{4,5},{5,4},{6,7},{7,6},{8,9},{9,8},{10,11... | collective-permute-start | bytes 2162696 | tf_op jit(solution)/shard_map/ppermute | solution.py:59
  105.1 16.9 %collective-permute-start.19 = (bf16[2,2,2,2,32,1024]{5,4,0,1,2,3:T(8,128)(2,1)S(1)}, bf16[2,2,2,2,32,1024]{5,4,0,1,2,3:T(8,128)(2,1)S(1)}, u32[]{:S(2)}, u32[]{:S(2)}) collective-permute-start(bf16[2,2,2,2,32,1024]{5,4,0,1,2,3:T(8,128)(2,1)S(1)} %pad_maximum_fusion.18), channel_id=1, source_target_pairs={{0,2},{2,0},{4,6},{6,4},{8,10},{10,8},{12,14},{14,12},{16,18},{18,... | collective-permute-start | bytes 3145736 | tf_op jit(solution)/shard_map/ppermute | solution.py:59
  109.5 39.0 %collective-permute-start.14 = (bf16[2,2,2,2,32,1024]{5,4,0,1,2,3:T(8,128)(2,1)}, bf16[2,2,2,2,32,1024]{5,4,0,1,2,3:T(8,128)(2,1)}, u32[]{:S(2)}, u32[]{:S(2)}) collective-permute-start(bf16[2,2,2,2,32,1024]{5,4,0,1,2,3:T(8,128)(2,1)} %pad_maximum_fusion.17), channel_id=1, source_target_pairs={{0,2},{2,0},{4,6},{6,4},{8,10},{10,8},{12,14},{14,12},{16,18},{18,... | collective-permute-start | bytes 3145736 | tf_op jit(solution)/shard_map/ppermute | solution.py:59
  119.4 48.3 %collective-permute-start.25 = (bf16[2,2,2,2,32,1152]{5,4,0,3,1,2:T(8,128)(2,1)}, bf16[2,2,2,2,32,1152]{5,4,0,3,1,2:T(8,128)(2,1)}, u32[]{:S(2)}, u32[]{:S(2)}) collective-permute-start(bf16[2,2,2,2,32,1152]{5,4,0,3,1,2:T(8,128)(2,1)} %pad_maximum_fusion.14), channel_id=1, source_target_pairs={{0,2},{2,0},{4,6},{6,4},{8,10},{10,8},{12,14},{14,12},{16,18},{18,... | collective-permute-start | bytes 3538952 | tf_op jit(solution)/shard_map/ppermute | solution.py:59
  122.0 51.1 %collective-permute-start.39 = (bf16[2,2,2,88,1024]{4,3,0,2,1:T(8,128)(2,1)}, bf16[2,2,2,88,1024]{4,3,0,2,1:T(8,128)(2,1)}, u32[]{:S(2)}, u32[]{:S(2)}) collective-permute-start(bf16[2,2,2,88,1024]{4,3,0,2,1:T(8,128)(2,1)} %pad_maximum_fusion.13), channel_id=1, source_target_pairs={{0,4},{2,6},{4,0},{6,2},{8,12},{10,14},{12,8},{14,10},{16,20},{18,... | collective-permute-start | bytes 4325384 | tf_op jit(solution)/shard_map/ppermute | solution.py:59
  122.5 53.9 %collective-permute-start.34 = (bf16[2,2,2,32,2816]{4,3,0,1,2:T(8,128)(2,1)}, bf16[2,2,2,32,2816]{4,3,0,1,2:T(8,128)(2,1)}, u32[]{:S(2)}, u32[]{:S(2)}) collective-permute-start(bf16[2,2,2,32,2816]{4,3,0,1,2:T(8,128)(2,1)} %pad_maximum_fusion.12), channel_id=1, source_target_pairs={{0,1},{1,0},{2,3},{3,2},{4,5},{5,4},{6,7},{7,6},{8,9},{9,8},{10,11... | collective-permute-start | bytes 4325384 | tf_op jit(solution)/shard_map/ppermute | solution.py:59
  123.6 56.7 %collective-permute-start.29 = (bf16[2,2,2,32,2816]{4,3,0,1,2:T(8,128)(2,1)}, bf16[2,2,2,32,2816]{4,3,0,1,2:T(8,128)(2,1)}, u32[]{:S(2)}, u32[]{:S(2)}) collective-permute-start(bf16[2,2,2,32,2816]{4,3,0,1,2:T(8,128)(2,1)} %pad_maximum_fusion.11), channel_id=1, source_target_pairs={{0,8},{2,10},{4,12},{6,14},{8,0},{10,2},{12,4},{14,6},{16,24},{18,... | collective-permute-start | bytes 4325384 | tf_op jit(solution)/shard_map/ppermute | solution.py:59
  151.6 20.6 %collective-permute-start.20 = (bf16[2,64,1024]{2,1,0:T(8,128)(2,1)S(1)}, bf16[2,64,1024]{2,1,0:T(8,128)(2,1)S(1)}, u32[]{:S(2)}, u32[]{:S(2)}) collective-permute-start(bf16[2,64,1024]{2,1,0:T(8,128)(2,1)S(1)} %convert_element_type.504), channel_id=1, source_target_pairs={{0,1},{2,3},{4,5},{6,7},{8,9},{10,11},{12,13},{14,15},{16,17},{18,... | collective-permute-start | bytes 786440 | tf_op jit(solution)/shard_map/ppermute | solution.py:94
  176.4 30.8 %collective-permute-start.40 = (bf16[2,2,2,2,88,1024]{5,4,0,3,1,2:T(8,128)(2,1)}, bf16[2,2,2,2,88,1024]{5,4,0,3,1,2:T(8,128)(2,1)}, u32[]{:S(2)}, u32[]{:S(2)}) collective-permute-start(bf16[2,2,2,2,88,1024]{5,4,0,3,1,2:T(8,128)(2,1)} %pad_maximum_fusion.5), channel_id=1, source_target_pairs={{0,2},{2,0},{4,6},{6,4},{8,10},{10,8},{12,14},{14,12},{16,18},{18,... | collective-permute-start | bytes 8650760 | tf_op jit(solution)/shard_map/ppermute | solution.py:59
  179.8 33.2 %collective-permute-start.35 = (bf16[2,2,2,2,32,2816]{5,4,0,1,2,3:T(8,128)(2,1)}, bf16[2,2,2,2,32,2816]{5,4,0,1,2,3:T(8,128)(2,1)}, u32[]{:S(2)}, u32[]{:S(2)}) collective-permute-start(bf16[2,2,2,2,32,2816]{5,4,0,1,2,3:T(8,128)(2,1)} %pad_maximum_fusion.4), channel_id=1, source_target_pairs={{0,2},{2,0},{4,6},{6,4},{8,10},{10,8},{12,14},{14,12},{16,18},{18,... | collective-permute-start | bytes 8650760 | tf_op jit(solution)/shard_map/ppermute | solution.py:59
  183.9 34.5 %collective-permute-start.30 = (bf16[2,2,2,2,32,2816]{5,4,0,1,2,3:T(8,128)(2,1)}, bf16[2,2,2,2,32,2816]{5,4,0,1,2,3:T(8,128)(2,1)}, u32[]{:S(2)}, u32[]{:S(2)}) collective-permute-start(bf16[2,2,2,2,32,2816]{5,4,0,1,2,3:T(8,128)(2,1)} %pad_maximum_fusion.3), channel_id=1, source_target_pairs={{0,2},{2,0},{4,6},{6,4},{8,10},{10,8},{12,14},{14,12},{16,18},{18,... | collective-permute-start | bytes 8650760 | tf_op jit(solution)/shard_map/ppermute | solution.py:59
  347.1 253.4 %collective-permute-start.77 = (bf16[2,2,2,2,88,1024]{5,4,0,1,2,3:T(8,128)(2,1)}, bf16[2,2,2,2,88,1024]{5,4,0,1,2,3:T(8,128)(2,1)}, u32[]{:S(2)}, u32[]{:S(2)}) collective-permute-start(bf16[2,2,2,2,88,1024]{5,4,0,1,2,3:T(8,128)(2,1)} %bitcast.417), channel_id=1, source_target_pairs={{0,2},{2,0},{4,6},{6,4},{8,10},{10,8},{12,14},{14,12},{16,18},{18,... | collective-permute-start | bytes 8650760 | tf_op jit(solution)/shard_map/ppermute | solution.py:81
  366.2 238.6 %collective-permute-start.72 = (bf16[2,2,2,2,32,2816]{5,4,0,2,3,1:T(8,128)(2,1)}, bf16[2,2,2,2,32,2816]{5,4,0,2,3,1:T(8,128)(2,1)}, u32[]{:S(2)}, u32[]{:S(2)}) collective-permute-start(bf16[2,2,2,2,32,2816]{5,4,0,2,3,1:T(8,128)(2,1)} %bitcast.418), channel_id=1, source_target_pairs={{0,2},{2,0},{4,6},{6,4},{8,10},{10,8},{12,14},{14,12},{16,18},{18,... | collective-permute-start | bytes 8650760 | tf_op jit(solution)/shard_map/ppermute | solution.py:81
  394.5 103.9 %collective-permute-start.62 = (bf16[2,2,2,2,32,1152]{5,4,0,3,1,2:T(8,128)(2,1)}, bf16[2,2,2,2,32,1152]{5,4,0,3,1,2:T(8,128)(2,1)}, u32[]{:S(2)}, u32[]{:S(2)}) collective-permute-start(bf16[2,2,2,2,32,1152]{5,4,0,3,1,2:T(8,128)(2,1)} %fusion.15), channel_id=1, source_target_pairs={{0,2},{2,0},{4,6},{6,4},{8,10},{10,8},{12,14},{14,12},{16,18},{18,... | collective-permute-start | bytes 3538952 | tf_op jit(solution)/shard_map/ppermute | solution.py:81
  402.5 93.3 %collective-permute-start.57 = (bf16[2,2,2,2,32,1024]{5,4,0,1,2,3:T(8,128)(2,1)}, bf16[2,2,2,2,32,1024]{5,4,0,1,2,3:T(8,128)(2,1)}, u32[]{:S(2)}, u32[]{:S(2)}) collective-permute-start(bf16[2,2,2,2,32,1024]{5,4,0,1,2,3:T(8,128)(2,1)} %bitcast.420), channel_id=1, source_target_pairs={{0,2},{2,0},{4,6},{6,4},{8,10},{10,8},{12,14},{14,12},{16,18},{18,... | collective-permute-start | bytes 3145736 | tf_op jit(solution)/shard_map/ppermute | solution.py:81
  453.9 46.7 %collective-permute-start.52 = (bf16[2,2,2,2,32,1024]{5,4,0,2,3,1:T(8,128)(2,1)}, bf16[2,2,2,2,32,1024]{5,4,0,2,3,1:T(8,128)(2,1)}, u32[]{:S(2)}, u32[]{:S(2)}) collective-permute-start(bf16[2,2,2,2,32,1024]{5,4,0,2,3,1:T(8,128)(2,1)} %bitcast.421), channel_id=1, source_target_pairs={{0,2},{2,0},{4,6},{6,4},{8,10},{10,8},{12,14},{14,12},{16,18},{18,... | collective-permute-start | bytes 3145736 | tf_op jit(solution)/shard_map/ppermute | solution.py:81
  500.6 14.0 %collective-permute-start.58 = (bf16[2,2,2,32,1024]{4,3,0,1,2:T(8,128)(2,1)S(1)}, bf16[2,2,2,32,1024]{4,3,0,1,2:T(8,128)(2,1)S(1)}, u32[]{:S(2)}, u32[]{:S(2)}) collective-permute-start(bf16[2,2,2,32,1024]{4,3,0,1,2:T(8,128)(2,1)S(1)} %dynamic-slice_bitcast_fusion.7), channel_id=1, source_target_pairs={{0,1},{1,0},{2,3},{3,2},{4,5},{5,4},{6,7},{7,6},{8,9},{9,8},{10,11... | collective-permute-start | bytes 1572872 | tf_op jit(solution)/shard_map/ppermute | solution.py:81
  502.5 16.2 %collective-permute-start.63 = (bf16[2,2,2,32,1152]{4,3,0,2,1:T(8,128)(2,1)S(1)}, bf16[2,2,2,32,1152]{4,3,0,2,1:T(8,128)(2,1)S(1)}, u32[]{:S(2)}, u32[]{:S(2)}) collective-permute-start(bf16[2,2,2,32,1152]{4,3,0,2,1:T(8,128)(2,1)S(1)} %dynamic-slice_bitcast_fusion.6), channel_id=1, source_target_pairs={{0,4},{2,6},{4,0},{6,2},{8,12},{10,14},{12,8},{14,10},{16,20},{18,... | collective-permute-start | bytes 1769480 | tf_op jit(solution)/shard_map/ppermute | solution.py:81
  504.5 44.5 %collective-permute-start.53 = (bf16[2,2,2,32,1024]{4,3,0,1,2:T(8,128)(2,1)S(1)}, bf16[2,2,2,32,1024]{4,3,0,1,2:T(8,128)(2,1)S(1)}, u32[]{:S(2)}, u32[]{:S(2)}) collective-permute-start(bf16[2,2,2,32,1024]{4,3,0,1,2:T(8,128)(2,1)S(1)} %dynamic-slice_bitcast_fusion.8), channel_id=1, source_target_pairs={{0,8},{2,10},{4,12},{6,14},{8,0},{10,2},{12,4},{14,6},{16,24},{18,... | collective-permute-start | bytes 1572872 | tf_op jit(solution)/shard_map/ppermute | solution.py:81
  514.6 21.9 %collective-permute-start.48 = (bf16[2,2,2,32,1024]{4,3,0,2,1:T(8,128)(2,1)S(1)}, bf16[2,2,2,32,1024]{4,3,0,2,1:T(8,128)(2,1)S(1)}, u32[]{:S(2)}, u32[]{:S(2)}) collective-permute-start(bf16[2,2,2,32,1024]{4,3,0,2,1:T(8,128)(2,1)S(1)} %dynamic-slice_bitcast_fusion.9), channel_id=1, source_target_pairs={{0,4},{2,6},{4,0},{6,2},{8,12},{10,14},{12,8},{14,10},{16,20},{18,... | collective-permute-start | bytes 1572872 | tf_op jit(solution)/shard_map/ppermute | solution.py:81
  518.7 16.1 %collective-permute-start.59 = (bf16[2,2,32,1024]{3,2,0,1:T(8,128)(2,1)S(1)}, bf16[2,2,32,1024]{3,2,0,1:T(8,128)(2,1)S(1)}, u32[]{:S(2)}, u32[]{:S(2)}) collective-permute-start(bf16[2,2,32,1024]{3,2,0,1:T(8,128)(2,1)S(1)} %dynamic-slice_bitcast_fusion.15), channel_id=1, source_target_pairs={{0,4},{2,6},{4,0},{6,2},{8,12},{10,14},{12,8},{14,10},{16,20},{18,... | collective-permute-start | bytes 786440 | tf_op jit(solution)/shard_map/ppermute | solution.py:81
  534.8 13.2 %collective-permute-start.43 = (bf16[2,2,2,32,1024]{4,3,0,1,2:T(8,128)(2,1)S(1)}, bf16[2,2,2,32,1024]{4,3,0,1,2:T(8,128)(2,1)S(1)}, u32[]{:S(2)}, u32[]{:S(2)}) collective-permute-start(bf16[2,2,2,32,1024]{4,3,0,1,2:T(8,128)(2,1)S(1)} %dynamic-slice_bitcast_fusion.10), channel_id=1, source_target_pairs={{0,1},{1,0},{2,3},{3,2},{4,5},{5,4},{6,7},{7,6},{8,9},{9,8},{10,11... | collective-permute-start | bytes 1572872 | tf_op jit(solution)/shard_map/ppermute | solution.py:81
  536.5 71.0 %collective-permute-start.67 = (bf16[2,2,2,2,32,2816]{5,4,0,3,1,2:T(8,128)(2,1)S(1)}, bf16[2,2,2,2,32,2816]{5,4,0,3,1,2:T(8,128)(2,1)S(1)}, u32[]{:S(2)}, u32[]{:S(2)}) collective-permute-start(bf16[2,2,2,2,32,2816]{5,4,0,3,1,2:T(8,128)(2,1)S(1)} %bitcast.434), channel_id=1, source_target_pairs={{0,2},{2,0},{4,6},{6,4},{8,10},{10,8},{12,14},{14,12},{16,18},{18,... | collective-permute-start | bytes 8650760 | tf_op jit(solution)/shard_map/ppermute | solution.py:81
  547.9 17.6 %collective-permute-start.64 = (bf16[2,2,32,1152]{3,2,0,1:T(8,128)(2,1)S(1)}, bf16[2,2,32,1152]{3,2,0,1:T(8,128)(2,1)S(1)}, u32[]{:S(2)}, u32[]{:S(2)}) collective-permute-start(bf16[2,2,32,1152]{3,2,0,1:T(8,128)(2,1)S(1)} %dynamic-slice_bitcast_fusion.14), channel_id=1, source_target_pairs={{0,8},{2,10},{4,12},{6,14},{8,0},{10,2},{12,4},{14,6},{16,24},{18,... | collective-permute-start | bytes 884744 | tf_op jit(solution)/shard_map/ppermute | solution.py:81
  604.1 26.5 %collective-permute-start.78 = (bf16[2,2,2,88,1024]{4,3,0,1,2:T(8,128)(2,1)S(1)}, bf16[2,2,2,88,1024]{4,3,0,1,2:T(8,128)(2,1)S(1)}, u32[]{:S(2)}, u32[]{:S(2)}) collective-permute-start(bf16[2,2,2,88,1024]{4,3,0,1,2:T(8,128)(2,1)S(1)} %dynamic-slice_bitcast_fusion), channel_id=1, source_target_pairs={{0,1},{1,0},{2,3},{3,2},{4,5},{5,4},{6,7},{7,6},{8,9},{9,8},{10,11... | collective-permute-start | bytes 4325384 | tf_op jit(solution)/shard_map/ppermute | solution.py:81
  607.5 26.5 %collective-permute-start.73 = (bf16[2,2,2,32,2816]{4,3,0,1,2:T(8,128)(2,1)S(1)}, bf16[2,2,2,32,2816]{4,3,0,1,2:T(8,128)(2,1)S(1)}, u32[]{:S(2)}, u32[]{:S(2)}) collective-permute-start(bf16[2,2,2,32,2816]{4,3,0,1,2:T(8,128)(2,1)S(1)} %dynamic-slice_bitcast_fusion.1), channel_id=1, source_target_pairs={{0,8},{2,10},{4,12},{6,14},{8,0},{10,2},{12,4},{14,6},{16,24},{18,... | collective-permute-start | bytes 4325384 | tf_op jit(solution)/shard_map/ppermute | solution.py:81
  610.1 31.2 %collective-permute-start.68 = (bf16[2,2,2,32,2816]{4,3,0,2,1:T(8,128)(2,1)S(1)}, bf16[2,2,2,32,2816]{4,3,0,2,1:T(8,128)(2,1)S(1)}, u32[]{:S(2)}, u32[]{:S(2)}) collective-permute-start(bf16[2,2,2,32,2816]{4,3,0,2,1:T(8,128)(2,1)S(1)} %dynamic-slice_bitcast_fusion.2), channel_id=1, source_target_pairs={{0,4},{2,6},{4,0},{6,2},{8,12},{10,14},{12,8},{14,10},{16,20},{18,... | collective-permute-start | bytes 4325384 | tf_op jit(solution)/shard_map/ppermute | solution.py:81
  631.3 21.6 %collective-permute-start.79 = (bf16[2,2,88,1024]{3,2,0,1:T(8,128)(2,1)S(1)}, bf16[2,2,88,1024]{3,2,0,1:T(8,128)(2,1)S(1)}, u32[]{:S(2)}, u32[]{:S(2)}) collective-permute-start(bf16[2,2,88,1024]{3,2,0,1:T(8,128)(2,1)S(1)} %dynamic-slice_bitcast_fusion.3), channel_id=1, source_target_pairs={{0,4},{2,6},{4,0},{6,2},{8,12},{10,14},{12,8},{14,10},{16,20},{18,... | collective-permute-start | bytes 2162696 | tf_op jit(solution)/shard_map/ppermute | solution.py:81
  634.3 19.0 %collective-permute-start.74 = (bf16[2,2,32,2816]{3,2,0,1:T(8,128)(2,1)S(1)}, bf16[2,2,32,2816]{3,2,0,1:T(8,128)(2,1)S(1)}, u32[]{:S(2)}, u32[]{:S(2)}) collective-permute-start(bf16[2,2,32,2816]{3,2,0,1:T(8,128)(2,1)S(1)} %dynamic-slice_bitcast_fusion.4), channel_id=1, source_target_pairs={{0,1},{1,0},{2,3},{3,2},{4,5},{5,4},{6,7},{7,6},{8,9},{9,8},{10,11... | collective-permute-start | bytes 2162696 | tf_op jit(solution)/shard_map/ppermute | solution.py:81
  641.7 15.3 %collective-permute-start.69 = (bf16[2,2,32,2816]{3,2,0,1:T(8,128)(2,1)S(1)}, bf16[2,2,32,2816]{3,2,0,1:T(8,128)(2,1)S(1)}, u32[]{:S(2)}, u32[]{:S(2)}) collective-permute-start(bf16[2,2,32,2816]{3,2,0,1:T(8,128)(2,1)S(1)} %dynamic-slice_bitcast_fusion.5), channel_id=1, source_target_pairs={{0,8},{2,10},{4,12},{6,14},{8,0},{10,2},{12,4},{14,6},{16,24},{18,... | collective-permute-start | bytes 2162696 | tf_op jit(solution)/shard_map/ppermute | solution.py:81
  662.8 14.5 %collective-permute-start.81 = (bf16[88,1024]{1,0:T(8,128)(2,1)S(1)}, bf16[88,1024]{1,0:T(8,128)(2,1)S(1)}, u32[]{:S(2)}, u32[]{:S(2)}) collective-permute-start(bf16[88,1024]{1,0:T(8,128)(2,1)S(1)} %dynamic-slice_bitcast_fusion.19), channel_id=1, source_target_pairs={{0,16},{2,18},{4,20},{6,22},{8,24},{10,26},{12,28},{14,30},{16,0},... | collective-permute-start | bytes 540680 | tf_op jit(solution)/shard_map/ppermute | solution.py:81
  663.4 13.2 %collective-permute-start.76 = (bf16[32,2816]{1,0:T(8,128)(2,1)S(1)}, bf16[32,2816]{1,0:T(8,128)(2,1)S(1)}, u32[]{:S(2)}, u32[]{:S(2)}) collective-permute-start(bf16[32,2816]{1,0:T(8,128)(2,1)S(1)} %dynamic-slice_bitcast_fusion.20), channel_id=1, source_target_pairs={{0,16},{2,18},{4,20},{6,22},{8,24},{10,26},{12,28},{14,30},{16,0},... | collective-permute-start | bytes 540680 | tf_op jit(solution)/shard_map/ppermute | solution.py:81
  666.2 12.4 %collective-permute-start.71 = (bf16[32,2816]{1,0:T(8,128)(2,1)S(1)}, bf16[32,2816]{1,0:T(8,128)(2,1)S(1)}, u32[]{:S(2)}, u32[]{:S(2)}) collective-permute-start(bf16[32,2816]{1,0:T(8,128)(2,1)S(1)} %dynamic-slice_bitcast_fusion.21), channel_id=1, source_target_pairs={{0,16},{2,18},{4,20},{6,22},{8,24},{10,26},{12,28},{14,30},{16,0},... | collective-permute-start | bytes 540680 | tf_op jit(solution)/shard_map/ppermute | solution.py:81
  (57 other events, 577.7 us)

commit v2 on v1

--- a/solution.py
+++ b/solution.py
@@ -1,3 +1,5 @@
+import functools
+
 import jax
 import jax.numpy as jnp
 from jax import lax
@@ -325,7 +327,360 @@
     )(*[a for a, _ in operands])
 
 
-def shards(
+def index_bits():
+    bits = []
+    for axis in ("dp", "fsdp"):
+        count = lax.axis_size(axis).bit_length() - 1
+        bits += [(axis, bit) for bit in reversed(range(count))]
+    return bits
+
+
+def bit_value(bit):
+    axis, at = bit
+    return lax.rem(lax.div(lax.axis_index(axis), 1 << at), 2)
+
+
+def flip_device(bit):
+    axis, at = bit
+    return {axis: lax.axis_index(axis) + (1 - 2 * bit_value(bit)) * (1 << at)}
+
+
+def greet(bits):
+    barrier = pltpu.get_barrier_semaphore()
+    for bit in bits:
+        pl.semaphore_signal(
+            barrier, inc=1, device_id=flip_device(bit), device_id_type=pl.DeviceIdType.MESH
+        )
+    pl.semaphore_wait(barrier, len(bits))
+
+
+class Sems:
+    def __init__(self, send, recv):
+        self.send, self.recv, self.used = send, recv, 0
+
+    def copy(self, src, dst, bit):
+        at = self.used
+        self.used += 1
+        return pltpu.make_async_remote_copy(
+            src_ref=src,
+            dst_ref=dst,
+            send_sem=self.send.at[at],
+            recv_sem=self.recv.at[at],
+            device_id=flip_device(bit),
+            device_id_type=pl.DeviceIdType.MESH,
+        )
+
+
+class Gather:
+    def __init__(self, buf, bits, order, sems, columns=slice(None)):
+        self.stages = []
+        held = []
+
+        def cube(flipped=None):
+            index = []
+            for bit in bits:
+                if bit == flipped:
+                    index.append(1 - bit_value(bit))
+                else:
+                    index.append(slice(None) if bit in held else bit_value(bit))
+            return buf.at[tuple(index) + (slice(None), columns)]
+
+        for bit in order[:-1]:
+            ref = cube()
+            copies = [sems.copy(ref, ref, bit)]
+            if bit == order[-2]:
+                copies.append(sems.copy(ref, ref, order[-1]))
+                far = cube(flipped=bit)
+            self.stages.append(copies)
+            held.append(bit)
+        self.stages.append([sems.copy(far, far, order[-1])])
+
+    def start(self, stage):
+        for copy in self.stages[stage]:
+            copy.start()
+
+    def arrive(self, stage):
+        self.stages[stage][0].wait_recv()
+
+    def advance(self, stage):
+        self.arrive(stage - 1)
+        self.start(stage)
+
+    def finish(self):
+        self.stages[-2][1].wait_recv()
+        self.stages[-1][0].wait_recv()
+
+    def drain(self):
+        for copies in self.stages:
+            for copy in copies:
+                copy.wait_send()
+
+
+FORWARD_COPIES = 80
+
+
+def forward_kernel(
+    steps, per_seq, bits, waves, feed_orders, three_order,
+    tok, s_key, s_value, s_query, s_gate, s_out, s_gain, s_one, s_two, s_three,
+    normed, pre_key, keys, values, pre_query, queries, pre_gate, attended, mixed, residual,
+    prefix, gain_row, full_attn, full_one, full_two, full_three,
+    held, all_keys, all_values, all_normed, totals, state_out, state_in, carry,
+    three_in, three_slab, send, recv, local,
+):
+    step = pl.program_id(0)
+    width = tok.shape[1]
+    last = bits[-1]
+    sems = Sems(send, recv)
+    attn = [
+        [Gather(held, bits, order, sems, columns) for order, columns in wave] for wave in waves
+    ]
+    feed = [
+        Gather(buf, bits, order, sems)
+        for buf, order in zip((full_one, full_two), feed_orders)
+    ]
+    three = Gather(full_three, bits[:-1], three_order, sems)
+    swap_three = sems.copy(s_three, three_in, last)
+    swap_state = sems.copy(state_out, state_in, last)
+    own = tuple(bit_value(bit) for bit in bits)
+    keep_attn = pltpu.make_async_copy(held, full_attn, local.at[3])
+
+    def feed_advance(stage):
+        for piece in feed:
+            piece.advance(stage)
+        if stage > 1:
+            three.advance(stage - 1)
+
+    @pl.when(step == 0)
+    def _():
+        place = [
+            pltpu.make_async_copy(s_one, full_one.at[own], local.at[0]),
+            pltpu.make_async_copy(s_two, full_two.at[own], local.at[1]),
+        ]
+        for copy in place:
+            copy.start()
+        for n, shard in enumerate((s_key, s_value, s_query, s_gate, s_out)):
+            held[own + (slice(None), slice(n * width, (n + 1) * width))] = shard[...]
+        held[own + (slice(None), slice(5 * width, 5 * width + 128))] = s_gain[...]
+        greet(bits)
+        for wave in attn:
+            for piece in wave:
+                piece.start(0)
+        swap_three.start()
+        for copy in place:
+            copy.wait()
+        for stage in range(1, len(bits)):
+            for wave in attn:
+                for piece in wave:
+                    piece.advance(stage)
+            if stage == 1:
+                for piece in feed:
+                    piece.start(0)
+                swap_three.wait_recv()
+                mine = (own[-1] == 0).astype(WIDE)
+                low, high = s_three[...], three_in[...]
+                three_slab[...] = jnp.concatenate(
+                    [mine * low + (1 - mine) * high, mine * high + (1 - mine) * low], axis=0
+                ).astype(LOW)
+                lay = pltpu.make_async_copy(three_slab, full_three.at[own[:-1]], local.at[2])
+                lay.start()
+                lay.wait()
+                three.start(0)
+        for piece in attn[0]:
+            piece.finish()
+        feed_advance(1)
+
+    @pl.when(step == 3)
+    def _():
+        feed_advance(2)
+
+    @pl.when(step == steps)
+    def _():
+        for wave in attn[1:]:
+            for piece in wave:
+                piece.finish()
+        keep_attn.start()
+        column = held[..., 5 * width : 5 * width + 128].reshape(width, 128)
+        gain_row[...] = column.astype(WIDE).T[:1]
+
+    @pl.when(step == steps + 1)
+    def _():
+        feed_advance(3)
+
+    def weight(n):
+        return held[..., n * width : (n + 1) * width].reshape(width, width)
+
+    same = head_square()
+
+    @pl.when(step < steps)
+    def _():
+        x = tok[...].astype(WIDE)
+        rows = (x * rms_scale(x)).astype(LOW)
+        normed[...] = rows
+        here = pl.ds(pl.multiple_of(step * BLOCK, BLOCK), BLOCK)
+        all_normed[here, :] = rows
+        pre = dot_nn(rows, weight(0))
+        pre_key[...] = pre.astype(LOW)
+        k = jax.nn.silu(pre).astype(LOW)
+        keys[...] = k
+        all_keys[here, :] = k
+        v = dot_nn(rows, weight(1)).astype(LOW)
+        values[...] = v
+        all_values[here, :] = v
+        seq = step // per_seq
+
+        @pl.when(step % per_seq == 0)
+        def _():
+            totals[seq] = jnp.zeros((HD, width), WIDE)
+
+        for g in groups(width):
+            totals[seq, :, g] += pack_state(dot_tn(k[:, g], v[:, g]), same)
+
+    @pl.when(step == steps - 1)
+    def _():
+        state_out[...] = totals[...].astype(LOW)
+        swap_state.start()
+
+    @pl.when(step >= steps)
+    def _():
+        at = step - steps
+        here = pl.ds(pl.multiple_of(at * BLOCK, BLOCK), BLOCK)
+        rows = all_normed[here, :]
+        pre = dot_nn(rows, weight(2))
+        pre_query[...] = pre.astype(LOW)
+        queries[...] = jax.nn.silu(pre).astype(LOW)
+        gate = dot_nn(rows, weight(3))
+        pre_gate[...] = gate.astype(LOW)
+
+        @pl.when(at == 0)
+        def _():
+            swap_state.wait_recv()
+
+        @pl.when(at % per_seq == 0)
+        def _():
+            carry[...] = state_in[at // per_seq].astype(WIDE) * own[-1].astype(WIDE)
+
+        marks = head_rows()
+        causal, _ = causal_masks()
+        prefix[0] = carry[...].astype(LOW)
+        for g in groups(width):
+            q, k, v = queries[:, g], all_keys[here, g], all_values[here, g]
+            scores = (dot_nt(q, split_heads(k, marks)) * causal).astype(LOW)
+            out = dot_nn(scores, split_heads(v, marks))
+            out += dot_nn(q, open_state(carry[:, g], same))
+            attended[:, g] = out.astype(LOW)
+            carry[:, g] += pack_state(dot_tn(k, v), same)
+        rows = attended[...].astype(WIDE)
+        rows = rows * rms_scale(rows) * gain_row[...] * jax.nn.sigmoid(gate)
+        rows = rows.astype(LOW)
+        mixed[...] = rows
+        residual[...] = tok[...].astype(WIDE) + dot_nn(rows, weight(4))
+
+    @pl.when(step == 2 * steps - 1)
+    def _():
+        feed_advance(4)
+        for piece in feed:
+            piece.finish()
+        three.finish()
+        for piece in [p for wave in attn for p in wave] + feed + [three]:
+            piece.drain()
+        swap_three.wait_send()
+        swap_state.wait_send()
+        keep_attn.wait()
+
+
+def tile_cuts(start, tiles):
+    cuts = []
+    for count in tiles:
+        cuts.append(slice(start, start + 128 * count))
+        start += 128 * count
+    return cuts
+
+
+def forward(tok, seq_count, shards_attn, gain_columns, s_one, s_two, s_three):
+    row_count, width = tok.shape
+    hidden = s_one.shape[1]
+    steps = row_count // BLOCK
+    per_seq = steps // seq_count
+    bits = index_bits()
+    orders = [[(s[0], s[1]) for s in reversed(order)] for order in stream_orders()]
+    third = width // 128
+    waves = [
+        list(zip(orders, tile_cuts(0, (6, 5, 5)))),
+        list(zip(orders, tile_cuts(2 * width, (5, 6, 5)))),
+        list(zip(orders, tile_cuts(4 * width, (3, 3, 3)))),
+    ]
+    feed_orders = [orders[0], orders[2]]
+    three_order = [bit for bit in orders[1] if bit != bits[-1]]
+    lead = (2,) * len(bits)
+    slab = s_one.shape[0]
+    deep = s_three.shape[0]
+    in_rows = pl.BlockSpec((BLOCK, width), lambda i: (i % steps, 0))
+    first = pl.BlockSpec((BLOCK, width), lambda i: (jnp.minimum(i, steps - 1), 0))
+    second = pl.BlockSpec((BLOCK, width), lambda i: (jnp.maximum(i - steps, 0), 0))
+    any_spec = pl.BlockSpec(memory_space=pl.ANY)
+    vmem = pl.BlockSpec(memory_space=pltpu.VMEM)
+    rows_low = jax.ShapeDtypeStruct((row_count, width), LOW)
+
+    def shape(*dims, dtype=LOW):
+        return jax.ShapeDtypeStruct(dims, dtype)
+
+    kernel = functools.partial(
+        forward_kernel, steps, per_seq, bits, waves, feed_orders, three_order
+    )
+    out = pl.pallas_call(
+        kernel,
+        grid=(2 * steps,),
+        in_specs=[in_rows] + [vmem] * 6 + [any_spec] * 2 + [vmem],
+        out_specs=[first] * 4 + [second] * 6
+        + [
+            pl.BlockSpec((1, HD, width), lambda i: (jnp.maximum(i - steps, 0), 0, 0)),
+            pl.BlockSpec((1, width), lambda i: (0, 0)),
+        ]
+        + [any_spec] * 4,
+        out_shape=[rows_low] * 9
+        + [
+            shape(row_count, width, dtype=WIDE),
+            shape(steps, HD, width),
+            shape(1, width, dtype=WIDE),
+            shape(*lead, slab, 5 * width + 128),
+            shape(*lead, slab, hidden),
+            shape(*lead, slab, hidden),
+            shape(*lead[:-1], 2 * deep, width),
+        ],
+        scratch_shapes=[
+            pltpu.VMEM(lead + (slab, 5 * width + 128), LOW),
+            pltpu.VMEM((row_count, width), LOW),
+            pltpu.VMEM((row_count, width), LOW),
+            pltpu.VMEM((row_count, width), LOW),
+            pltpu.VMEM((seq_count, HD, width), WIDE),
+            pltpu.VMEM((seq_count, HD, width), LOW),
+            pltpu.VMEM((seq_count, HD, width), LOW),
+            pltpu.VMEM((HD, width), WIDE),
+            pltpu.VMEM((deep, width), WIDE),
+            pltpu.VMEM((2 * deep, width), LOW),
+            pltpu.SemaphoreType.DMA((FORWARD_COPIES,)),
+            pltpu.SemaphoreType.DMA((FORWARD_COPIES,)),
+            pltpu.SemaphoreType.DMA((4,)),
+        ],
+        compiler_params=pltpu.CompilerParams(
+            dimension_semantics=("arbitrary",),
+            vmem_limit_bytes=58 << 20,
+            collective_id=1,
+            has_side_effects=True,
+        ),
+        cost_estimate=pl.CostEstimate(
+            flops=16 * row_count * width * width, bytes_accessed=64 << 20, transcendentals=0
+        ),
+    )(tok, *shards_attn, gain_columns, s_one, s_two, s_three.astype(WIDE))
+    return list(out[:12]) + [
+        out[12].reshape(-1, 5 * width + 128),
+        out[13].reshape(-1, hidden),
+        out[14].reshape(-1, hidden),
+        out[15].reshape(-1, width),
+    ]
+
+
+def plain_shards(
     tokens,
     lengths,
     w_query,
@@ -463,6 +818,126 @@
     )
 
 
+def fused_shards(
+    tokens,
+    lengths,
+    w_query,
+    w_key,
+    w_value,
+    w_gate,
+    out_gain,
+    w_out,
+    w_one,
+    w_two,
+    w_three,
+    cotangent,
+):
+    seq_count, local_length, width = tokens.shape
+    row_count = seq_count * local_length
+    hidden = w_one.shape[1]
+    steps = row_count // BLOCK
+    per_seq = local_length // BLOCK
+    orders = stream_orders()
+    tok = tokens.reshape(row_count, width)
+    cot = cotangent.reshape(row_count, width)
+    limits = lengths - lax.axis_index("fsdp") * local_length
+    gain_columns = jnp.broadcast_to(out_gain[:, None], (out_gain.shape[0], 128))
+    rows = rows_spec(width)
+    narrow = ((row_count, width), LOW, rows)
+    wide = ((row_count, width), WIDE, rows)
+    big = ((row_count, hidden), LOW, rows_spec(hidden))
+    state_spec = pl.BlockSpec((1, HD, width), lambda i: (i // per_seq, 0, 0))
+    state = ((seq_count, HD, width), WIDE, state_spec)
+    square = 2 * row_count * width * width
+
+    (
+        normed_low, pre_key, keys, values, pre_query, queries, pre_gate, attended, mixed,
+        residual, prefix, gain, full_attn, full_one, full_two, full_three,
+    ) = forward(
+        tok, seq_count, (w_key, w_value, w_query, w_gate, w_out), gain_columns, w_one, w_two, w_three
+    )
+
+    def part(n):
+        return pl.BlockSpec((width, width), lambda i: (0, n), pipeline_mode=pl.Buffered(1))
+
+    (
+        layer_out, normed_two, glu, grad_up_one, grad_up_two, upstream_low, grad_residual,
+        grad_residual_low, grad_pre_gate, grad_attended, grad_totals, grad_gain_term,
+    ) = call(
+        lambda *refs: feed_kernel(per_seq, *refs),
+        steps,
+        [(limits, pl.BlockSpec(memory_space=pltpu.SMEM)), (residual, rows), (cot, rows),
+         (full_one, whole_spec(full_one)), (full_two, whole_spec(full_two)),
+         (full_three, whole_spec(full_three)), (full_attn, part(4)),
+         (gain, whole_spec(gain)), (pre_gate, rows), (attended, rows), (queries, rows)],
+        [narrow, narrow, big, big, big, narrow, wide, narrow, narrow, narrow, state,
+         ((1, width), WIDE, pl.BlockSpec((1, width), lambda i: (0, 0)))],
+        flops=12 * row_count * width * hidden + square,
+    )
+    outgoing = shift_sum(grad_totals, "fsdp", True)
+    grad_one = scatter_rows(dot_tn(normed_two, grad_up_one), orders[1])
+    grad_two = scatter_rows(dot_tn(normed_two, grad_up_two), orders[2])
+    grad_three = scatter_rows(dot_tn(glu, upstream_low), orders[0])
+    gain_term = jnp.broadcast_to(grad_gain_term.reshape(width, 1), (width, 128))
+    grad_out = scatter_rows(
+        jnp.concatenate([dot_tn(mixed, grad_residual_low), gain_term], axis=1), orders[1]
+    )
+    grad_gain = grad_out[:, width]
+    grad_out = grad_out[:, :width]
+
+    def back(i):
+        return (i // per_seq) * per_seq + per_seq - 1 - i % per_seq
+
+    back_rows = rows_spec(width, order=back)
+    back_narrow = ((row_count, width), LOW, back_rows)
+    grad_pre_query, grad_pre_key, grad_pre_value = call(
+        lambda *refs: attend_back_kernel(per_seq, *refs),
+        steps,
+        [(queries, back_rows), (keys, back_rows), (values, back_rows),
+         (grad_attended, back_rows), (pre_query, back_rows), (pre_key, back_rows),
+         (prefix, pl.BlockSpec((1, HD, width), lambda i: (back(i), 0, 0))),
+         (outgoing, state_spec)],
+        [back_narrow, back_narrow, back_narrow],
+        scratch=[pltpu.VMEM((HD, width), WIDE)],
+        flops=6 * square,
+    )
+    grad_query = scatter_rows(dot_tn(normed_low, grad_pre_query), orders[0])
+    grad_key = scatter_rows(dot_tn(normed_low, grad_pre_key), orders[1])
+    grad_value = scatter_rows(dot_tn(normed_low, grad_pre_value), orders[2])
+    grad_gate = scatter_rows(dot_tn(normed_low, grad_pre_gate), orders[0])
+    (input_grad,) = call(
+        input_kernel,
+        steps,
+        [(grad_pre_query, rows), (grad_pre_key, rows), (grad_pre_value, rows),
+         (grad_pre_gate, rows), (full_attn, part(2)), (full_attn, part(0)),
+         (full_attn, part(1)), (full_attn, part(3)), (tok, rows), (grad_residual, rows)],
+        [wide],
+        flops=4 * square,
+    )
+    return (
+        layer_out.reshape(tokens.shape),
+        input_grad.reshape(tokens.shape),
+        grad_query,
+        grad_key,
+        grad_value,
+        grad_gate,
+        grad_gain,
+        grad_out,
+        grad_one,
+        grad_two,
+        grad_three,
+    )
+
+
+def shards(*arrays):
+    tokens, w_query, w_three = arrays[0], arrays[2], arrays[10]
+    sizes = (lax.axis_size("dp"), lax.axis_size("fsdp"))
+    fits = w_query.shape[0] % 16 == 0 and w_three.shape[0] % 8 == 0 and tokens.shape[1] >= 4 * BLOCK
+    if sizes == (16, 2) and fits:
+        return fused_shards(*arrays)
+    return plain_shards(*arrays)
+
+
 def solution(mesh):
     in_specs = (
         P("dp", "fsdp", None),

time: 688 us -> 619 us (0.90)
  Pallas kernels: 221 us -> 316 us
  waiting for transfers between devices: 193 us -> 109 us
  starting transfers between devices: 82.1 us -> 42.8 us
  other arithmetic: 60.1 us -> 25.9 us
    pallas_call x0 -> x1, Pallas kernels: none -> 150 us  [forward(): pl.pallas_call(kernel, grid=(2 * steps,), in_specs=[in_rows] + [vmem] * 6...]
    ppermute x40 -> x0, waiting for transfers between devices: 74 us -> none  [gather_rows(): other = lax.ppermute(data, axis, perm)]
    pallas_call x6 -> x3, Pallas kernels: 221 us -> 166 us  [call(): pl.pallas_call(kernel, grid=(steps,), in_specs=[spec for _, spec in opera...]
    ppermute x40 -> x0, starting transfers between devices: 36.8 us -> none  [gather_rows(): other = lax.ppermute(data, axis, perm)]
    another operation x78 -> x1, other arithmetic: 33.4 us -> 0.02 us  [the longest x77 33.4 us: gather_rows(): jnp.stack([jnp.where(mine, data, other), jnp.where(mine, other, data)], a...]
    another operation x10 -> x2, local copies, waits for them, and re-layouts: 15.4 us -> 0.09 us  [the longest x8 15.3 us: gather_rows(): jnp.stack([jnp.where(mine, data, other), jnp.where(mine, other, data)], a...]
    dynamic_slice x7 -> x4, local copies, waits for them, and re-layouts: 7 us -> 15.7 us  [scatter_rows(): keep = lax.dynamic_index_in_dim(data, own, place, keepdims=False)]
    ppermute x40, waiting for transfers between devices: 116 us -> 109 us  [scatter_rows(): come = lax.ppermute(send, axis, perm)]
  transfers between devices with their start and end apart: 82 -> 41, of which waited for: 39 -> 24; matrix products, arithmetic and copies ran while one was open for 22% -> 18% of each run, Pallas kernels for 17% -> 10%
where the time goes in v2:
time: 619 us; the launch traced here: 614 us
  Pallas kernels  316 us (51%)
  waiting for transfers between devices  109 us (18%)
  matrix products  85 us (14%)
  starting transfers between devices  42.8 us (7%)
  local copies, waits for them, and re-layouts  33.3 us (5%)
  other arithmetic  25.9 us (4%)
    pallas_call x3, Pallas kernels, call(): pl.pallas_call(kernel, grid=(steps,), in_specs=[spec for _, spec in opera...  166 us
    pallas_call x1, Pallas kernels, forward(): pl.pallas_call(kernel, grid=(2 * steps,), in_specs=[in_rows] + [vmem] * 6...  150 us
    ppermute x40, waiting for transfers between devices, scatter_rows(): come = lax.ppermute(send, axis, perm)  109 us
    dot_general x8, matrix products, dot_tn(): lax.dot_general(a, b, (((0,), (0,)), ((), ())), preferred_element_type=WIDE)  85 us
    ppermute x40, starting transfers between devices, scatter_rows(): come = lax.ppermute(send, axis, perm)  41.5 us
    convert_element_type x32, other arithmetic, scatter_rows(): data = data.astype(jnp.bfloat16)  16 us
    dynamic_slice x4, local copies, waits for them, and re-layouts, scatter_rows(): keep = lax.dynamic_index_in_dim(data, own, place, keepdims=False)  15.7 us
  transfers between devices with their start and end apart: 41, of which 24 were waited for; matrix products, arithmetic and copies ran while one was open for 18% of the time, Pallas kernels for 10%

profile of v2, /device:TPU:0, one launch (start us, length us, event | category | flops | bytes accessed | tf_op | source)
XLA Modules:
  0.0 613.7 jit_solution(17991380095921872832)
XLA Ops:
  0.7 1.7 convert_element_type.488.s_three
  4.8 149.7 %shard_map.203 = (bf16[2048,1024]{1,0:T(8,128)(2,1)}, bf16[2048,1024]{1,0:T(8,128)(2,1)}, bf16[2048,1024]{1,0:T(8,128)(2,1)}, bf16[2048,1024]{1,0:T(8,128)(2,1)}...) custom-call(bf16[2048,1024]{1,0:T(8,128)(2,1)} %bitcast.266, ...), custom_call_target="tpu_custom_call" | custom-call | flops 34359738368 | bytes 67108864 | tf_op jit(solution)/shard_map/pallas_call | solution.py:630
  154.6 102.0 %shard_map.204 = (bf16[2048,1024]{1,0:T(8,128)(2,1)}, bf16[2048,1024]{1,0:T(8,128)(2,1)}, bf16[2048,2816]{1,0:T(8,128)(2,1)}, bf16[2048,2816]{1,0:T(8,128)(2,1)}...) custom-call(s32[2]{0:T(128)} %broadcast_subtract_fusion.refs_0_, ...), custom_call_target="tpu_custom_call" | custom-call | flops 75161927680 | bytes 53219336 | tf_op jit(solution)/shard_map/pallas_call | solution.py:316
  256.6 18.1 %convolution_convert_fusion = bf16[2816,1024]{1,0:T(8,128)(2,1)} fusion(bf16[2048,2816]{1,0:T(8,128)(2,1)} %get-tuple-element.71, bf16[2048,1024]{1,0:T(8,128)(2,1)} %get-tuple-element.72), kind=kOutput, calls=%fused_computation.6 | convolution fusion | flops 11814043648 | bytes 21495808 | tf_op jit(solution)/shard_map/dot_general | solution.py:109
  274.7 5.4 constant_dynamic-slice_fusion.1
  280.1 2.0 copy.94
  282.6 18.5 %convolution_convert_fusion.2 = bf16[1024,2816]{1,0:T(8,128)(2,1)} fusion(bf16[2048,1024]{1,0:T(8,128)(2,1)S(1)} %copy-done.17, bf16[2048,2816]{1,0:T(8,128)(2,1)} %get-tuple-element.69), kind=kOutput, calls=%fused_computation.8 | convolution fusion | flops 11814043648 | bytes 21495808 | tf_op jit(solution)/shard_map/dot_general | solution.py:109
  301.1 14.2 %convolution_convert_fusion.1 = bf16[1024,2816]{1,0:T(8,128)(2,1)} fusion(bf16[2048,1024]{1,0:T(8,128)(2,1)S(1)} %copy-done.17, bf16[2048,2816]{1,0:T(8,128)(2,1)S(1)} %bitcast.281), kind=kOutput, calls=%fused_computation.7 | convolution fusion | flops 11814043648 | bytes 21495808 | tf_op jit(solution)/shard_map/dot_general | solution.py:109
  315.3 8.0 %constant_dynamic-slice_fusion.3 = (bf16[2,2,2,1,2,32,2816]{6,5,4,3,2,1,0:T(8,128)(2,1)}, bf16[2,2,2,1,2,32,2816]{6,5,4,3,2,1,0:T(8,128)(2,1)}, bf16[2,2,2,1,2,3...) fusion(bf16[2,2,2,2,2,32,2816]{6,5,4,3,2,1,0:T(8,128)(2,1)} %bitcast.265, s32[]{:T(128)S(6)} %select_n.125, ...), kind=kLoop, calls=%fused_computation.137 | loop fusion | bytes 23068680 | tf_op jit(solution)/shard_map/jit(dynamic_index_in_dim)/dynamic_slice | solution.py:82
  323.3 3.7 copy.95
  327.4 8.2 %convolution_convert_fusion.3 = bf16[1024,1024]{1,0:T(8,128)(2,1)S(1)} fusion(bf16[2048,1024]{1,0:T(8,128)(2,1)} %get-tuple-element.65, bf16[2048,1024]{1,0:T(8,128)(2,1)} %get-tuple-element.66), kind=kOutput, calls=%fused_computation.35 | convolution fusion | flops 4296015872 | bytes 10485760 | tf_op jit(solution)/shard_map/dot_general | solution.py:109
  339.6 5.7 convolution_convert_fusion.4
  345.4 3.6 copy.96
  349.8 37.5 %shard_map.205 = (bf16[2048,1024]{1,0:T(8,128)(2,1)}, bf16[2048,1024]{1,0:T(8,128)(2,1)}, bf16[2048,1024]{1,0:T(8,128)(2,1)}) custom-call(bf16[2048,1024]{1,0:T(8,128)(2,1)} %get-tuple-element.50.refs_10_.refs_0_, bf16[2048,1024]{1,0:T(8,128)(2,1)} %get-tuple-element.52.refs_1_, bf16[2048,1024]{1,0:T(8,128)(2,1)} %get-tuple-element.53.refs_2_, ...), custom_call_target="tpu_custom_call" | custom-call | flops 25769803776 | bytes 26738688 | tf_op jit(solution)/shard_map/pallas_call | solution.py:316
  387.3 7.1 %convolution_convert_fusion.5 = bf16[1024,1024]{1,0:T(8,128)(2,1)S(1)} fusion(bf16[2048,1024]{1,0:T(8,128)(2,1)S(1)} %copy-done.16, bf16[2048,1024]{1,0:T(8,128)(2,1)} %get-tuple-element.61.grad_value), kind=kOutput, calls=%fused_computation.37 | convolution fusion | flops 4296015872 | bytes 10485760 | tf_op jit(solution)/shard_map/dot_general | solution.py:109
  398.7 5.8 convolution_convert_fusion.7
  404.5 26.9 %shard_map.206 = f32[2048,1024]{1,0:T(8,128)} custom-call(bf16[2048,1024]{1,0:T(8,128)(2,1)} %get-tuple-element.59.grad_query, bf16[2048,1024]{1,0:T(8,128)(2,1)} %get-tuple-element.60.grad_key, bf16[2048,1024]{1,0:T(8,128)(2,1)} %get-tuple-element.61.grad_value, bf16[2048,1024]{1,0:T(8,128)(2,1)} %get-tuple-element.62.grad_gate, ...), custom_call_target="tpu_custom_call" | custom-call | flops 17179869184 | bytes 72351744 | tf_op jit(solution)/shard_map/pallas_call | solution.py:316
  431.4 7.3 %convolution_convert_fusion.6 = bf16[1024,1024]{1,0:T(8,128)(2,1)S(1)} fusion(bf16[2048,1024]{1,0:T(8,128)(2,1)} %get-tuple-element.64, bf16[2048,1024]{1,0:T(8,128)(2,1)S(1)} %copy-done.5), kind=kOutput, calls=%fused_computation.38 | convolution fusion | flops 4296015872 | bytes 10485760 | tf_op jit(solution)/shard_map/dot_general | solution.py:109
  445.8 1.6 fusion.8
  447.4 2.4 collective-permute-start.17
  452.4 8.2 %collective-permute-done.22 = bf16[2,2,2,32,1152]{4,3,0,2,1:T(8,128)(2,1)S(1)} collective-permute-done((bf16[2,2,2,32,1152]{4,3,0,2,1:T(8,128)(2,1)S(1)}, bf16[2,2,2,32,1152]{4,3,0,2,1:T(8,128)(2,1)S(1)}, u32[]{:S(2)}, u32[]{:S(2)}) %collective-permute-start.22) | collective-permute-done | bytes 589856 | tf_op jit(solution)/shard_map/ppermute | solution.py:83
  462.1 2.0 collective-permute-start.2
  464.3 9.2 %collective-permute-done.7 = bf16[2,2,2,32,1024]{4,3,0,2,1:T(8,128)(2,1)S(1)} collective-permute-done((bf16[2,2,2,32,1024]{4,3,0,2,1:T(8,128)(2,1)S(1)}, bf16[2,2,2,32,1024]{4,3,0,2,1:T(8,128)(2,1)S(1)}, u32[]{:S(2)}, u32[]{:S(2)}) %collective-permute-start.7) | collective-permute-done | bytes 524320 | tf_op jit(solution)/shard_map/ppermute | solution.py:83
  473.8 1.9 collective-permute-done.2
  478.3 5.1 collective-permute-done.23
  483.4 3.2 collective-permute-start.13
  487.3 5.2 collective-permute-done.13
  494.6 5.1 collective-permute-done.3
  500.1 1.8 collective-permute-start.14
  502.0 2.7 collective-permute-done.19
  506.9 2.7 collective-permute-done.9
  513.3 3.1 collective-permute-done.25
  525.0 2.3 collective-permute-done.5
  528.0 3.2 fusion
  531.3 1.8 collective-permute-start.37
  533.1 2.6 fusion.1
  535.8 1.9 collective-permute-start.32
  538.7 20.9 %collective-permute-done.37 = bf16[2,2,2,88,1024]{4,3,0,1,2:T(8,128)(2,1)S(1)} collective-permute-done((bf16[2,2,2,88,1024]{4,3,0,1,2:T(8,128)(2,1)S(1)}, bf16[2,2,2,88,1024]{4,3,0,1,2:T(8,128)(2,1)S(1)}, u32[]{:S(2)}, u32[]{:S(2)}) %collective-permute-start.37) | collective-permute-done | bytes 1441824 | tf_op jit(solution)/shard_map/ppermute | solution.py:83
  560.4 1.9 collective-permute-start.38
  562.2 4.1 collective-permute-done.32
  567.4 5.5 collective-permute-done.27
  573.9 8.2 %collective-permute-done.38 = bf16[2,2,88,1024]{3,2,0,1:T(8,128)(2,1)S(1)} collective-permute-done((bf16[2,2,88,1024]{3,2,0,1:T(8,128)(2,1)S(1)}, bf16[2,2,88,1024]{3,2,0,1:T(8,128)(2,1)S(1)}, u32[]{:S(2)}, u32[]{:S(2)}) %collective-permute-start.38) | collective-permute-done | bytes 720928 | tf_op jit(solution)/shard_map/ppermute | solution.py:83
  582.4 3.1 collective-permute-start.39
  585.8 1.8 collective-permute-start.34
  588.7 2.0 collective-permute-start.29
  590.7 6.1 collective-permute-done.39
  597.3 2.8 collective-permute-start.35
  600.5 10.1 %collective-permute-done.35 = bf16[32,2816]{1,0:T(8,128)(2,1)S(1)} collective-permute-done((bf16[32,2816]{1,0:T(8,128)(2,1)S(1)}, bf16[32,2816]{1,0:T(8,128)(2,1)S(1)}, u32[]{:S(2)}, u32[]{:S(2)}) %collective-permute-start.35) | collective-permute-done | bytes 180256 | tf_op jit(solution)/shard_map/ppermute | solution.py:83
  (184 shorter events, 54.1 us)
Async XLA Ops:
  280.1 21.0 %slice-start = ((s8[11534336]{0:T(1024)(128)(4,1)}), s8[4194304]{0:T(1024)(128)(4,1)S(1)}, s32[]{:S(2)}) async-start(s8[11534336]{0:T(1024)(128)(4,1)} %bitcast.280), calls=%async_computation | async-start | bytes 8388608
  282.1 245.9 %collective-permute-start.36 = (bf16[2,2,2,2,88,1024]{5,4,0,1,2,3:T(8,128)(2,1)}, bf16[2,2,2,2,88,1024]{5,4,0,1,2,3:T(8,128)(2,1)}, u32[]{:S(2)}, u32[]{:S(2)}) collective-permute-start(bf16[2,2,2,2,88,1024]{5,4,0,1,2,3:T(8,128)(2,1)} %bitcast.248), channel_id=1, source_target_pairs={{0,2},{2,0},{4,6},{6,4},{8,10},{10,8},{12,14},{14,12},{16,18},{18,... | collective-permute-start | bytes 8650760 | tf_op jit(solution)/shard_map/ppermute | solution.py:83
  282.6 18.5 %slice-start.1 = ((s8[11534336]{0:T(1024)(128)(4,1)}), s8[4194304]{0:T(1024)(128)(4,1)S(1)}, s32[]{:S(2)}) async-start(s8[11534336]{0:T(1024)(128)(4,1)} %bitcast.280), calls=%async_computation.1 | async-start | bytes 8388608
  282.6 18.5 %slice-start.2 = ((s8[11534336]{0:T(1024)(128)(4,1)}), s8[3145728]{0:T(1024)(128)(4,1)S(1)}, s32[]{:S(2)}) async-start(s8[11534336]{0:T(1024)(128)(4,1)} %bitcast.280), calls=%async_computation.2 | async-start | bytes 6291456
  327.0 206.1 %collective-permute-start.31 = (bf16[2,2,2,2,32,2816]{5,4,0,2,3,1:T(8,128)(2,1)}, bf16[2,2,2,2,32,2816]{5,4,0,2,3,1:T(8,128)(2,1)}, u32[]{:S(2)}, u32[]{:S(2)}) collective-permute-start(bf16[2,2,2,2,32,2816]{5,4,0,2,3,1:T(8,128)(2,1)} %bitcast.249), channel_id=1, source_target_pairs={{0,2},{2,0},{4,6},{6,4},{8,10},{10,8},{12,14},{14,12},{16,18},{18,... | collective-permute-start | bytes 8650760 | tf_op jit(solution)/shard_map/ppermute | solution.py:83
  338.1 101.7 %collective-permute-start.21 = (bf16[2,2,2,2,32,1152]{5,4,0,3,1,2:T(8,128)(2,1)}, bf16[2,2,2,2,32,1152]{5,4,0,3,1,2:T(8,128)(2,1)}, u32[]{:S(2)}, u32[]{:S(2)}) collective-permute-start(bf16[2,2,2,2,32,1152]{5,4,0,3,1,2:T(8,128)(2,1)} %fusion.15), channel_id=1, source_target_pairs={{0,2},{2,0},{4,6},{6,4},{8,10},{10,8},{12,14},{14,12},{16,18},{18,... | collective-permute-start | bytes 3538952 | tf_op jit(solution)/shard_map/ppermute | solution.py:83
  338.3 10.6 %collective-permute-start = (bf16[2,64,1024]{2,1,0:T(8,128)(2,1)S(1)}, bf16[2,64,1024]{2,1,0:T(8,128)(2,1)S(1)}, u32[]{:S(2)}, u32[]{:S(2)}) collective-permute-start(bf16[2,64,1024]{2,1,0:T(8,128)(2,1)S(1)} %convert_element_type.489), channel_id=1, source_target_pairs={{1,0},{3,2},{5,4},{7,6},{9,8},{11,10},{13,12},{15,14},{17,16},{19,... | collective-permute-start | bytes 786440 | tf_op jit(solution)/shard_map/ppermute | solution.py:96
  349.8 37.5 %copy-start.16 = (bf16[2048,1024]{1,0:T(8,128)(2,1)S(1)}, bf16[2048,1024]{1,0:T(8,128)(2,1)}, u32[]{:S(2)}) copy-start(bf16[2048,1024]{1,0:T(8,128)(2,1)} %get-tuple-element.64) | copy-start | bytes 12582916
  397.1 45.8 %collective-permute-start.16 = (bf16[2,2,2,2,32,1024]{5,4,0,1,2,3:T(8,128)(2,1)}, bf16[2,2,2,2,32,1024]{5,4,0,1,2,3:T(8,128)(2,1)}, u32[]{:S(2)}, u32[]{:S(2)}) collective-permute-start(bf16[2,2,2,2,32,1024]{5,4,0,1,2,3:T(8,128)(2,1)} %bitcast.251), channel_id=1, source_target_pairs={{0,2},{2,0},{4,6},{6,4},{8,10},{10,8},{12,14},{14,12},{16,18},{18,... | collective-permute-start | bytes 3145736 | tf_op jit(solution)/shard_map/ppermute | solution.py:83
  398.5 46.7 %collective-permute-start.11 = (bf16[2,2,2,2,32,1024]{5,4,0,2,3,1:T(8,128)(2,1)}, bf16[2,2,2,2,32,1024]{5,4,0,2,3,1:T(8,128)(2,1)}, u32[]{:S(2)}, u32[]{:S(2)}) collective-permute-start(bf16[2,2,2,2,32,1024]{5,4,0,2,3,1:T(8,128)(2,1)} %bitcast.252), channel_id=1, source_target_pairs={{0,2},{2,0},{4,6},{6,4},{8,10},{10,8},{12,14},{14,12},{16,18},{18,... | collective-permute-start | bytes 3145736 | tf_op jit(solution)/shard_map/ppermute | solution.py:83
  404.5 26.9 %copy-start.5 = (bf16[2048,1024]{1,0:T(8,128)(2,1)S(1)}, bf16[2048,1024]{1,0:T(8,128)(2,1)}, u32[]{:S(2)}) copy-start(bf16[2048,1024]{1,0:T(8,128)(2,1)} %get-tuple-element.60.grad_key) | copy-start | bytes 12582916
  439.8 7.6 %collective-permute-start.6 = (bf16[2,2,2,2,32,1024]{5,4,0,3,1,2:T(8,128)(2,1)S(1)}, bf16[2,2,2,2,32,1024]{5,4,0,3,1,2:T(8,128)(2,1)S(1)}, u32[]{:S(2)}, u32[]{:S(2)}) collective-permute-start(bf16[2,2,2,2,32,1024]{5,4,0,3,1,2:T(8,128)(2,1)S(1)} %bitcast.274), channel_id=1, source_target_pairs={{0,2},{2,0},{4,6},{6,4},{8,10},{10,8},{12,14},{14,12},{16,18},{18,... | collective-permute-start | bytes 3145736 | tf_op jit(solution)/shard_map/ppermute | solution.py:83
  442.9 7.4 %collective-permute-start.1 = (bf16[2,2,2,2,32,1024]{5,4,0,1,2,3:T(8,128)(2,1)S(1)}, bf16[2,2,2,2,32,1024]{5,4,0,1,2,3:T(8,128)(2,1)S(1)}, u32[]{:S(2)}, u32[]{:S(2)}) collective-permute-start(bf16[2,2,2,2,32,1024]{5,4,0,1,2,3:T(8,128)(2,1)S(1)} %bitcast.273), channel_id=1, source_target_pairs={{0,2},{2,0},{4,6},{6,4},{8,10},{10,8},{12,14},{14,12},{16,18},{18,... | collective-permute-start | bytes 3145736 | tf_op jit(solution)/shard_map/ppermute | solution.py:83
  445.2 15.3 %collective-permute-start.22 = (bf16[2,2,2,32,1152]{4,3,0,2,1:T(8,128)(2,1)S(1)}, bf16[2,2,2,32,1152]{4,3,0,2,1:T(8,128)(2,1)S(1)}, u32[]{:S(2)}, u32[]{:S(2)}) collective-permute-start(bf16[2,2,2,32,1152]{4,3,0,2,1:T(8,128)(2,1)S(1)} %dynamic-slice_bitcast_fusion.6), channel_id=1, source_target_pairs={{0,4},{2,6},{4,0},{6,2},{8,12},{10,14},{12,8},{14,10},{16,20},{18,... | collective-permute-start | bytes 1769480 | tf_op jit(solution)/shard_map/ppermute | solution.py:83
  447.4 14.7 %collective-permute-start.17 = (bf16[2,2,2,32,1024]{4,3,0,1,2:T(8,128)(2,1)S(1)}, bf16[2,2,2,32,1024]{4,3,0,1,2:T(8,128)(2,1)S(1)}, u32[]{:S(2)}, u32[]{:S(2)}) collective-permute-start(bf16[2,2,2,32,1024]{4,3,0,1,2:T(8,128)(2,1)S(1)} %dynamic-slice_bitcast_fusion.7), channel_id=1, source_target_pairs={{0,1},{1,0},{2,3},{3,2},{4,5},{5,4},{6,7},{7,6},{8,9},{9,8},{10,11... | collective-permute-start | bytes 1572872 | tf_op jit(solution)/shard_map/ppermute | solution.py:83
  450.3 27.1 %collective-permute-start.12 = (bf16[2,2,2,32,1024]{4,3,0,1,2:T(8,128)(2,1)S(1)}, bf16[2,2,2,32,1024]{4,3,0,1,2:T(8,128)(2,1)S(1)}, u32[]{:S(2)}, u32[]{:S(2)}) collective-permute-start(bf16[2,2,2,32,1024]{4,3,0,1,2:T(8,128)(2,1)S(1)} %dynamic-slice_bitcast_fusion.8), channel_id=1, source_target_pairs={{0,8},{2,10},{4,12},{6,14},{8,0},{10,2},{12,4},{14,6},{16,24},{18,... | collective-permute-start | bytes 1572872 | tf_op jit(solution)/shard_map/ppermute | solution.py:83
  452.3 21.2 %copy-start.8 = (bf16[2,2,2,1,2,32,2816]{6,5,0,4,1,2,3:T(8,128)(2,1)S(1)}, bf16[2,2,2,1,2,32,2816]{6,5,0,4,1,2,3:T(8,128)(2,1)}, u32[]{:S(2)}) copy-start(bf16[2,2,2,1,2,32,2816]{6,5,0,4,1,2,3:T(8,128)(2,1)} %copy.96) | copy-start | bytes 8650756
  460.6 13.0 %collective-permute-start.7 = (bf16[2,2,2,32,1024]{4,3,0,2,1:T(8,128)(2,1)S(1)}, bf16[2,2,2,32,1024]{4,3,0,2,1:T(8,128)(2,1)S(1)}, u32[]{:S(2)}, u32[]{:S(2)}) collective-permute-start(bf16[2,2,2,32,1024]{4,3,0,2,1:T(8,128)(2,1)S(1)} %dynamic-slice_bitcast_fusion.9), channel_id=1, source_target_pairs={{0,4},{2,6},{4,0},{6,2},{8,12},{10,14},{12,8},{14,10},{16,20},{18,... | collective-permute-start | bytes 1572872 | tf_op jit(solution)/shard_map/ppermute | solution.py:83
  462.1 13.5 %collective-permute-start.2 = (bf16[2,2,2,32,1024]{4,3,0,1,2:T(8,128)(2,1)S(1)}, bf16[2,2,2,32,1024]{4,3,0,1,2:T(8,128)(2,1)S(1)}, u32[]{:S(2)}, u32[]{:S(2)}) collective-permute-start(bf16[2,2,2,32,1024]{4,3,0,1,2:T(8,128)(2,1)S(1)} %dynamic-slice_bitcast_fusion.10), channel_id=1, source_target_pairs={{0,1},{1,0},{2,3},{3,2},{4,5},{5,4},{6,7},{7,6},{8,9},{9,8},{10,11... | collective-permute-start | bytes 1572872 | tf_op jit(solution)/shard_map/ppermute | solution.py:83
  473.6 64.1 %collective-permute-start.26 = (bf16[2,2,2,2,32,2816]{5,4,0,3,1,2:T(8,128)(2,1)S(1)}, bf16[2,2,2,2,32,2816]{5,4,0,3,1,2:T(8,128)(2,1)S(1)}, u32[]{:S(2)}, u32[]{:S(2)}) collective-permute-start(bf16[2,2,2,2,32,2816]{5,4,0,3,1,2:T(8,128)(2,1)S(1)} %bitcast.268), channel_id=1, source_target_pairs={{0,2},{2,0},{4,6},{6,4},{8,10},{10,8},{12,14},{14,12},{16,18},{18,... | collective-permute-start | bytes 8650760 | tf_op jit(solution)/shard_map/ppermute | solution.py:83
  475.7 7.7 %collective-permute-start.23 = (bf16[2,2,32,1152]{3,2,0,1:T(8,128)(2,1)S(1)}, bf16[2,2,32,1152]{3,2,0,1:T(8,128)(2,1)S(1)}, u32[]{:S(2)}, u32[]{:S(2)}) collective-permute-start(bf16[2,2,32,1152]{3,2,0,1:T(8,128)(2,1)S(1)} %dynamic-slice_bitcast_fusion.14), channel_id=1, source_target_pairs={{0,8},{2,10},{4,12},{6,14},{8,0},{10,2},{12,4},{14,6},{16,24},{18,... | collective-permute-start | bytes 884744 | tf_op jit(solution)/shard_map/ppermute | solution.py:83
  477.4 9.3 %collective-permute-start.18 = (bf16[2,2,32,1024]{3,2,0,1:T(8,128)(2,1)S(1)}, bf16[2,2,32,1024]{3,2,0,1:T(8,128)(2,1)S(1)}, u32[]{:S(2)}, u32[]{:S(2)}) collective-permute-start(bf16[2,2,32,1024]{3,2,0,1:T(8,128)(2,1)S(1)} %dynamic-slice_bitcast_fusion.15), channel_id=1, source_target_pairs={{0,4},{2,6},{4,0},{6,2},{8,12},{10,14},{12,8},{14,10},{16,20},{18,... | collective-permute-start | bytes 786440 | tf_op jit(solution)/shard_map/ppermute | solution.py:83
  483.4 9.2 %collective-permute-start.13 = (bf16[2,2,32,1024]{3,2,0,1:T(8,128)(2,1)S(1)}, bf16[2,2,32,1024]{3,2,0,1:T(8,128)(2,1)S(1)}, u32[]{:S(2)}, u32[]{:S(2)}) collective-permute-start(bf16[2,2,32,1024]{3,2,0,1:T(8,128)(2,1)S(1)} %dynamic-slice_bitcast_fusion.16), channel_id=1, source_target_pairs={{0,1},{1,0},{2,3},{3,2},{4,5},{5,4},{6,7},{7,6},{8,9},{9,8},{10,11... | collective-permute-start | bytes 786440 | tf_op jit(solution)/shard_map/ppermute | solution.py:83
  486.7 7.5 %collective-permute-start.8 = (bf16[2,2,32,1024]{3,2,0,1:T(8,128)(2,1)S(1)}, bf16[2,2,32,1024]{3,2,0,1:T(8,128)(2,1)S(1)}, u32[]{:S(2)}, u32[]{:S(2)}) collective-permute-start(bf16[2,2,32,1024]{3,2,0,1:T(8,128)(2,1)S(1)} %dynamic-slice_bitcast_fusion.17), channel_id=1, source_target_pairs={{0,8},{2,10},{4,12},{6,14},{8,0},{10,2},{12,4},{14,6},{16,24},{18,... | collective-permute-start | bytes 786440 | tf_op jit(solution)/shard_map/ppermute | solution.py:83
  492.5 7.1 %collective-permute-start.3 = (bf16[2,2,32,1024]{3,2,0,1:T(8,128)(2,1)S(1)}, bf16[2,2,32,1024]{3,2,0,1:T(8,128)(2,1)S(1)}, u32[]{:S(2)}, u32[]{:S(2)}) collective-permute-start(bf16[2,2,32,1024]{3,2,0,1:T(8,128)(2,1)S(1)} %dynamic-slice_bitcast_fusion.18), channel_id=1, source_target_pairs={{0,4},{2,6},{4,0},{6,2},{8,12},{10,14},{12,8},{14,10},{16,20},{18,... | collective-permute-start | bytes 786440 | tf_op jit(solution)/shard_map/ppermute | solution.py:83
  494.2 5.9 collective-permute-start.24
  494.6 33.4 %copy-start = (bf16[2,2,2,1,2,88,1024]{6,5,4,3,2,1,0:T(8,128)(2,1)S(1)}, bf16[2,2,2,1,2,88,1024]{6,5,4,3,2,1,0:T(8,128)(2,1)}, u32[]{:S(2)}) copy-start(bf16[2,2,2,1,2,88,1024]{6,5,4,3,2,1,0:T(8,128)(2,1)} %get-tuple-element.73) | copy-start | bytes 8650756
  499.6 5.0 collective-permute-start.19
  500.1 6.1 collective-permute-start.14
  504.6 5.0 collective-permute-start.9
  506.2 6.1 collective-permute-start.4
  509.6 6.8 %collective-permute-start.25 = (bf16[32,1152]{1,0:T(8,128)(2,1)S(1)}, bf16[32,1152]{1,0:T(8,128)(2,1)S(1)}, u32[]{:S(2)}, u32[]{:S(2)}) collective-permute-start(bf16[32,1152]{1,0:T(8,128)(2,1)S(1)} %dynamic-slice_bitcast_fusion.27), channel_id=1, source_target_pairs={{0,16},{2,18},{4,20},{6,22},{8,24},{10,26},{12,28},{14,30},{16,0},... | collective-permute-start | bytes 221192 | tf_op jit(solution)/shard_map/ppermute | solution.py:83
  512.3 6.8 %collective-permute-start.20 = (bf16[32,1024]{1,0:T(8,128)(2,1)S(1)}, bf16[32,1024]{1,0:T(8,128)(2,1)S(1)}, u32[]{:S(2)}, u32[]{:S(2)}) collective-permute-start(bf16[32,1024]{1,0:T(8,128)(2,1)S(1)} %dynamic-slice_bitcast_fusion.28), channel_id=1, source_target_pairs={{0,16},{2,18},{4,20},{6,22},{8,24},{10,26},{12,28},{14,30},{16,0},... | collective-permute-start | bytes 196616 | tf_op jit(solution)/shard_map/ppermute | solution.py:83
  516.4 5.7 collective-permute-start.15
  519.1 5.2 collective-permute-start.10
  522.1 5.2 collective-permute-start.5
  531.3 28.3 %collective-permute-start.37 = (bf16[2,2,2,88,1024]{4,3,0,1,2:T(8,128)(2,1)S(1)}, bf16[2,2,2,88,1024]{4,3,0,1,2:T(8,128)(2,1)S(1)}, u32[]{:S(2)}, u32[]{:S(2)}) collective-permute-start(bf16[2,2,2,88,1024]{4,3,0,1,2:T(8,128)(2,1)S(1)} %dynamic-slice_bitcast_fusion), channel_id=1, source_target_pairs={{0,1},{1,0},{2,3},{3,2},{4,5},{5,4},{6,7},{7,6},{8,9},{9,8},{10,11... | collective-permute-start | bytes 4325384 | tf_op jit(solution)/shard_map/ppermute | solution.py:83
  535.8 30.5 %collective-permute-start.32 = (bf16[2,2,2,32,2816]{4,3,0,1,2:T(8,128)(2,1)S(1)}, bf16[2,2,2,32,2816]{4,3,0,1,2:T(8,128)(2,1)S(1)}, u32[]{:S(2)}, u32[]{:S(2)}) collective-permute-start(bf16[2,2,2,32,2816]{4,3,0,1,2:T(8,128)(2,1)S(1)} %dynamic-slice_bitcast_fusion.1), channel_id=1, source_target_pairs={{0,8},{2,10},{4,12},{6,14},{8,0},{10,2},{12,4},{14,6},{16,24},{18,... | collective-permute-start | bytes 4325384 | tf_op jit(solution)/shard_map/ppermute | solution.py:83
  538.6 34.2 %collective-permute-start.27 = (bf16[2,2,2,32,2816]{4,3,0,2,1:T(8,128)(2,1)S(1)}, bf16[2,2,2,32,2816]{4,3,0,2,1:T(8,128)(2,1)S(1)}, u32[]{:S(2)}, u32[]{:S(2)}) collective-permute-start(bf16[2,2,2,32,2816]{4,3,0,2,1:T(8,128)(2,1)S(1)} %dynamic-slice_bitcast_fusion.2), channel_id=1, source_target_pairs={{0,4},{2,6},{4,0},{6,2},{8,12},{10,14},{12,8},{14,10},{16,20},{18,... | collective-permute-start | bytes 4325384 | tf_op jit(solution)/shard_map/ppermute | solution.py:83
  560.4 21.8 %collective-permute-start.38 = (bf16[2,2,88,1024]{3,2,0,1:T(8,128)(2,1)S(1)}, bf16[2,2,88,1024]{3,2,0,1:T(8,128)(2,1)S(1)}, u32[]{:S(2)}, u32[]{:S(2)}) collective-permute-start(bf16[2,2,88,1024]{3,2,0,1:T(8,128)(2,1)S(1)} %dynamic-slice_bitcast_fusion.3), channel_id=1, source_target_pairs={{0,4},{2,6},{4,0},{6,2},{8,12},{10,14},{12,8},{14,10},{16,20},{18,... | collective-permute-start | bytes 2162696 | tf_op jit(solution)/shard_map/ppermute | solution.py:83
  566.7 18.8 %collective-permute-start.33 = (bf16[2,2,32,2816]{3,2,0,1:T(8,128)(2,1)S(1)}, bf16[2,2,32,2816]{3,2,0,1:T(8,128)(2,1)S(1)}, u32[]{:S(2)}, u32[]{:S(2)}) collective-permute-start(bf16[2,2,32,2816]{3,2,0,1:T(8,128)(2,1)S(1)} %dynamic-slice_bitcast_fusion.4), channel_id=1, source_target_pairs={{0,1},{1,0},{2,3},{3,2},{4,5},{5,4},{6,7},{7,6},{8,9},{9,8},{10,11... | collective-permute-start | bytes 2162696 | tf_op jit(solution)/shard_map/ppermute | solution.py:83
  573.3 15.2 %collective-permute-start.28 = (bf16[2,2,32,2816]{3,2,0,1:T(8,128)(2,1)S(1)}, bf16[2,2,32,2816]{3,2,0,1:T(8,128)(2,1)S(1)}, u32[]{:S(2)}, u32[]{:S(2)}) collective-permute-start(bf16[2,2,32,2816]{3,2,0,1:T(8,128)(2,1)S(1)} %dynamic-slice_bitcast_fusion.5), channel_id=1, source_target_pairs={{0,8},{2,10},{4,12},{6,14},{8,0},{10,2},{12,4},{14,6},{16,24},{18,... | collective-permute-start | bytes 2162696 | tf_op jit(solution)/shard_map/ppermute | solution.py:83
  582.4 14.4 %collective-permute-start.39 = (bf16[2,88,1024]{2,1,0:T(8,128)(2,1)S(1)}, bf16[2,88,1024]{2,1,0:T(8,128)(2,1)S(1)}, u32[]{:S(2)}, u32[]{:S(2)}) collective-permute-start(bf16[2,88,1024]{2,1,0:T(8,128)(2,1)S(1)} %dynamic-slice_bitcast_fusion.11), channel_id=1, source_target_pairs={{0,8},{2,10},{4,12},{6,14},{8,0},{10,2},{12,4},{14,6},{16,24},{18,... | collective-permute-start | bytes 1081352 | tf_op jit(solution)/shard_map/ppermute | solution.py:83
  585.8 11.4 %collective-permute-start.34 = (bf16[2,32,2816]{2,1,0:T(8,128)(2,1)S(1)}, bf16[2,32,2816]{2,1,0:T(8,128)(2,1)S(1)}, u32[]{:S(2)}, u32[]{:S(2)}) collective-permute-start(bf16[2,32,2816]{2,1,0:T(8,128)(2,1)S(1)} %dynamic-slice_bitcast_fusion.12), channel_id=1, source_target_pairs={{0,4},{2,6},{4,0},{6,2},{8,12},{10,14},{12,8},{14,10},{16,20},{18,... | collective-permute-start | bytes 1081352 | tf_op jit(solution)/shard_map/ppermute | solution.py:83
  588.7 11.4 %collective-permute-start.29 = (bf16[2,32,2816]{2,1,0:T(8,128)(2,1)S(1)}, bf16[2,32,2816]{2,1,0:T(8,128)(2,1)S(1)}, u32[]{:S(2)}, u32[]{:S(2)}) collective-permute-start(bf16[2,32,2816]{2,1,0:T(8,128)(2,1)S(1)} %dynamic-slice_bitcast_fusion.13), channel_id=1, source_target_pairs={{0,1},{1,0},{2,3},{3,2},{4,5},{5,4},{6,7},{7,6},{8,9},{9,8},{10,11... | collective-permute-start | bytes 1081352 | tf_op jit(solution)/shard_map/ppermute | solution.py:83
  596.9 14.4 %collective-permute-start.40 = (bf16[88,1024]{1,0:T(8,128)(2,1)S(1)}, bf16[88,1024]{1,0:T(8,128)(2,1)S(1)}, u32[]{:S(2)}, u32[]{:S(2)}) collective-permute-start(bf16[88,1024]{1,0:T(8,128)(2,1)S(1)} %dynamic-slice_bitcast_fusion.19), channel_id=1, source_target_pairs={{0,16},{2,18},{4,20},{6,22},{8,24},{10,26},{12,28},{14,30},{16,0},... | collective-permute-start | bytes 540680 | tf_op jit(solution)/shard_map/ppermute | solution.py:83
  597.3 13.2 %collective-permute-start.35 = (bf16[32,2816]{1,0:T(8,128)(2,1)S(1)}, bf16[32,2816]{1,0:T(8,128)(2,1)S(1)}, u32[]{:S(2)}, u32[]{:S(2)}) collective-permute-start(bf16[32,2816]{1,0:T(8,128)(2,1)S(1)} %dynamic-slice_bitcast_fusion.20), channel_id=1, source_target_pairs={{0,16},{2,18},{4,20},{6,22},{8,24},{10,26},{12,28},{14,30},{16,0},... | collective-permute-start | bytes 540680 | tf_op jit(solution)/shard_map/ppermute | solution.py:83
  600.2 12.3 %collective-permute-start.30 = (bf16[32,2816]{1,0:T(8,128)(2,1)S(1)}, bf16[32,2816]{1,0:T(8,128)(2,1)S(1)}, u32[]{:S(2)}, u32[]{:S(2)}) collective-permute-start(bf16[32,2816]{1,0:T(8,128)(2,1)S(1)} %dynamic-slice_bitcast_fusion.21), channel_id=1, source_target_pairs={{0,16},{2,18},{4,20},{6,22},{8,24},{10,26},{12,28},{14,30},{16,0},... | collective-permute-start | bytes 540680 | tf_op jit(solution)/shard_map/ppermute | solution.py:83
  (14 other events, 67.3 us)

commit v3 on v2

--- a/solution.py
+++ b/solution.py
@@ -210,10 +210,10 @@
 
 
 def feed_kernel(
-    per_seq, limits, residual, cotangent, w_one, w_two, w_three, w_out, gain, pre_gate,
+    per_seq, turned, limits, residual, cotangent, w_one, w_two, w_three, w_out, gain, pre_gate,
     attended, queries,
     layer_out, normed, glu, grad_one, grad_two, upstream_low, grad_residual, grad_low,
-    grad_gate, grad_attended, totals, grad_gain,
+    grad_gate, grad_attended, totals, grad_gain, held=None,
 ):
     step = pl.program_id(0)
     row_count = residual.shape[0]
@@ -222,7 +222,7 @@
     res = residual[...]
     scale = rms_scale(res)
     rows = (res * scale).astype(LOW)
-    normed[...] = rows
+    normed[...] = rows.T if turned else rows
     upstream = cotangent[...].astype(WIDE) * valid
     up_low = upstream.astype(LOW)
     upstream_low[...] = up_low
@@ -230,10 +230,15 @@
         one = dot_nn(rows, w_one[:, c])
         two = dot_nn(rows, w_two[:, c])
         back = dot_nt(up_low, w_three[c, :])
-        glu[:, c] = (one * two).astype(LOW)
+        product = (one * two).astype(LOW)
+        if turned:
+            held[:, c] = product
+            glu[c, :] = product.T
+        else:
+            glu[:, c] = product
         grad_one[:, c] = (back * two).astype(LOW)
         grad_two[:, c] = (back * one).astype(LOW)
-    layer_out[...] = (valid * (res + dot_nn(glu[...], w_three[...]))).astype(LOW)
+    layer_out[...] = (valid * (res + dot_nn(held[...] if turned else glu[...], w_three[...]))).astype(LOW)
     back = dot_nt(grad_one[...], w_one[...]) + dot_nt(grad_two[...], w_two[...])
     grad = upstream + norm_back(res, scale, back)
     grad_residual[...] = grad
@@ -414,6 +419,548 @@
         for copies in self.stages:
             for copy in copies:
                 copy.wait_send()
+
+
+class Scatter:
+    def __init__(self, sems, core, bits, order, acc, send, come, recvs, columns, slots):
+        self.bits, self.order, self.acc, self.columns = bits, order, acc, columns
+        self.come, self.recvs, self.slots = come, recvs, slots
+        tail = (slice(None),)
+        full = (slice(None),) * len(bits) + tail + (slots,)
+        self.core = sems.copy(send.at[full], come.at[full], core)
+        self.copies = []
+        for k, bit in enumerate(order):
+            done = order[:k]
+            index = tuple(
+                1 - bit_value(b) if b == bit else bit_value(b) if b in done else slice(None)
+                for b in bits
+            )
+            free = (slice(None),) * (len(bits) - k - 1)
+            self.copies.append(
+                sems.copy(
+                    acc.at[index + tail + (columns,)],
+                    recvs[k].at[free + tail + (columns,)],
+                    bit,
+                )
+            )
+
+    def add(self, done, source, columns):
+        free = [b for b in self.bits if b not in done]
+
+        def one(k, _):
+            at = [lax.rem(lax.div(k, 1 << (len(free) - 1 - n)), 2) for n in range(len(free))]
+            mine = tuple(bit_value(b) if b in done else at[free.index(b)] for b in self.bits)
+            here = mine + (slice(None), self.columns)
+            there = tuple(at) + (slice(None), columns)
+            total = self.acc[here].astype(WIDE) + source[there].astype(WIDE)
+            self.acc[here] = total.astype(LOW)
+            return 0
+
+        lax.fori_loop(0, 1 << len(free), one, 0)
+
+    def launch(self):
+        self.core.start()
+
+    def advance(self, k):
+        if k == 0:
+            self.core.wait_recv()
+            self.add([], self.come, self.slots)
+        else:
+            self.copies[k - 1].wait_recv()
+            self.add(self.order[:k], self.recvs[k - 1], self.columns)
+        self.copies[k].start()
+
+    def result(self):
+        self.copies[-1].wait_recv()
+        own = tuple(bit_value(b) for b in self.bits)
+        here = (slice(None), self.columns)
+        return self.acc[own + here].astype(WIDE) + self.recvs[-1][here].astype(WIDE)
+
+    def drain(self, core=True):
+        if core:
+            self.core.wait_send()
+        for copy in self.copies:
+            copy.wait_send()
+
+
+def run_events(step, events):
+    for at in sorted(events):
+
+        @pl.when(step == at)
+        def _():
+            for action in events[at]:
+                action()
+
+
+def half_rows(ref, core):
+    rows = ref[:, core]
+    return rows.reshape(rows.shape[0] * rows.shape[1], rows.shape[2])
+
+
+def attend_back_step(
+    same, queries, keys, values, grad_attended, pre_query, pre_key, prefix,
+    grad_query, grad_key, grad_value, carry,
+):
+    marks = head_rows()
+    causal, causal_t = causal_masks()
+    for g in groups(queries.shape[1]):
+        q, k, v, ga = queries[:, g], keys[:, g], values[:, g], grad_attended[:, g]
+        qs, ks, vs, gs = (split_heads(rows, marks) for rows in (q, k, v, ga))
+        state = open_state(prefix[0, :, g].astype(WIDE), same)
+        grad_state = open_state(carry[:, g], same)
+        grad_scores = (dot_nt(ga, vs) * causal).astype(LOW)
+        gq = dot_nn(grad_scores, ks) + dot_nt(ga, state)
+        grad_scores = (dot_nt(v, gs) * causal_t).astype(LOW)
+        gk = dot_nn(grad_scores, qs) + dot_nt(v, grad_state)
+        scores = (dot_nt(k, qs) * causal_t).astype(LOW)
+        gv = dot_nn(scores, gs) + dot_nn(k, grad_state)
+        grad_query[:, g] = (gq * silu_slope(pre_query[:, g].astype(WIDE))).astype(LOW)
+        grad_key[:, g] = (gk * silu_slope(pre_key[:, g].astype(WIDE))).astype(LOW)
+        grad_value[:, g] = gv.astype(LOW)
+        carry[:, g] += pack_state(dot_tn(q, ga), same)
+
+
+CHUNK = 256
+
+
+def feed_back_kernel(
+    plan, per_seq, bits, orders,
+    normed, grad_one, grad_two, glu, upstream,
+    queries, keys, values, grad_attended, pre_query, pre_key, prefix, totals,
+    out_one, out_two, out_three, grad_query, grad_key, grad_value,
+    acc, come1, come2, come3, come4, send, come,
+    acc3, come31, come32, come33, send3, come3c, last_send, last_come,
+    state_out, state_in, carry, send_sems, recv_sems,
+):
+    step = pl.program_id(0)
+    parts, base = plan
+    core, links = bits[-2], bits[:-2] + bits[-1:]
+    mine = bit_value(core)
+    other = 1 - mine
+    sems = Sems(send_sems, recv_sems)
+    hidden = out_one.shape[1]
+    wide_a = parts[0][1] * CHUNK
+    wide_b = hidden - wide_a
+    recvs = (come1, come2, come3, come4)
+    pieces = []
+    for slot, (begin, span, order) in enumerate(
+        ((0, wide_a, orders[0]), (hidden, wide_a, orders[2]),
+         (wide_a, wide_b, orders[0]), (hidden + wide_a, wide_b, orders[2]))
+    ):
+        pieces.append(
+            Scatter(
+                sems, core, links, order, acc, send.at[slot % 2], come.at[slot], recvs,
+                slice(begin, begin + span), slice(0, span),
+            )
+        )
+    one_a, two_a, one_b, two_b = pieces
+    half = upstream.shape[1] // 2
+    threes = [
+        Scatter(
+            sems, core, links[:-1], [b for b in orders[1] if b != bits[-1]], acc3, send3, come3c,
+            (come31, come32, come33), slice(n * half, (n + 1) * half),
+            slice(n * half, (n + 1) * half),
+        )
+        for n in range(2)
+    ]
+    cuts = [slice(n * half, (n + 1) * half) for n in range(2)]
+    swaps = [sems.copy(last_send.at[:, c], last_come.at[:, c], bits[-1]) for c in cuts]
+    swap_state = sems.copy(state_out, state_in, bits[-1])
+    side = bit_value(bits[-1])
+
+    def swap_three(n):
+        total = threes[n].result()
+        deep = total.shape[0] // 2
+        low, high = total[:deep], total[deep:]
+        upper = side.astype(WIDE)
+        out_three[:, cuts[n]] = low * (1 - upper) + high * upper
+        last_send[:, cuts[n]] = low * upper + high * (1 - upper)
+        swaps[n].start()
+
+    def end_three(n):
+        swaps[n].wait_recv()
+        out_three[:, cuts[n]] += last_come[:, cuts[n]]
+
+    def end(piece, out, begin):
+        span = piece.columns.stop - piece.columns.start
+        out[:, begin : begin + span] = piece.result()
+
+    ends = [begin + count for begin, count in parts]
+
+    @pl.when(step == 0)
+    def _():
+        greet(bits)
+        state_out[...] = totals[...].astype(LOW)
+        swap_state.start()
+
+    run_events(step, {
+        parts[3][0]: [one_a.core.wait_send],
+        parts[4][0]: [two_a.core.wait_send],
+        ends[0] + 4: [functools.partial(one_a.advance, 0)],
+        ends[1] + 5: [functools.partial(two_a.advance, 0)],
+        ends[2] + 3: [functools.partial(threes[0].advance, 0)],
+        ends[3] + 4: [functools.partial(one_b.advance, 0)],
+        ends[4] + 5: [functools.partial(two_b.advance, 0)],
+        base - 2: [functools.partial(one_a.advance, 1)],
+        base: [functools.partial(two_a.advance, 1)],
+        base + 1: [functools.partial(threes[1].advance, 0),
+                   functools.partial(threes[0].advance, 1),
+                   functools.partial(one_a.advance, 2)],
+        base + 2: [functools.partial(one_a.advance, 3),
+                   functools.partial(two_a.advance, 2)],
+        base + 3: [functools.partial(one_b.advance, 1),
+                   functools.partial(two_b.advance, 1),
+                   functools.partial(threes[0].advance, 2)],
+        base + 4: [functools.partial(two_a.advance, 3),
+                   functools.partial(swap_three, 0)],
+        base + 5: [functools.partial(threes[1].advance, 1),
+                   functools.partial(one_b.advance, 2),
+                   functools.partial(two_b.advance, 2)],
+        base + 6: [functools.partial(one_b.advance, 3),
+                   functools.partial(two_b.advance, 3),
+                   functools.partial(threes[1].advance, 2)],
+        base + 7: [functools.partial(swap_three, 1),
+                   functools.partial(end, one_a, out_one, 0),
+                   functools.partial(end, two_a, out_two, 0),
+                   functools.partial(end_three, 0)],
+    })
+
+    def weight_chunk(rhs, chunk, piece_base, slot, span_base):
+        rows = rhs[...]
+        lead = acc.shape[:-1]
+        at = pl.ds(pl.multiple_of(chunk * CHUNK, CHUNK), CHUNK)
+        give = dot_nn(half_rows(normed, other), rows).astype(LOW).reshape(lead + (CHUNK,))
+        send[(slot,) + (slice(None),) * len(lead) + (at,)] = give
+        keep = dot_nn(half_rows(normed, mine), rows).astype(LOW).reshape(lead + (CHUNK,))
+        at = pl.ds(pl.multiple_of(span_base + chunk * CHUNK, CHUNK), CHUNK)
+        acc[(slice(None),) * len(lead) + (at,)] = keep
+
+    def chunk_phase(part, rhs, slot, span_base):
+        begin, count = parts[part]
+
+        @pl.when((step >= begin) & (step < begin + count))
+        def _():
+            weight_chunk(rhs, step - begin, None, slot, span_base)
+
+    chunk_phase(0, grad_one, 0, 0)
+    chunk_phase(1, grad_two, 1, hidden)
+    chunk_phase(3, grad_one, 0, wide_a)
+    chunk_phase(4, grad_two, 1, hidden + wide_a)
+
+    for n in range(2):
+        begin, count = parts[2 + 3 * n]
+
+        @pl.when((step >= begin) & (step < begin + count))
+        def _():
+            k = step - begin
+            at = tuple(lax.rem(lax.div(k, 1 << (2 - d)), 2) for d in range(3))
+            deep = glu.shape[0] // 2
+            rows = upstream[:, cuts[n]]
+
+            def part(c):
+                left = glu[pl.ds(pl.multiple_of(c * deep, 16), deep), :]
+                return dot_nn(left, rows).astype(LOW)
+
+            send3[at + (slice(None), cuts[n])] = part(other)
+            acc3[at + (slice(None), cuts[n])] = part(mine)
+
+    run_events(step, {
+        ends[0] - 1: [one_a.launch],
+        ends[1] - 1: [two_a.launch],
+        ends[2] - 1: [threes[0].launch],
+        ends[3] - 1: [one_b.launch],
+        ends[4] - 1: [two_b.launch],
+        ends[5] - 1: [threes[1].launch, swap_state.wait_recv],
+    })
+
+    @pl.when(step >= base)
+    def _():
+        at = step - base
+
+        @pl.when(at % per_seq == 0)
+        def _():
+            carry[...] = state_in[at // per_seq].astype(WIDE) * (1 - side).astype(WIDE)
+
+        attend_back_step(
+            head_square(), queries, keys, values, grad_attended, pre_query, pre_key, prefix,
+            grad_query, grad_key, grad_value, carry,
+        )
+
+    @pl.when(step == pl.num_programs(0) - 1)
+    def _():
+        end(one_b, out_one, wide_a)
+        end(two_b, out_two, wide_a)
+        end_three(1)
+        one_a.drain(core=False)
+        two_a.drain(core=False)
+        for piece in [one_b, two_b] + threes:
+            piece.drain()
+        for copy in swaps:
+            copy.wait_send()
+        swap_state.wait_send()
+
+
+def clip(value, low, high):
+    return jnp.minimum(jnp.maximum(value, low), high)
+
+
+def feed_back(
+    seq_count, normed, grad_one, grad_two, glu, upstream, queries, keys, values, grad_attended,
+    pre_query, pre_key, prefix, totals,
+):
+    row_count, width = queries.shape
+    hidden = grad_one.shape[1]
+    steps = row_count // BLOCK
+    per_seq = steps // seq_count
+    bits = index_bits()
+    orders = [[(s[0], s[1]) for s in order[1:]] for order in stream_orders()]
+    chunks = hidden // CHUNK
+    more, less = chunks - chunks // 2, chunks // 2
+    lead3 = 8
+    counts = (more, more, lead3, less, less, lead3)
+    parts = []
+    for count in counts:
+        parts.append((sum(c for _, c in parts), count))
+    base = sum(counts)
+    deep = hidden // lead3
+    slab = width // 32
+    p = parts
+
+    def one_at(i):
+        return clip(i - p[0][0], 0, more - 1) + clip(i - p[3][0] + 1, 0, less)
+
+    def two_at(i):
+        return clip(i - p[1][0], 0, more - 1) + clip(i - p[4][0] + 1, 0, less)
+
+    def glu_at(i):
+        return jnp.where(
+            i < p[3][0], clip(i - p[2][0], 0, lead3 - 1), clip(i - p[5][0], 0, lead3 - 1)
+        )
+
+    def back(i):
+        at = clip(i - base, 0, steps - 1)
+        return (at // per_seq) * per_seq + per_seq - 1 - at % per_seq
+
+    rows = pl.BlockSpec((BLOCK, width), lambda i: (back(i), 0))
+    vmem = pl.BlockSpec(memory_space=pltpu.VMEM)
+    rows_low = jax.ShapeDtypeStruct((row_count, width), LOW)
+    wide = (more * CHUNK)
+    low = functools.partial(pltpu.VMEM, dtype=LOW)
+    kernel = functools.partial(feed_back_kernel, (parts, base), per_seq, bits, orders)
+    return pl.pallas_call(
+        kernel,
+        grid=(base + steps,),
+        in_specs=[
+            vmem,
+            pl.BlockSpec((row_count, CHUNK), lambda i: (0, one_at(i))),
+            pl.BlockSpec((row_count, CHUNK), lambda i: (0, two_at(i))),
+            pl.BlockSpec((deep, row_count), lambda i: (glu_at(i), 0)),
+            vmem,
+        ]
+        + [rows] * 6
+        + [pl.BlockSpec((1, HD, width), lambda i: (back(i), 0, 0)), vmem],
+        out_specs=[vmem] * 3 + [rows] * 3,
+        out_shape=[
+            jax.ShapeDtypeStruct((slab, hidden), WIDE),
+            jax.ShapeDtypeStruct((slab, hidden), WIDE),
+            jax.ShapeDtypeStruct((hidden // 32, width), WIDE),
+        ]
+        + [rows_low] * 3,
+        scratch_shapes=[
+            low((2, 2, 2, 2, slab, 2 * hidden)),
+            low((2, 2, 2, slab, 2 * hidden)),
+            low((2, 2, slab, 2 * hidden)),
+            low((2, slab, 2 * hidden)),
+            low((slab, 2 * hidden)),
+            low((2, 2, 2, 2, 2, slab, wide)),
+            low((4, 2, 2, 2, 2, slab, wide)),
+            low((2, 2, 2, deep // 2, width)),
+            low((2, 2, deep // 2, width)),
+            low((2, deep // 2, width)),
+            low((deep // 2, width)),
+            low((2, 2, 2, deep // 2, width)),
+            low((2, 2, 2, deep // 2, width)),
+            pltpu.VMEM((hidden // 32, width), WIDE),
+            pltpu.VMEM((hidden // 32, width), WIDE),
+            low((seq_count, HD, width)),
+            low((seq_count, HD, width)),
+            pltpu.VMEM((HD, width), WIDE),
+            pltpu.SemaphoreType.DMA((31,)),
+            pltpu.SemaphoreType.DMA((31,)),
+        ],
+        compiler_params=pltpu.CompilerParams(
+            dimension_semantics=("arbitrary",),
+            vmem_limit_bytes=62 << 20,
+            collective_id=2,
+            has_side_effects=True,
+        ),
+        cost_estimate=pl.CostEstimate(
+            flops=6 * row_count * width * hidden + 12 * row_count * width * width,
+            bytes_accessed=128 << 20,
+            transcendentals=0,
+        ),
+    )(
+        normed.reshape(8, 2, width // 16, row_count), grad_one, grad_two, glu, upstream,
+        queries, keys, values, grad_attended, pre_query, pre_key, prefix, totals,
+    )
+
+
+def attend_weights_kernel(
+    bits, orders,
+    normed, mixed, grad_low, grad_query, grad_key, grad_value, grad_gate, gain_term,
+    rows_query, rows_key, rows_value, rows_gate, w_key, w_value, w_query, w_gate, tok,
+    grad_residual,
+    out, input_grad,
+    acc, come1, come2, come3, come4, send, come, send_sems, recv_sems,
+):
+    step = pl.program_id(0)
+    core, links = bits[-2], bits[:-2] + bits[-1:]
+    mine = bit_value(core)
+    other = 1 - mine
+    sems = Sems(send_sems, recv_sems)
+    width = tok.shape[1]
+    per = width // CHUNK
+    chunks = 5 * per
+    lead = acc.shape[:-1]
+    fill = (slice(None),) * len(lead)
+    pieces, first = [], 0
+    sizes = (3, 3, 3, 3, 3, 3, 2)
+    for n, size in enumerate(sizes):
+        begin = first * CHUNK + (128 if first >= per else 0)
+        first += size
+        stop = first * CHUNK + (128 if first >= per else 0)
+        pieces.append(
+            Scatter(
+                sems, core, links, orders[n % 3], acc, send, come, (come1, come2, come3, come4),
+                slice(begin, stop), slice(begin, stop),
+            )
+        )
+
+    def end(n):
+        piece = pieces[n]
+        out[:, piece.columns] = piece.result()
+
+    @pl.when(step == 0)
+    def _():
+        greet(bits)
+
+    table = {
+        5: [(0, 0)], 8: [(1, 0)], 11: [(2, 0)], 14: [(3, 0), (0, 1)], 17: [(4, 0), (1, 1)],
+        20: [(5, 0), (2, 1), (0, 2)], 21: [(6, 0), (3, 1), (1, 2), (0, 3)],
+        22: [(4, 1), (2, 2), (1, 3)], 23: [(5, 1), (6, 1), (3, 2), (2, 3)],
+        24: [(4, 2), (3, 3)], 25: [(5, 2), (6, 2), (4, 3)], 26: [(5, 3), (6, 3)],
+    }
+    run_events(step, {
+        at: [functools.partial(pieces[n].advance, k) for n, k in todo]
+        for at, todo in table.items()
+    })
+
+    def chunk_phase(n, lhs, rhs):
+        @pl.when((step >= n * per) & (step < (n + 1) * per))
+        def _():
+            shift = 128 if n else 0
+            at = pl.ds(pl.multiple_of(step * CHUNK + shift, 128), CHUNK)
+            rows = rhs[...]
+            give = dot_nn(half_rows(lhs, other), rows).astype(LOW)
+            send[fill + (at,)] = give.reshape(lead + (CHUNK,))
+            keep = dot_nn(half_rows(lhs, mine), rows).astype(LOW)
+            acc[fill + (at,)] = keep.reshape(lead + (CHUNK,))
+
+    chunk_phase(0, mixed, grad_low)
+    chunk_phase(1, normed, grad_query)
+    chunk_phase(2, normed, grad_key)
+    chunk_phase(3, normed, grad_value)
+    chunk_phase(4, normed, grad_gate)
+
+    @pl.when(step == 0)
+    def _():
+        column = jnp.broadcast_to(gain_term[...], (128, width)).T
+        column = column.reshape(8, 2, width // 16, 128)
+        upper = mine.astype(WIDE)
+        low, high = column[:, 0], column[:, 1]
+        at = fill + (slice(width, width + 128),)
+        acc[at] = (low * (1 - upper) + high * upper).astype(LOW).reshape(lead + (128,))
+        send[at] = (low * upper + high * (1 - upper)).astype(LOW).reshape(lead + (128,))
+
+    launches, first = {}, 0
+    for n, size in enumerate(sizes):
+        first += size
+        launches[first - 1] = [pieces[n].launch]
+    run_events(step, launches)
+
+    @pl.when(step >= chunks)
+    def _():
+        grad = dot_nt(rows_query[...], w_query[...]) + dot_nt(rows_key[...], w_key[...])
+        grad += dot_nt(rows_value[...], w_value[...]) + dot_nt(rows_gate[...], w_gate[...])
+        x = tok[...].astype(WIDE)
+        input_grad[...] = grad_residual[...] + norm_back(x, rms_scale(x), grad)
+
+    @pl.when(step == pl.num_programs(0) - 1)
+    def _():
+        for n in range(len(pieces)):
+            end(n)
+        for piece in pieces:
+            piece.drain()
+
+
+def attend_weights(
+    normed, mixed, grad_low, grad_query, grad_key, grad_value, grad_gate, gain_term, full_attn,
+    tok, grad_residual,
+):
+    row_count, width = tok.shape
+    steps = row_count // BLOCK
+    bits = index_bits()
+    orders = [[(s[0], s[1]) for s in order[1:]] for order in stream_orders()]
+    per = width // CHUNK
+    chunks = 5 * per
+    slab = width // 32
+    vmem = pl.BlockSpec(memory_space=pltpu.VMEM)
+    rows = pl.BlockSpec((BLOCK, width), lambda i: (clip(i - chunks, 0, steps - 1), 0))
+
+    def chunk(n):
+        return pl.BlockSpec((row_count, CHUNK), lambda i: (0, clip(i - n * per, 0, per - 1)))
+
+    def part(n):
+        return pl.BlockSpec((width, width), lambda i: (0, n), pipeline_mode=pl.Buffered(1))
+
+    low = functools.partial(pltpu.VMEM, dtype=LOW)
+    columns = 5 * width + 128
+    split = (8, 2, width // 16, row_count)
+    return pl.pallas_call(
+        functools.partial(attend_weights_kernel, bits, orders),
+        grid=(chunks + steps,),
+        in_specs=[vmem, vmem] + [chunk(n) for n in range(5)] + [vmem] + [rows] * 4
+        + [part(n) for n in range(4)] + [rows, rows],
+        out_specs=[vmem, rows],
+        out_shape=[
+            jax.ShapeDtypeStruct((slab, columns), WIDE),
+            jax.ShapeDtypeStruct((row_count, width), WIDE),
+        ],
+        scratch_shapes=[
+            low((2, 2, 2, 2, slab, columns)),
+            low((2, 2, 2, slab, columns)),
+            low((2, 2, slab, columns)),
+            low((2, slab, columns)),
+            low((slab, columns)),
+            low((2, 2, 2, 2, slab, columns)),
+            low((2, 2, 2, 2, slab, columns)),
+            pltpu.SemaphoreType.DMA((35,)),
+            pltpu.SemaphoreType.DMA((35,)),
+        ],
+        compiler_params=pltpu.CompilerParams(
+            dimension_semantics=("arbitrary",),
+            vmem_limit_bytes=62 << 20,
+            collective_id=3,
+            has_side_effects=True,
+        ),
+        cost_estimate=pl.CostEstimate(
+            flops=18 * row_count * width * width, bytes_accessed=64 << 20, transcendentals=0
+        ),
+    )(
+        normed.reshape(split), mixed.reshape(split), grad_low, grad_query, grad_key, grad_value,
+        grad_gate, gain_term, grad_query, grad_key, grad_value, grad_gate,
+        full_attn, full_attn, full_attn, full_attn, tok, grad_residual,
+    )
 
 
 FORWARD_COPIES = 80
@@ -515,7 +1062,7 @@
     def _():
         x = tok[...].astype(WIDE)
         rows = (x * rms_scale(x)).astype(LOW)
-        normed[...] = rows
+        normed[...] = rows.T
         here = pl.ds(pl.multiple_of(step * BLOCK, BLOCK), BLOCK)
         all_normed[here, :] = rows
         pre = dot_nn(rows, weight(0))
@@ -572,7 +1119,7 @@
         rows = attended[...].astype(WIDE)
         rows = rows * rms_scale(rows) * gain_row[...] * jax.nn.sigmoid(gate)
         rows = rows.astype(LOW)
-        mixed[...] = rows
+        mixed[...] = rows.T
         residual[...] = tok[...].astype(WIDE) + dot_nn(rows, weight(4))
 
     @pl.when(step == 2 * steps - 1)
@@ -617,6 +1164,9 @@
     in_rows = pl.BlockSpec((BLOCK, width), lambda i: (i % steps, 0))
     first = pl.BlockSpec((BLOCK, width), lambda i: (jnp.minimum(i, steps - 1), 0))
     second = pl.BlockSpec((BLOCK, width), lambda i: (jnp.maximum(i - steps, 0), 0))
+    first_turned = pl.BlockSpec((width, BLOCK), lambda i: (0, jnp.minimum(i, steps - 1)))
+    second_turned = pl.BlockSpec((width, BLOCK), lambda i: (0, jnp.maximum(i - steps, 0)))
+    turned_low = jax.ShapeDtypeStruct((width, row_count), LOW)
     any_spec = pl.BlockSpec(memory_space=pl.ANY)
     vmem = pl.BlockSpec(memory_space=pltpu.VMEM)
     rows_low = jax.ShapeDtypeStruct((row_count, width), LOW)
@@ -631,13 +1181,13 @@
         kernel,
         grid=(2 * steps,),
         in_specs=[in_rows] + [vmem] * 6 + [any_spec] * 2 + [vmem],
-        out_specs=[first] * 4 + [second] * 6
+        out_specs=[first_turned] + [first] * 3 + [second] * 4 + [second_turned, second]
         + [
             pl.BlockSpec((1, HD, width), lambda i: (jnp.maximum(i - steps, 0), 0, 0)),
             pl.BlockSpec((1, width), lambda i: (0, 0)),
         ]
         + [any_spec] * 4,
-        out_shape=[rows_low] * 9
+        out_shape=[turned_low] + [rows_low] * 7 + [turned_low]
         + [
             shape(row_count, width, dtype=WIDE),
             shape(steps, HD, width),
@@ -752,7 +1302,7 @@
         layer_out, normed_two, glu, grad_up_one, grad_up_two, upstream_low, grad_residual,
         grad_residual_low, grad_pre_gate, grad_attended, grad_totals, grad_gain_term,
     ) = call(
-        lambda *refs: feed_kernel(per_seq, *refs),
+        lambda *refs: feed_kernel(per_seq, False, *refs),
         steps,
         [(limits, pl.BlockSpec(memory_space=pltpu.SMEM)), (residual, rows), (cot, rows),
          (full_one, whole_spec(full_one)), (full_two, whole_spec(full_two)),
@@ -845,6 +1395,11 @@
     rows = rows_spec(width)
     narrow = ((row_count, width), LOW, rows)
     wide = ((row_count, width), WIDE, rows)
+
+    def turned_rows(size):
+        return pl.BlockSpec((size, BLOCK), lambda i: (0, i))
+
+    turned = ((width, row_count), LOW, turned_rows(width))
     big = ((row_count, hidden), LOW, rows_spec(hidden))
     state_spec = pl.BlockSpec((1, HD, width), lambda i: (i // per_seq, 0, 0))
     state = ((seq_count, HD, width), WIDE, state_spec)
@@ -864,55 +1419,28 @@
         layer_out, normed_two, glu, grad_up_one, grad_up_two, upstream_low, grad_residual,
         grad_residual_low, grad_pre_gate, grad_attended, grad_totals, grad_gain_term,
     ) = call(
-        lambda *refs: feed_kernel(per_seq, *refs),
+        lambda *refs: feed_kernel(per_seq, True, *refs),
         steps,
         [(limits, pl.BlockSpec(memory_space=pltpu.SMEM)), (residual, rows), (cot, rows),
          (full_one, whole_spec(full_one)), (full_two, whole_spec(full_two)),
          (full_three, whole_spec(full_three)), (full_attn, part(4)),
          (gain, whole_spec(gain)), (pre_gate, rows), (attended, rows), (queries, rows)],
-        [narrow, narrow, big, big, big, narrow, wide, narrow, narrow, narrow, state,
+        [narrow, turned, ((hidden, row_count), LOW, turned_rows(hidden)), big, big, narrow, wide, narrow, narrow, narrow, state,
          ((1, width), WIDE, pl.BlockSpec((1, width), lambda i: (0, 0)))],
+        scratch=[pltpu.VMEM((BLOCK, hidden), LOW)],
         flops=12 * row_count * width * hidden + square,
     )
-    outgoing = shift_sum(grad_totals, "fsdp", True)
-    grad_one = scatter_rows(dot_tn(normed_two, grad_up_one), orders[1])
-    grad_two = scatter_rows(dot_tn(normed_two, grad_up_two), orders[2])
-    grad_three = scatter_rows(dot_tn(glu, upstream_low), orders[0])
-    gain_term = jnp.broadcast_to(grad_gain_term.reshape(width, 1), (width, 128))
-    grad_out = scatter_rows(
-        jnp.concatenate([dot_tn(mixed, grad_residual_low), gain_term], axis=1), orders[1]
-    )
-    grad_gain = grad_out[:, width]
-    grad_out = grad_out[:, :width]
-
-    def back(i):
-        return (i // per_seq) * per_seq + per_seq - 1 - i % per_seq
-
-    back_rows = rows_spec(width, order=back)
-    back_narrow = ((row_count, width), LOW, back_rows)
-    grad_pre_query, grad_pre_key, grad_pre_value = call(
-        lambda *refs: attend_back_kernel(per_seq, *refs),
-        steps,
-        [(queries, back_rows), (keys, back_rows), (values, back_rows),
-         (grad_attended, back_rows), (pre_query, back_rows), (pre_key, back_rows),
-         (prefix, pl.BlockSpec((1, HD, width), lambda i: (back(i), 0, 0))),
-         (outgoing, state_spec)],
-        [back_narrow, back_narrow, back_narrow],
-        scratch=[pltpu.VMEM((HD, width), WIDE)],
-        flops=6 * square,
-    )
-    grad_query = scatter_rows(dot_tn(normed_low, grad_pre_query), orders[0])
-    grad_key = scatter_rows(dot_tn(normed_low, grad_pre_key), orders[1])
-    grad_value = scatter_rows(dot_tn(normed_low, grad_pre_value), orders[2])
-    grad_gate = scatter_rows(dot_tn(normed_low, grad_pre_gate), orders[0])
-    (input_grad,) = call(
-        input_kernel,
-        steps,
-        [(grad_pre_query, rows), (grad_pre_key, rows), (grad_pre_value, rows),
-         (grad_pre_gate, rows), (full_attn, part(2)), (full_attn, part(0)),
-         (full_attn, part(1)), (full_attn, part(3)), (tok, rows), (grad_residual, rows)],
-        [wide],
-        flops=4 * square,
+    grad_one, grad_two, grad_three, grad_pre_query, grad_pre_key, grad_pre_value = feed_back(
+        seq_count, normed_two, grad_up_one, grad_up_two, glu, upstream_low, queries, keys, values,
+        grad_attended, pre_query, pre_key, prefix, grad_totals,
+    )
+    grads, input_grad = attend_weights(
+        normed_low, mixed, grad_residual_low, grad_pre_query, grad_pre_key, grad_pre_value,
+        grad_pre_gate, grad_gain_term, full_attn, tok, grad_residual,
+    )
+    grad_out, grad_gain = grads[:, :width], grads[:, width]
+    grad_query, grad_key, grad_value, grad_gate = (
+        grads[:, 128 + n * width : 128 + (n + 1) * width] for n in range(1, 5)
     )
     return (
         layer_out.reshape(tokens.shape),

time: 619 us -> 507 us (0.82)
  Pallas kernels: 316 us -> 487 us
  waiting for transfers between devices: 109 us -> 0 us
  matrix products: 85 us -> 0 us
  starting transfers between devices: 42.8 us -> 0 us
  other arithmetic: 25.9 us -> 2.86 us
  local copies, waits for them, and re-layouts: 33.3 us -> 15.4 us
    pallas_call x0 -> x2, Pallas kernels: none -> 236 us  [the longest x1 146 us: feed_back(): pl.pallas_call(kernel, grid=(base + steps,), in_specs=[vmem, pl.BlockSpec...]
    ppermute x41 -> x0, waiting for transfers between devices: 109 us -> none  [the longest x40 109 us: scatter_rows(): come = lax.ppermute(send, axis, perm)]
    dot_general x8 -> x0, matrix products: 85 us -> none  [dot_tn(): lax.dot_general(a, b, (((0,), (0,)), ((), ())), preferred_element_type=WIDE)]
    pallas_call x3 -> x1, Pallas kernels: 166 us -> 102 us  [call(): pl.pallas_call(kernel, grid=(steps,), in_specs=[spec for _, spec in opera...]
    ppermute x41 -> x0, starting transfers between devices: 42.8 us -> none  [the longest x40 41.5 us: scatter_rows(): come = lax.ppermute(send, axis, perm)]
    dynamic_slice x11 -> x0, local copies, waits for them, and re-layouts: 27.3 us -> none  [the longest x4 15.7 us: scatter_rows(): keep = lax.dynamic_index_in_dim(data, own, place, keepdims=False)]
    convert_element_type x34 -> x0, other arithmetic: 16.9 us -> none  [the longest x32 16 us: scatter_rows(): data = data.astype(jnp.bfloat16)]
    unnamed x42 -> x10, local copies, waits for them, and re-layouts: 1.91 us -> 10.7 us
  transfers between devices with their start and end apart: 41 -> 0, of which waited for: 24 -> 0; matrix products, arithmetic and copies ran while one was open for 18% -> 0% of each run, Pallas kernels for 10% -> 0%
where the time goes in v3:
time: 507 us; the launch traced here: 506 us
  Pallas kernels  487 us (96%)
  local copies, waits for them, and re-layouts  15.4 us (3%)
    pallas_call x1, Pallas kernels, forward(): pl.pallas_call(kernel, grid=(2 * steps,), in_specs=[in_rows] + [vmem] * 6...  150 us
    pallas_call x1, Pallas kernels, feed_back(): pl.pallas_call(kernel, grid=(base + steps,), in_specs=[vmem, pl.BlockSpec...  146 us
    pallas_call x1, Pallas kernels, call(): pl.pallas_call(kernel, grid=(steps,), in_specs=[spec for _, spec in opera...  102 us
    pallas_call x1, Pallas kernels, attend_weights(): pl.pallas_call(functools.partial(attend_weights_kernel, bits, orders), gr...  89.8 us
    unnamed x10, local copies, waits for them, and re-layouts  10.7 us

profile of v3, /device:TPU:0, one launch (start us, length us, event | category | flops | bytes accessed | tf_op | source)
XLA Modules:
  0.0 506.4 jit_solution(1278708711558799696)
XLA Ops:
  0.6 1.2 broadcast_subtract_fusion.refs_0_
  1.8 1.3 broadcast_in_dim.2.s_gain
  3.1 1.7 convert_element_type.3.s_three
  4.8 149.8 %shard_map.203 = (bf16[1024,2048]{1,0:T(8,128)(2,1)}, bf16[2048,1024]{1,0:T(8,128)(2,1)}, bf16[2048,1024]{1,0:T(8,128)(2,1)}, bf16[2048,1024]{1,0:T(8,128)(2,1)}...) custom-call(bf16[2048,1024]{1,0:T(8,128)(2,1)} %bitcast.13, ...), custom_call_target="tpu_custom_call" | custom-call | flops 34359738368 | bytes 67108864 | tf_op jit(solution)/shard_map/pallas_call | solution.py:1180
  154.7 101.9 %shard_map.204 = (bf16[2048,1024]{1,0:T(8,128)(2,1)}, bf16[1024,2048]{1,0:T(8,128)(2,1)}, bf16[2816,2048]{1,0:T(8,128)(2,1)}, bf16[2048,2816]{1,0:T(8,128)(2,1)}...) custom-call(s32[2]{0:T(128)} %broadcast_subtract_fusion.refs_0_, ...), custom_call_target="tpu_custom_call" | custom-call | flops 75161927680 | bytes 53219336 | tf_op jit(solution)/shard_map/pallas_call | solution.py:321
  256.6 145.9 %shard_map.205 = (f32[32,2816]{1,0:T(8,128)}, f32[32,2816]{1,0:T(8,128)}, f32[88,1024]{1,0:T(8,128)}, bf16[2048,1024]{1,0:T(8,128)(2,1)}, bf16[2048,1024]{1,0:T(8,128)(2,1)}, /*index=5*/bf16[2048,1024]{1,0:T(8,128)(2,1)}) custom-call(bf16[8,2,64,2048]{3,2,1,0:T(8,128)(2,1)} %bitcast.26, bf16[2048,2816]{1,0:T(8,128)(2,1)} %get-tuple-element.61.grad_one, ...), custom_call_target="tpu_custom_call" | custom-call | flops 61203283968 | bytes 134217728 | tf_op jit(solution)/shard_map/pallas_call | solution.py:750
  402.5 89.8 %shard_map.206 = (f32[32,5248]{1,0:T(8,128)}, f32[2048,1024]{1,0:T(8,128)}) custom-call(bf16[8,2,64,2048]{3,2,1,0:T(8,128)(2,1)} %bitcast.24, bf16[8,2,64,2048]{3,2,1,0:T(8,128)(2,1)} %bitcast.25, bf16[2048,1024]{1,0:T(8,128)(2,1)} %get-tuple-element.59.grad_low, bf16[2048,1024]{1,0:T(8,128)(2,1)} %get-tuple-element.72.grad_query.rows_query, ...), custom_call_target="tpu_custom_call" | custom-call | flops 38654705664 | bytes 67108864 | tf_op jit(solution)/shard_map/pallas_call | solution.py:929
  492.3 1.3 slice_reduce_fusion
  493.7 2.0 fusion
  495.7 0.0 copy-start.2
  495.7 0.0 copy-start.1
  495.7 0.0 copy-start
  495.7 8.5 %copy.27 = f32[2,1024,1024]{2,1,0:T(8,128)} copy(f32[2,1024,1024]{2,1,0:T(8,128)} %bitcast.11) | data formatting | bytes 16777216
  504.2 0.0 copy-done.2
  504.2 0.7 copy.28
  504.9 0.0 copy-done.1
  505.0 0.7 copy.29
  505.7 0.0 copy-done
  505.7 0.7 copy.30
Async XLA Ops:
  495.7 8.5 %copy-start.2 = (f32[32,2816]{1,0:T(8,128)S(1)}, f32[32,2816]{1,0:T(8,128)}, u32[]{:S(2)}) copy-start(f32[32,2816]{1,0:T(8,128)} %get-tuple-element.107) | copy-start | bytes 1081348
  495.7 9.3 %copy-start.1 = (f32[32,2816]{1,0:T(8,128)S(1)}, f32[32,2816]{1,0:T(8,128)}, u32[]{:S(2)}) copy-start(f32[32,2816]{1,0:T(8,128)} %get-tuple-element.108) | copy-start | bytes 1081348
  495.7 10.0 %copy-start = (f32[88,1024]{1,0:T(8,128)S(1)}, f32[88,1024]{1,0:T(8,128)}, u32[]{:S(2)}) copy-start(f32[88,1024]{1,0:T(8,128)} %get-tuple-element.109) | copy-start | bytes 1081348

commit v4 on v2

--- a/solution.py
+++ b/solution.py
@@ -210,19 +210,20 @@
 
 
 def feed_kernel(
-    per_seq, limits, residual, cotangent, w_one, w_two, w_three, w_out, gain, pre_gate,
+    per_seq, turned, lengths, residual, cotangent, w_one, w_two, w_three, w_out, gain, pre_gate,
     attended, queries,
-    layer_out, normed, glu, grad_one, grad_two, upstream_low, grad_residual, grad_low,
-    grad_gate, grad_attended, totals, grad_gain,
+    layer_out, normed, glu, grad_one, grad_two, upstream_low, grad_residual, gated,
+    grad_attended, totals, grad_gain, held=None,
 ):
     step = pl.program_id(0)
     row_count = residual.shape[0]
     spot = lax.broadcasted_iota(jnp.int32, (row_count, 1), 0) + (step % per_seq) * row_count
-    valid = (spot < limits[step // per_seq]).astype(WIDE)
+    limit = lengths[step // per_seq] - lax.axis_index("fsdp") * per_seq * row_count
+    valid = (spot < limit).astype(WIDE)
     res = residual[...]
     scale = rms_scale(res)
     rows = (res * scale).astype(LOW)
-    normed[...] = rows
+    normed[...] = rows.T if turned else rows
     upstream = cotangent[...].astype(WIDE) * valid
     up_low = upstream.astype(LOW)
     upstream_low[...] = up_low
@@ -230,30 +231,36 @@
         one = dot_nn(rows, w_one[:, c])
         two = dot_nn(rows, w_two[:, c])
         back = dot_nt(up_low, w_three[c, :])
-        glu[:, c] = (one * two).astype(LOW)
+        product = (one * two).astype(LOW)
+        if turned:
+            held[:, c] = product
+            glu[c, :] = product.T
+        else:
+            glu[:, c] = product
         grad_one[:, c] = (back * two).astype(LOW)
         grad_two[:, c] = (back * one).astype(LOW)
-    layer_out[...] = (valid * (res + dot_nn(glu[...], w_three[...]))).astype(LOW)
+    layer_out[...] = (valid * (res + dot_nn(held[...] if turned else glu[...], w_three[...]))).astype(LOW)
     back = dot_nt(grad_one[...], w_one[...]) + dot_nt(grad_two[...], w_two[...])
     grad = upstream + norm_back(res, scale, back)
     grad_residual[...] = grad
     grad = grad.astype(LOW)
-    grad_low[...] = grad
+    width = grad.shape[1]
+    gated[:, :width] = grad
     grad = dot_nt(grad, w_out[...])
     gate = jax.nn.sigmoid(pre_gate[...].astype(WIDE))
     att = attended[...].astype(WIDE)
     scale = rms_scale(att)
     hat = att * scale
-    gated = grad * gate
+    grad = grad * gate
 
     @pl.when(step == 0)
     def _():
         grad_gain[...] = jnp.zeros_like(grad_gain)
 
-    grad_gain[...] += jnp.sum(gated * hat, axis=0, keepdims=True)
-    gated = gated * gain[...]
-    grad_gate[...] = (gated * hat * (1.0 - gate)).astype(LOW)
-    grad_att = norm_back(att, scale, gated).astype(LOW)
+    grad_gain[...] += jnp.sum(grad * hat, axis=0, keepdims=True)
+    grad = grad * gain[...]
+    gated[:, width:] = (grad * hat * (1.0 - gate)).astype(LOW)
+    grad_att = norm_back(att, scale, grad).astype(LOW)
     grad_attended[...] = grad_att
 
     @pl.when(step % per_seq == 0)
@@ -335,30 +342,52 @@
     return bits
 
 
+LINKS = {
+    "1": (("dp", 3),),
+    "0": (("dp", 2),),
+    "z": (("dp", 3), ("dp", 2)),
+    "y": (("dp", 1),),
+    "x": (("fsdp", 0),),
+}
+CORE = ("dp", 0)
+SIDE = ("fsdp", 0)
+
+
 def bit_value(bit):
     axis, at = bit
     return lax.rem(lax.div(lax.axis_index(axis), 1 << at), 2)
 
 
-def flip_device(bit):
-    axis, at = bit
-    return {axis: lax.axis_index(axis) + (1 - 2 * bit_value(bit)) * (1 << at)}
-
-
-def greet(bits):
+def flips_of(name):
+    group = LINKS[name]
+    if len(group) == 1:
+        return [group]
+    return [group[:1], group[1:], group]
+
+
+def flip_device(flips):
+    place = {}
+    for axis, at in flips:
+        moved = place.get(axis, lax.axis_index(axis))
+        place[axis] = moved + (1 - 2 * bit_value((axis, at))) * (1 << at)
+    return place
+
+
+def greet(bits, far=True):
+    partners = [(bit,) for bit in bits] + ([LINKS["z"]] if far else [])
     barrier = pltpu.get_barrier_semaphore()
-    for bit in bits:
+    for flips in partners:
         pl.semaphore_signal(
-            barrier, inc=1, device_id=flip_device(bit), device_id_type=pl.DeviceIdType.MESH
+            barrier, inc=1, device_id=flip_device(flips), device_id_type=pl.DeviceIdType.MESH
         )
-    pl.semaphore_wait(barrier, len(bits))
+    pl.semaphore_wait(barrier, len(partners))
 
 
 class Sems:
     def __init__(self, send, recv):
         self.send, self.recv, self.used = send, recv, 0
 
-    def copy(self, src, dst, bit):
+    def copy(self, src, dst, flips):
         at = self.used
         self.used += 1
         return pltpu.make_async_remote_copy(
@@ -366,89 +395,742 @@
             dst_ref=dst,
             send_sem=self.send.at[at],
             recv_sem=self.recv.at[at],
-            device_id=flip_device(bit),
+            device_id=flip_device(flips),
             device_id_type=pl.DeviceIdType.MESH,
         )
 
 
 class Gather:
     def __init__(self, buf, bits, order, sems, columns=slice(None)):
-        self.stages = []
-        held = []
-
-        def cube(flipped=None):
+        self.stages, held = [], []
+
+        def cube(flips=()):
             index = []
             for bit in bits:
-                if bit == flipped:
-                    index.append(1 - bit_value(bit))
+                if bit in held:
+                    index.append(slice(None))
                 else:
-                    index.append(slice(None) if bit in held else bit_value(bit))
+                    index.append(1 - bit_value(bit) if bit in flips else bit_value(bit))
             return buf.at[tuple(index) + (slice(None), columns)]
 
-        for bit in order[:-1]:
-            ref = cube()
-            copies = [sems.copy(ref, ref, bit)]
-            if bit == order[-2]:
-                copies.append(sems.copy(ref, ref, order[-1]))
-                far = cube(flipped=bit)
-            self.stages.append(copies)
-            held.append(bit)
-        self.stages.append([sems.copy(far, far, order[-1])])
-
-    def start(self, stage):
-        for copy in self.stages[stage]:
+        for n, name in enumerate(order):
+            ref, flips = cube(), flips_of(name)
+            self.stages.append([sems.copy(ref, ref, flip) for flip in flips])
+            if n == len(order) - 1:
+                self.near = sems.copy(ref, ref, (CORE,))
+                far = [cube(flip) for flip in flips]
+                self.stages.append([sems.copy(ref, ref, (CORE,)) for ref in far])
+            held.extend(LINKS[name])
+
+    def start(self, k):
+        for copy in self.stages[k]:
             copy.start()
-
-    def arrive(self, stage):
-        self.stages[stage][0].wait_recv()
-
-    def advance(self, stage):
-        self.arrive(stage - 1)
-        self.start(stage)
+        if k == len(self.stages) - 2:
+            self.near.start()
+
+    def advance(self, k):
+        if k:
+            for copy in self.stages[k - 1]:
+                copy.wait_recv()
+        self.start(k)
 
     def finish(self):
-        self.stages[-2][1].wait_recv()
-        self.stages[-1][0].wait_recv()
+        self.near.wait_recv()
+        for copy in self.stages[-1]:
+            copy.wait_recv()
 
     def drain(self):
-        for copies in self.stages:
-            for copy in copies:
-                copy.wait_send()
-
-
-FORWARD_COPIES = 80
+        for copy in [c for stage in self.stages for c in stage] + [self.near]:
+            copy.wait_send()
+
+
+class Scatter:
+    def __init__(self, sems, bits, order, acc, send, come, recvs, columns, slots):
+        self.bits, self.order, self.acc, self.columns = bits, order, acc, columns
+        self.come, self.recvs, self.slots = come, recvs, slots
+        rows = (slice(None),)
+        full = (slice(None),) * len(bits) + rows
+        self.core = sems.copy(send.at[full + (slots,)], come.at[full + (slots,)], (CORE,))
+        self.copies, self.done = [], []
+        for k, name in enumerate(order):
+            (bit,) = LINKS[name]
+            done = [LINKS[n][0] for n in order[:k]]
+            index = tuple(
+                1 - bit_value(b) if b == bit else bit_value(b) if b in done else slice(None)
+                for b in bits
+            )
+            free = (slice(None),) * (len(bits) - k - 1)
+            source = acc.at[index + rows + (columns,)]
+            self.copies.append(sems.copy(source, recvs[k].at[free + rows + (columns,)], (bit,)))
+            self.done.append(done)
+
+    def add(self, done, source, columns):
+        free = [b for b in self.bits if b not in done]
+
+        def one(k):
+            at = [(k // (1 << (len(free) - 1 - n))) % 2 for n in range(len(free))]
+            mine = tuple(bit_value(b) if b in done else at[free.index(b)] for b in self.bits)
+            here = mine + (slice(None), self.columns)
+            self.acc[here] = self.acc[here] + source[tuple(at) + (slice(None), columns)]
+
+        if len(free) <= 2:
+            for k in range(1 << len(free)):
+                one(k)
+        else:
+            lax.fori_loop(0, 1 << len(free), lambda k, c: (one(k), c)[1], 0)
+
+    def launch(self):
+        self.core.start()
+
+    def advance(self, k):
+        if k == 0:
+            self.core.wait_recv()
+            self.add([], self.come, self.slots)
+        else:
+            self.copies[k - 1].wait_recv()
+            self.add(self.done[k - 1] + [LINKS[self.order[k - 1]][0]], self.recvs[k - 1], self.columns)
+        self.copies[k].start()
+
+    def result(self):
+        self.copies[-1].wait_recv()
+        own = tuple(bit_value(b) for b in self.bits)
+        here = (slice(None), self.columns)
+        return self.acc[own + here].astype(WIDE) + self.recvs[-1][here].astype(WIDE)
+
+    def drain(self, core=True):
+        if core:
+            self.core.wait_send()
+        for copy in self.copies:
+            copy.wait_send()
+
+
+def run_events(step, events):
+    for at in sorted(events):
+
+        @pl.when(step == at)
+        def _():
+            for action in events[at]:
+                action()
+
+
+def planned(table, pieces, low, high):
+    events = {}
+    for at, todo in table:
+        if low <= at < high:
+            events[at] = [functools.partial(pieces[name].advance, k) for name, k in todo]
+    return events
+
+
+FORWARD_PLAN = (
+    (0, (
+        ("a00", 0), ("a01", 0), ("a11", 0), ("f5", 0), ("f0", 0), ("f4", 0), ("a02", 0),
+        ("a00", 1), ("a01", 1), ("a10", 0), ("a12", 0), ("a02", 1), ("a00", 2), ("a11", 1),
+        ("a01", 2), ("a12", 1), ("a02", 2), ("a11", 2), ("a20", 0), ("a12", 2), ("a21", 0),
+        ("a10", 1), ("a22", 0), ("a20", 1), ("a00", 3), ("a21", 1), ("f1", 0), ("f3", 0),
+        ("a11", 3), ("a20", 2), ("a01", 3), ("a02", 3), ("f5", 1), ("a12", 3), ("a10", 2),
+        ("f1", 1), ("a22", 1), ("f3", 1), ("a11", 4), ("a00", 4), ("a21", 2),
+    )),
+    (1, (("a20", 3), ("a12", 4), ("f0", 1), ("f2", 0))),
+    (2, (("f1", 2),)),
+    (3, (("f5", 2),)),
+    (4, (("a22", 2),)),
+    (5, (("f3", 2),)),
+    (6, (("a20", 4), ("f2", 1))),
+    (7, (("a21", 3),)),
+    (8, (("f0", 2), ("a22", 3), ("f1", 3), ("a10", 3), ("a21", 4))),
+    (9, (("f2", 2), ("f4", 1))),
+    (10, (("f5", 3), ("f2", 3))),
+    (11, (("f3", 3), ("f1", 4))),
+    (12, (("f0", 3),)),
+    (13, (("f4", 2),)),
+    (14, (("f2", 4), ("f5", 4))),
+    (16, (("f4", 3), ("f0", 4), ("f3", 4))),
+)
+FEED_BACK_PLAN = (
+    (7, (("one0", 0), ("two0", 0))),
+    (13, (("one0", 1), ("two0", 1))),
+    (15, (("three0", 0), ("three1", 0))),
+    (16, (("one0", 2),)),
+    (17, (("two0", 2),)),
+    (18, (("one1", 0), ("two1", 0), ("two0", 3))),
+    (20, (("one0", 3), ("one2", 0))),
+    (21, (("two2", 0), ("three1", 1), ("three0", 1))),
+    (24, (("one1", 1), ("two1", 1), ("one2", 1))),
+    (25, (("three1", 2), ("two2", 1), ("three0", 2))),
+    (26, (("one1", 2), ("three0", 3), ("one2", 2))),
+    (27, (
+        ("three1", 3), ("two1", 2), ("two2", 2), ("one2", 3), ("one1", 3), ("two1", 3),
+        ("two2", 3),
+    )),
+)
+ATTEND_BACK_PLAN = (
+    (4, (("p0", 0),)),
+    (6, (("p1", 0), ("p2", 0))),
+    (9, (("p3", 0), ("p0", 1), ("p2", 1), ("p4", 0))),
+    (10, (("p5", 0),)),
+    (11, (("p1", 1), ("p6", 0))),
+    (12, (("p2", 2),)),
+    (14, (("p2", 3), ("p4", 1), ("p0", 2), ("p3", 1), ("p5", 1))),
+    (15, (("p1", 2), ("p6", 1))),
+    (16, (("p4", 2), ("p0", 3), ("p3", 2), ("p5", 2))),
+    (17, (("p4", 3), ("p1", 3), ("p6", 2))),
+    (18, (("p6", 3), ("p5", 3), ("p3", 3))),
+)
+
+
+def attend_back_step(
+    same, queries, keys, values, grad_attended, pre_query, pre_key, prefix, grads, carry,
+):
+    marks = head_rows()
+    causal, causal_t = causal_masks()
+    width = queries.shape[1]
+    for g in groups(width):
+        q, k, v, ga = queries[:, g], keys[:, g], values[:, g], grad_attended[:, g]
+        qs, ks, vs, gs = (split_heads(rows, marks) for rows in (q, k, v, ga))
+        state = open_state(prefix[0, :, g].astype(WIDE), same)
+        grad_state = open_state(carry[:, g], same)
+        grad_scores = (dot_nt(ga, vs) * causal).astype(LOW)
+        gq = dot_nn(grad_scores, ks) + dot_nt(ga, state)
+        grad_scores = (dot_nt(v, gs) * causal_t).astype(LOW)
+        gk = dot_nn(grad_scores, qs) + dot_nt(v, grad_state)
+        scores = (dot_nt(k, qs) * causal_t).astype(LOW)
+        gv = dot_nn(scores, gs) + dot_nn(k, grad_state)
+        gq = gq * silu_slope(pre_query[:, g].astype(WIDE))
+        gk = gk * silu_slope(pre_key[:, g].astype(WIDE))
+        for n, grad in enumerate((gq, gk, gv)):
+            grads[:, n * width + g.start : n * width + g.stop] = grad.astype(LOW)
+        carry[:, g] += pack_state(dot_tn(q, ga), same)
+
+
+def clip(value, low, high):
+    return jnp.minimum(jnp.maximum(value, low), high)
+
+
+CHUNK = 256
+PAIRS = (4, 4, 3)
+PAIR_ORDERS = (("0xy1", "y0x1"), ("xy10", "x0y1"), ("yx01", "yx01"))
+THREE_ORDERS = ("01y", "y01")
+THREE_AFTER = 1
+
+
+def feed_back_blocks():
+    pairs, three, at = [], None, 0
+    for n, count in enumerate(PAIRS):
+        if n == THREE_AFTER:
+            three = (at, 8)
+            at += 8
+        pairs.append((at, count))
+        at += count
+    return pairs, three, at
+
+
+class ThreeScatter(Scatter):
+    def last_swap(self, sems, out, give, take):
+        self.out, self.give, self.take = out, give, take
+        cols = self.columns
+        self.swap = sems.copy(give.at[:, cols], take.at[:, cols], (SIDE,))
+
+    def advance(self, k):
+        if k < len(self.order):
+            super().advance(k)
+            return
+        cols = self.columns
+        total = self.result()
+        deep = total.shape[0] // 2
+        low, high = total[:deep], total[deep:]
+        upper = bit_value(SIDE).astype(WIDE)
+        self.out[:, cols] = low * (1 - upper) + high * upper
+        self.give[:, cols] = low * upper + high * (1 - upper)
+        self.swap.start()
+
+    def finish(self):
+        self.swap.wait_recv()
+        self.out[:, self.columns] += self.take[:, self.columns]
+        self.swap.wait_send()
+
+
+def feed_back_kernel(
+    per_seq, bits,
+    normed_hbm, grad_one, grad_two, glu, upstream_hbm,
+    queries, keys, values, grad_attended, pre_query, pre_key, prefix, totals,
+    out_one, out_two, out_three, grads,
+    normed, upstream, acc, come1, come2, come3, come4, send, come,
+    acc3, come31, come32, come33, send3, take3, last_send, last_come,
+    state_out, state_in, carry, part, part3, send_sems, recv_sems, local,
+):
+    step = pl.program_id(0)
+    pairs, three_block, base = feed_back_blocks()
+    links = [bit for bit in bits if bit != CORE]
+    mine, side = bit_value(CORE), bit_value(SIDE)
+    other = 1 - mine
+    sems = Sems(send_sems, recv_sems)
+    hidden, width = out_one.shape[1], out_three.shape[1]
+    recvs = (come1, come2, come3, come4)
+    pieces, ends, first = {}, [], 0
+    for n, count in enumerate(PAIRS):
+        for w, (name, out) in enumerate((("one", out_one), ("two", out_two))):
+            begin = w * hidden + first * CHUNK
+            span = count * CHUNK
+            pieces[f"{name}{n}"] = Scatter(
+                sems, links, PAIR_ORDERS[n][w], acc, send.at[n % 2, w], come.at[n, w], recvs,
+                slice(begin, begin + span), slice(0, span),
+            )
+            ends.append((pieces[f"{name}{n}"], out, first * CHUNK))
+        first += count
+    half = width // 2
+    threes = []
+    for n in range(2):
+        cols = slice(n * half, (n + 1) * half)
+        piece = ThreeScatter(
+            sems, links[:-1], THREE_ORDERS[n], acc3, send3, take3, (come31, come32, come33),
+            cols, cols,
+        )
+        piece.last_swap(sems, out_three, last_send, last_come)
+        pieces[f"three{n}"] = piece
+        threes.append(piece)
+    swap_state = sems.copy(state_out, state_in, (SIDE,))
+    load = [
+        pltpu.make_async_copy(normed_hbm, normed, local.at[0]),
+        pltpu.make_async_copy(upstream_hbm, upstream, local.at[1]),
+    ]
+
+    @pl.when(step == 0)
+    def _():
+        for copy in load:
+            copy.start()
+        greet(bits, far=False)
+        state_out[...] = totals[...].astype(LOW)
+        swap_state.start()
+        load[0].wait()
+
+    @pl.when(step == three_block[0])
+    def _():
+        load[1].wait()
+
+    for n in range(2, len(PAIRS)):
+
+        @pl.when(step == pairs[n][0])
+        def _():
+            pieces[f"one{n - 2}"].core.wait_send()
+            pieces[f"two{n - 2}"].core.wait_send()
+
+    @pl.when(step < base)
+    def _():
+        run_events(step, planned(FEED_BACK_PLAN, pieces, 0, base))
+
+    @pl.when(step >= base)
+    def _():
+        run_events(step, planned(FEED_BACK_PLAN, pieces, base, base + 8))
+
+    lead = acc.shape[:-1]
+    fill = (slice(None),) * len(lead)
+
+    def weight_chunk(w, rhs, chunk, group, first):
+        part[...] = dot_nn(normed[...], rhs[...]).astype(LOW).reshape(part.shape)
+        at = pl.ds(pl.multiple_of(chunk * CHUNK, CHUNK), CHUNK)
+        send[(group % 2, w) + fill + (at,)] = part[:, other].reshape(lead + (CHUNK,))
+        at = pl.ds(pl.multiple_of(w * hidden + (first + chunk) * CHUNK, CHUNK), CHUNK)
+        acc[fill + (at,)] = part[:, mine].reshape(lead + (CHUNK,))
+
+    first = 0
+    for n, (begin, count) in enumerate(pairs):
+
+        @pl.when((step >= begin) & (step < begin + count))
+        def _():
+            weight_chunk(0, grad_one, step - begin, n, first)
+            weight_chunk(1, grad_two, step - begin, n, first)
+
+        @pl.when(step == begin + count - 1)
+        def _():
+            pieces[f"one{n}"].launch()
+            pieces[f"two{n}"].launch()
+
+        first += count
+
+    begin, count = three_block
+
+    @pl.when((step >= begin) & (step < begin + count))
+    def _():
+        k = step - begin
+        at = tuple((k // (1 << (2 - d))) % 2 for d in range(3))
+        part3[...] = dot_nn(glu[...], upstream[...]).astype(LOW).reshape(part3.shape)
+        send3[at] = part3[other]
+        acc3[at] = part3[mine]
+
+    @pl.when(step == begin + count - 1)
+    def _():
+        for piece in threes:
+            piece.launch()
+
+    @pl.when(step >= base)
+    def _():
+        at = step - base
+
+        @pl.when(at == 0)
+        def _():
+            swap_state.wait_recv()
+
+        @pl.when(at % per_seq == 0)
+        def _():
+            carry[...] = state_in[at // per_seq].astype(WIDE) * (1 - side).astype(WIDE)
+
+        attend_back_step(
+            head_square(), queries, keys, values, grad_attended, pre_query, pre_key, prefix,
+            grads, carry,
+        )
+
+    @pl.when(step == pl.num_programs(0) - 1)
+    def _():
+        for actions in planned(FEED_BACK_PLAN, pieces, base + 8, 1000).values():
+            for action in actions:
+                action()
+        for piece, out, begin in ends:
+            span = piece.columns.stop - piece.columns.start
+            out[:, begin : begin + span] = piece.result()
+        for n in range(len(PAIRS)):
+            for name in ("one", "two"):
+                pieces[f"{name}{n}"].drain(core=n + 2 >= len(PAIRS))
+        for piece in threes:
+            piece.finish()
+            piece.drain()
+        swap_state.wait_send()
+
+
+def feed_back(
+    seq_count, normed, grad_one, grad_two, glu, upstream, queries, keys, values, grad_attended,
+    pre_query, pre_key, prefix, totals,
+):
+    row_count, width = queries.shape
+    hidden = grad_one.shape[1]
+    steps = row_count // BLOCK
+    per_seq = steps // seq_count
+    bits = index_bits()
+    pairs, three, base = feed_back_blocks()
+    deep = hidden // 8
+    slab = width // 32
+
+    def pair_at(i):
+        done = sum(clip(i - begin, 0, count) for begin, count in pairs)
+        return jnp.minimum(done, sum(PAIRS) - 1)
+
+    def back(i):
+        at = clip(i - base, 0, steps - 1)
+        return (at // per_seq) * per_seq + per_seq - 1 - at % per_seq
+
+    rows = pl.BlockSpec((BLOCK, width), lambda i: (back(i), 0))
+    pair = pl.BlockSpec((row_count, CHUNK), lambda i: (0, pair_at(i)))
+    vmem = pl.BlockSpec(memory_space=pltpu.VMEM)
+    hbm = pl.BlockSpec(memory_space=pl.ANY)
+    low = functools.partial(pltpu.VMEM, dtype=LOW)
+    span = max(PAIRS) * CHUNK
+    copies = 10 * len(PAIRS) + 2 * 5 + 1
+    return pl.pallas_call(
+        functools.partial(feed_back_kernel, per_seq, bits),
+        grid=(base + steps,),
+        in_specs=[
+            hbm, pair, pair,
+            pl.BlockSpec((deep, row_count), lambda i: (clip(i - three[0], 0, 7), 0)),
+            hbm,
+        ]
+        + [rows] * 6
+        + [pl.BlockSpec((1, HD, width), lambda i: (back(i), 0, 0)), vmem],
+        out_specs=[vmem] * 3 + [pl.BlockSpec((BLOCK, 3 * width), lambda i: (back(i), 0))],
+        out_shape=[
+            jax.ShapeDtypeStruct((slab, hidden), WIDE),
+            jax.ShapeDtypeStruct((slab, hidden), WIDE),
+            jax.ShapeDtypeStruct((hidden // 32, width), WIDE),
+            jax.ShapeDtypeStruct((row_count, 3 * width), LOW),
+        ],
+        scratch_shapes=[
+            low((width, row_count)),
+            low((row_count, width)),
+            low((2, 2, 2, 2, slab, 2 * hidden)),
+            low((2, 2, 2, slab, 2 * hidden)),
+            low((2, 2, slab, 2 * hidden)),
+            low((2, slab, 2 * hidden)),
+            low((slab, 2 * hidden)),
+            low((2, 2, 2, 2, 2, 2, slab, span)),
+            low((len(PAIRS), 2, 2, 2, 2, 2, slab, span)),
+            low((2, 2, 2, deep // 2, width)),
+            low((2, 2, deep // 2, width)),
+            low((2, deep // 2, width)),
+            low((deep // 2, width)),
+            low((2, 2, 2, deep // 2, width)),
+            low((2, 2, 2, deep // 2, width)),
+            pltpu.VMEM((hidden // 32, width), WIDE),
+            pltpu.VMEM((hidden // 32, width), WIDE),
+            low((seq_count, HD, width)),
+            low((seq_count, HD, width)),
+            pltpu.VMEM((HD, width), WIDE),
+            low((8, 2, width // 16, CHUNK)),
+            low((2, deep // 2, width)),
+            pltpu.SemaphoreType.DMA((copies,)),
+            pltpu.SemaphoreType.DMA((copies,)),
+            pltpu.SemaphoreType.DMA((2,)),
+        ],
+        compiler_params=pltpu.CompilerParams(
+            dimension_semantics=("arbitrary",),
+            vmem_limit_bytes=63 << 20,
+            collective_id=2,
+            has_side_effects=True,
+        ),
+        cost_estimate=pl.CostEstimate(
+            flops=6 * row_count * width * hidden + 12 * row_count * width * width,
+            bytes_accessed=128 << 20,
+            transcendentals=0,
+        ),
+    )(
+        normed, grad_one, grad_two, glu, upstream, queries, keys, values, grad_attended,
+        pre_query, pre_key, prefix, totals,
+    )
+
+
+WIDE_CHUNK = 512
+PARTS = (2, 2, 1, 2, 1, 1, 1)
+PART_ORDERS = ("01xy", "y01x", "x0y1", "xy01", "y0x1", "yx10", "x0y1")
+
+
+def attend_weights_kernel(
+    bits,
+    normed_hbm, mixed_hbm, gated, grads, gain_term, rows_three, rows_gate, weights_hbm, tok,
+    grad_residual,
+    out, input_grad,
+    normed, mixed, weights, acc, come1, come2, come3, come4, send, come, part,
+    send_sems, recv_sems, local,
+):
+    step = pl.program_id(0)
+    links = [bit for bit in bits if bit != CORE]
+    mine = bit_value(CORE)
+    other = 1 - mine
+    sems = Sems(send_sems, recv_sems)
+    width = tok.shape[1]
+    per = width // WIDE_CHUNK
+    chunks = 5 * per
+    lead = acc.shape[:-1]
+    fill = (slice(None),) * len(lead)
+
+    def column(chunk):
+        return chunk * WIDE_CHUNK + (128 if chunk >= per else 0)
+
+    pieces, first = {}, 0
+    launches = {}
+    for n, count in enumerate(PARTS):
+        cols = slice(column(first), column(first + count))
+        first += count
+        pieces[f"p{n}"] = Scatter(
+            sems, links, PART_ORDERS[n], acc, send, come, (come1, come2, come3, come4), cols, cols
+        )
+        launches[first - 1] = [pieces[f"p{n}"].launch]
+    load = [
+        pltpu.make_async_copy(mixed_hbm, mixed, local.at[0]),
+        pltpu.make_async_copy(normed_hbm, normed, local.at[1]),
+        pltpu.make_async_copy(weights_hbm.at[:, : 4 * width], weights, local.at[2]),
+    ]
+
+    @pl.when(step == 0)
+    def _():
+        for copy in load:
+            copy.start()
+        greet(bits, far=False)
+        load[0].wait()
+
+    @pl.when(step == per)
+    def _():
+        load[1].wait()
+
+    @pl.when(step == chunks)
+    def _():
+        load[2].wait()
+
+    run_events(step, planned(ATTEND_BACK_PLAN, pieces, 0, chunks + 8))
+
+    def chunk_phase(begin, end, lhs, rhs, shift):
+        @pl.when((step >= begin) & (step < end))
+        def _():
+            at = pl.ds(pl.multiple_of(step * WIDE_CHUNK + shift, 128), WIDE_CHUNK)
+            part[...] = dot_nn(lhs[...], rhs[...]).astype(LOW).reshape(part.shape)
+            send[fill + (at,)] = part[:, other].reshape(lead + (WIDE_CHUNK,))
+            acc[fill + (at,)] = part[:, mine].reshape(lead + (WIDE_CHUNK,))
+
+    chunk_phase(0, per, mixed, gated, 0)
+    chunk_phase(per, 2 * per, normed, gated, 128)
+    chunk_phase(2 * per, chunks, normed, grads, 128)
+
+    @pl.when(step == 0)
+    def _():
+        column = jnp.broadcast_to(gain_term[...], (128, width)).T
+        column = column.reshape(8, 2, width // 16, 128)
+        upper = mine.astype(WIDE)
+        low, high = column[:, 0], column[:, 1]
+        at = fill + (slice(width, width + 128),)
+        acc[at] = (low * (1 - upper) + high * upper).astype(LOW).reshape(lead + (128,))
+        send[at] = (low * upper + high * (1 - upper)).astype(LOW).reshape(lead + (128,))
+
+    run_events(step, launches)
+
+    @pl.when(step >= chunks)
+    def _():
+        def weight(n):
+            return weights[:, n * width : (n + 1) * width]
+
+        def row(n):
+            return rows_three[:, n * width : (n + 1) * width]
+
+        grad = dot_nt(row(0), weight(2)) + dot_nt(row(1), weight(0))
+        grad += dot_nt(row(2), weight(1)) + dot_nt(rows_gate[...], weight(3))
+        x = tok[...].astype(WIDE)
+        grad = grad_residual[...] + norm_back(x, rms_scale(x), grad)
+        input_grad[...] = grad.astype(input_grad.dtype)
+
+    @pl.when(step == pl.num_programs(0) - 1)
+    def _():
+        for actions in planned(ATTEND_BACK_PLAN, pieces, chunks + 8, 1000).values():
+            for action in actions:
+                action()
+        for piece in pieces.values():
+            out[:, piece.columns] = piece.result()
+        for piece in pieces.values():
+            piece.drain()
+
+
+def attend_weights(normed, mixed, gated, grads, gain_term, full_attn, tok, grad_residual):
+    row_count, width = tok.shape
+    steps = row_count // BLOCK
+    bits = index_bits()
+    per = width // WIDE_CHUNK
+    chunks = 5 * per
+    slab = width // 32
+    vmem = pl.BlockSpec(memory_space=pltpu.VMEM)
+    hbm = pl.BlockSpec(memory_space=pl.ANY)
+
+    def rows(size, column=0):
+        return pl.BlockSpec((BLOCK, size), lambda i: (clip(i - chunks, 0, steps - 1), column))
+
+    def chunk(begin, count):
+        return pl.BlockSpec(
+            (row_count, WIDE_CHUNK), lambda i: (0, clip(i - begin, 0, count - 1))
+        )
+
+    low = functools.partial(pltpu.VMEM, dtype=LOW)
+    columns = 5 * width + 128
+    copies = 5 * len(PARTS)
+    return pl.pallas_call(
+        functools.partial(attend_weights_kernel, bits),
+        grid=(chunks + steps,),
+        in_specs=[hbm, hbm, chunk(0, 2 * per), chunk(2 * per, 3 * per), vmem, rows(3 * width),
+                  rows(width, 1), hbm, rows(width), rows(width)],
+        out_specs=[vmem, rows(width)],
+        out_shape=[
+            jax.ShapeDtypeStruct((slab, columns), WIDE),
+            jax.ShapeDtypeStruct((row_count, width), WIDE),
+        ],
+        scratch_shapes=[
+            low((width, row_count)),
+            low((width, row_count)),
+            low((width, 4 * width)),
+            low((2, 2, 2, 2, slab, columns)),
+            low((2, 2, 2, slab, columns)),
+            low((2, 2, slab, columns)),
+            low((2, slab, columns)),
+            low((slab, columns)),
+            low((2, 2, 2, 2, slab, columns)),
+            low((2, 2, 2, 2, slab, columns)),
+            low((8, 2, width // 16, WIDE_CHUNK)),
+            pltpu.SemaphoreType.DMA((copies,)),
+            pltpu.SemaphoreType.DMA((copies,)),
+            pltpu.SemaphoreType.DMA((3,)),
+        ],
+        compiler_params=pltpu.CompilerParams(
+            dimension_semantics=("arbitrary",),
+            vmem_limit_bytes=62 << 20,
+            collective_id=3,
+            has_side_effects=True,
+        ),
+        cost_estimate=pl.CostEstimate(
+            flops=18 * row_count * width * width, bytes_accessed=64 << 20, transcendentals=0
+        ),
+    )(normed, mixed, gated, grads, gain_term, grads, gated, full_attn, tok, grad_residual)
+
+
+ATTEND_PIECES = (
+    (("a00", "10yx", 6), ("a01", "zxy", 5), ("a02", "zyx", 5)),
+    (("a10", "zyx", 9), ("a11", "x10y", 4), ("a12", "10xy", 3)),
+    (("a20", "10xy", 4), ("a21", "10yx", 2), ("a22", "zyx", 3)),
+)
+FEED_PIECES = (
+    (("f0", "y10x", 13), ("f1", "10yx", 9)),
+    (("f2", "10yx", 7), ("f3", "1xy0", 15)),
+)
+THREE_PIECES = (("f4", "zy", 3), ("f5", "10y", 5))
+FORWARD_COPIES = 128
+
+
+class ThreeGather(Gather):
+    def first_swap(self, sems, columns, give, take, slab, target, local):
+        self.cols, self.give, self.take, self.slab = columns, give, take, slab
+        self.swap = sems.copy(give.at[:, columns], take.at[:, columns], (SIDE,))
+        self.place = pltpu.make_async_copy(slab.at[:, columns], target.at[:, columns], local)
+
+    def advance(self, k):
+        if k == 0:
+            self.swap.start()
+            return
+        if k == 1:
+            self.swap.wait_recv()
+            upper = bit_value(SIDE).astype(WIDE)
+            mine, theirs = self.give[:, self.cols], self.take[:, self.cols]
+            low = mine * (1 - upper) + theirs * upper
+            high = mine * upper + theirs * (1 - upper)
+            self.slab[:, self.cols] = jnp.concatenate([low, high], axis=0).astype(LOW)
+            self.place.start()
+            self.place.wait()
+        super().advance(k - 1)
+
+    def drain(self):
+        super().drain()
+        self.swap.wait_send()
 
 
 def forward_kernel(
-    steps, per_seq, bits, waves, feed_orders, three_order,
+    steps, per_seq, bits,
     tok, s_key, s_value, s_query, s_gate, s_out, s_gain, s_one, s_two, s_three,
     normed, pre_key, keys, values, pre_query, queries, pre_gate, attended, mixed, residual,
     prefix, gain_row, full_attn, full_one, full_two, full_three,
     held, all_keys, all_values, all_normed, totals, state_out, state_in, carry,
-    three_in, three_slab, send, recv, local,
+    three_out, three_in, three_slab, send, recv, local,
 ):
     step = pl.program_id(0)
     width = tok.shape[1]
-    last = bits[-1]
     sems = Sems(send, recv)
-    attn = [
-        [Gather(held, bits, order, sems, columns) for order, columns in wave] for wave in waves
-    ]
-    feed = [
-        Gather(buf, bits, order, sems)
-        for buf, order in zip((full_one, full_two), feed_orders)
-    ]
-    three = Gather(full_three, bits[:-1], three_order, sems)
-    swap_three = sems.copy(s_three, three_in, last)
-    swap_state = sems.copy(state_out, state_in, last)
     own = tuple(bit_value(bit) for bit in bits)
-    keep_attn = pltpu.make_async_copy(held, full_attn, local.at[3])
-
-    def feed_advance(stage):
-        for piece in feed:
-            piece.advance(stage)
-        if stage > 1:
-            three.advance(stage - 1)
+    side = bit_value(SIDE).astype(WIDE)
+    pieces, waves, start = {}, [], 0
+    for wave in ATTEND_PIECES:
+        waves.append([])
+        for name, order, tiles in wave:
+            cols = slice(start, start + 128 * tiles)
+            start += 128 * tiles
+            pieces[name] = Gather(held, bits, order, sems, cols)
+            waves[-1].append(pieces[name])
+    feed = []
+    for buf, parts in zip((full_one, full_two), FEED_PIECES):
+        start = 0
+        for name, order, tiles in parts:
+            cols = slice(start, start + 128 * tiles)
+            start += 128 * tiles
+            pieces[name] = Gather(buf, bits, order, sems, cols)
+            feed.append(pieces[name])
+    start = 0
+    for n, (name, order, tiles) in enumerate(THREE_PIECES):
+        cols = slice(start, start + 128 * tiles)
+        start += 128 * tiles
+        pieces[name] = ThreeGather(full_three, bits[:-1], order, sems, cols)
+        pieces[name].first_swap(
+            sems, cols, three_out, three_in, three_slab, full_three.at[own[:-1]], local.at[2 + n]
+        )
+        feed.append(pieces[name])
+    swap_state = sems.copy(state_out, state_in, (SIDE,))
+    keep_attn = pltpu.make_async_copy(held, full_attn, local.at[4])
 
     @pl.when(step == 0)
     def _():
@@ -461,50 +1143,26 @@
         for n, shard in enumerate((s_key, s_value, s_query, s_gate, s_out)):
             held[own + (slice(None), slice(n * width, (n + 1) * width))] = shard[...]
         held[own + (slice(None), slice(5 * width, 5 * width + 128))] = s_gain[...]
+        three_out[...] = s_three[...].astype(WIDE)
         greet(bits)
-        for wave in attn:
-            for piece in wave:
-                piece.start(0)
-        swap_three.start()
         for copy in place:
             copy.wait()
-        for stage in range(1, len(bits)):
-            for wave in attn:
-                for piece in wave:
-                    piece.advance(stage)
-            if stage == 1:
-                for piece in feed:
-                    piece.start(0)
-                swap_three.wait_recv()
-                mine = (own[-1] == 0).astype(WIDE)
-                low, high = s_three[...], three_in[...]
-                three_slab[...] = jnp.concatenate(
-                    [mine * low + (1 - mine) * high, mine * high + (1 - mine) * low], axis=0
-                ).astype(LOW)
-                lay = pltpu.make_async_copy(three_slab, full_three.at[own[:-1]], local.at[2])
-                lay.start()
-                lay.wait()
-                three.start(0)
-        for piece in attn[0]:
+        for actions in planned(FORWARD_PLAN, pieces, 0, 1).values():
+            for action in actions:
+                action()
+        for piece in waves[0]:
             piece.finish()
-        feed_advance(1)
-
-    @pl.when(step == 3)
-    def _():
-        feed_advance(2)
 
     @pl.when(step == steps)
     def _():
-        for wave in attn[1:]:
+        for wave in waves[1:]:
             for piece in wave:
                 piece.finish()
         keep_attn.start()
         column = held[..., 5 * width : 5 * width + 128].reshape(width, 128)
         gain_row[...] = column.astype(WIDE).T[:1]
 
-    @pl.when(step == steps + 1)
-    def _():
-        feed_advance(3)
+    run_events(step + 1, planned(FORWARD_PLAN, pieces, 1, 2 * steps + 1))
 
     def weight(n):
         return held[..., n * width : (n + 1) * width].reshape(width, width)
@@ -515,7 +1173,7 @@
     def _():
         x = tok[...].astype(WIDE)
         rows = (x * rms_scale(x)).astype(LOW)
-        normed[...] = rows
+        normed[...] = rows.T
         here = pl.ds(pl.multiple_of(step * BLOCK, BLOCK), BLOCK)
         all_normed[here, :] = rows
         pre = dot_nn(rows, weight(0))
@@ -557,7 +1215,7 @@
 
         @pl.when(at % per_seq == 0)
         def _():
-            carry[...] = state_in[at // per_seq].astype(WIDE) * own[-1].astype(WIDE)
+            carry[...] = state_in[at // per_seq].astype(WIDE) * side
 
         marks = head_rows()
         causal, _ = causal_masks()
@@ -572,28 +1230,20 @@
         rows = attended[...].astype(WIDE)
         rows = rows * rms_scale(rows) * gain_row[...] * jax.nn.sigmoid(gate)
         rows = rows.astype(LOW)
-        mixed[...] = rows
+        mixed[...] = rows.T
         residual[...] = tok[...].astype(WIDE) + dot_nn(rows, weight(4))
 
     @pl.when(step == 2 * steps - 1)
     def _():
-        feed_advance(4)
+        for actions in planned(FORWARD_PLAN, pieces, 2 * steps + 1, 1000).values():
+            for action in actions:
+                action()
         for piece in feed:
             piece.finish()
-        three.finish()
-        for piece in [p for wave in attn for p in wave] + feed + [three]:
+        for piece in pieces.values():
             piece.drain()
-        swap_three.wait_send()
         swap_state.wait_send()
         keep_attn.wait()
-
-
-def tile_cuts(start, tiles):
-    cuts = []
-    for count in tiles:
-        cuts.append(slice(start, start + 128 * count))
-        start += 128 * count
-    return cuts
 
 
 def forward(tok, seq_count, shards_attn, gain_columns, s_one, s_two, s_three):
@@ -602,65 +1252,58 @@
     steps = row_count // BLOCK
     per_seq = steps // seq_count
     bits = index_bits()
-    orders = [[(s[0], s[1]) for s in reversed(order)] for order in stream_orders()]
-    third = width // 128
-    waves = [
-        list(zip(orders, tile_cuts(0, (6, 5, 5)))),
-        list(zip(orders, tile_cuts(2 * width, (5, 6, 5)))),
-        list(zip(orders, tile_cuts(4 * width, (3, 3, 3)))),
-    ]
-    feed_orders = [orders[0], orders[2]]
-    three_order = [bit for bit in orders[1] if bit != bits[-1]]
     lead = (2,) * len(bits)
     slab = s_one.shape[0]
     deep = s_three.shape[0]
+    columns = 5 * width + 128
     in_rows = pl.BlockSpec((BLOCK, width), lambda i: (i % steps, 0))
     first = pl.BlockSpec((BLOCK, width), lambda i: (jnp.minimum(i, steps - 1), 0))
     second = pl.BlockSpec((BLOCK, width), lambda i: (jnp.maximum(i - steps, 0), 0))
+    first_turned = pl.BlockSpec((width, BLOCK), lambda i: (0, jnp.minimum(i, steps - 1)))
+    second_turned = pl.BlockSpec((width, BLOCK), lambda i: (0, jnp.maximum(i - steps, 0)))
     any_spec = pl.BlockSpec(memory_space=pl.ANY)
     vmem = pl.BlockSpec(memory_space=pltpu.VMEM)
-    rows_low = jax.ShapeDtypeStruct((row_count, width), LOW)
 
     def shape(*dims, dtype=LOW):
         return jax.ShapeDtypeStruct(dims, dtype)
 
-    kernel = functools.partial(
-        forward_kernel, steps, per_seq, bits, waves, feed_orders, three_order
-    )
+    rows_low, turned_low = shape(row_count, width), shape(width, row_count)
+    low = functools.partial(pltpu.VMEM, dtype=LOW)
     out = pl.pallas_call(
-        kernel,
+        functools.partial(forward_kernel, steps, per_seq, bits),
         grid=(2 * steps,),
         in_specs=[in_rows] + [vmem] * 6 + [any_spec] * 2 + [vmem],
-        out_specs=[first] * 4 + [second] * 6
+        out_specs=[first_turned] + [first] * 3 + [second] * 4 + [second_turned, second]
         + [
             pl.BlockSpec((1, HD, width), lambda i: (jnp.maximum(i - steps, 0), 0, 0)),
             pl.BlockSpec((1, width), lambda i: (0, 0)),
         ]
         + [any_spec] * 4,
-        out_shape=[rows_low] * 9
+        out_shape=[turned_low] + [rows_low] * 7 + [turned_low]
         + [
             shape(row_count, width, dtype=WIDE),
             shape(steps, HD, width),
             shape(1, width, dtype=WIDE),
-            shape(*lead, slab, 5 * width + 128),
+            shape(*lead, slab, columns),
             shape(*lead, slab, hidden),
             shape(*lead, slab, hidden),
             shape(*lead[:-1], 2 * deep, width),
         ],
         scratch_shapes=[
-            pltpu.VMEM(lead + (slab, 5 * width + 128), LOW),
-            pltpu.VMEM((row_count, width), LOW),
-            pltpu.VMEM((row_count, width), LOW),
-            pltpu.VMEM((row_count, width), LOW),
+            low(lead + (slab, columns)),
+            low((row_count, width)),
+            low((row_count, width)),
+            low((row_count, width)),
             pltpu.VMEM((seq_count, HD, width), WIDE),
-            pltpu.VMEM((seq_count, HD, width), LOW),
-            pltpu.VMEM((seq_count, HD, width), LOW),
+            low((seq_count, HD, width)),
+            low((seq_count, HD, width)),
             pltpu.VMEM((HD, width), WIDE),
             pltpu.VMEM((deep, width), WIDE),
-            pltpu.VMEM((2 * deep, width), LOW),
+            pltpu.VMEM((deep, width), WIDE),
+            low((2 * deep, width)),
             pltpu.SemaphoreType.DMA((FORWARD_COPIES,)),
             pltpu.SemaphoreType.DMA((FORWARD_COPIES,)),
-            pltpu.SemaphoreType.DMA((4,)),
+            pltpu.SemaphoreType.DMA((5,)),
         ],
         compiler_params=pltpu.CompilerParams(
             dimension_semantics=("arbitrary",),
@@ -671,9 +1314,9 @@
         cost_estimate=pl.CostEstimate(
             flops=16 * row_count * width * width, bytes_accessed=64 << 20, transcendentals=0
         ),
-    )(tok, *shards_attn, gain_columns, s_one, s_two, s_three.astype(WIDE))
+    )(tok, *shards_attn, gain_columns, s_one, s_two, s_three)
     return list(out[:12]) + [
-        out[12].reshape(-1, 5 * width + 128),
+        out[12].reshape(-1, columns),
         out[13].reshape(-1, hidden),
         out[14].reshape(-1, hidden),
         out[15].reshape(-1, width),
@@ -702,7 +1345,6 @@
     orders = stream_orders()
     tok = tokens.reshape(row_count, width)
     cot = cotangent.reshape(row_count, width)
-    limits = lengths - lax.axis_index("fsdp") * local_length
     full_key = gather_rows(w_key, orders[0])
     full_value = gather_rows(w_value, orders[1])
     full_query = gather_rows(w_query, orders[2])
@@ -750,18 +1392,20 @@
     )
     (
         layer_out, normed_two, glu, grad_up_one, grad_up_two, upstream_low, grad_residual,
-        grad_residual_low, grad_pre_gate, grad_attended, grad_totals, grad_gain_term,
+        gated, grad_attended, grad_totals, grad_gain_term,
     ) = call(
-        lambda *refs: feed_kernel(per_seq, *refs),
+        lambda *refs: feed_kernel(per_seq, False, *refs),
         steps,
-        [(limits, pl.BlockSpec(memory_space=pltpu.SMEM)), (residual, rows), (cot, rows),
+        [(lengths, pl.BlockSpec(memory_space=pltpu.SMEM)), (residual, rows), (cot, rows),
          (full_one, whole_spec(full_one)), (full_two, whole_spec(full_two)),
          (full_three, whole_spec(full_three)), (full_out, whole_spec(full_out)),
          (gain, whole_spec(gain)), (pre_gate, rows), (attended, rows), (queries, rows)],
-        [narrow, narrow, big, big, big, narrow, wide, narrow, narrow, narrow, state,
+        [narrow, narrow, big, big, big, narrow, wide,
+         ((row_count, 2 * width), LOW, rows_spec(2 * width)), narrow, state,
          ((1, width), WIDE, pl.BlockSpec((1, width), lambda i: (0, 0)))],
         flops=12 * row_count * width * hidden + square,
     )
+    grad_residual_low, grad_pre_gate = gated[:, :width], gated[:, width:]
     outgoing = shift_sum(grad_totals, "fsdp", True)
     grad_one = scatter_rows(dot_tn(normed_two, grad_up_one), orders[1])
     grad_two = scatter_rows(dot_tn(normed_two, grad_up_two), orders[2])
@@ -815,6 +1459,40 @@
         grad_one,
         grad_two,
         grad_three,
+    )
+
+
+def feed(
+    seq_count, lengths, residual, cot, full_one, full_two, full_three, full_attn, gain, pre_gate,
+    attended, queries,
+):
+    row_count, width = residual.shape
+    hidden = full_one.shape[1]
+    steps = row_count // BLOCK
+    per_seq = steps // seq_count
+    rows = rows_spec(width)
+    narrow = ((row_count, width), LOW, rows)
+    wide = ((row_count, width), WIDE, rows)
+    big = ((row_count, hidden), LOW, rows_spec(hidden))
+
+    def turned(size):
+        return ((size, row_count), LOW, pl.BlockSpec((size, BLOCK), lambda i: (0, i)))
+
+    state_spec = pl.BlockSpec((1, HD, width), lambda i: (i // per_seq, 0, 0))
+    out_part = pl.BlockSpec((width, width), lambda i: (0, 4), pipeline_mode=pl.Buffered(1))
+    return call(
+        lambda *refs: feed_kernel(per_seq, True, *refs),
+        steps,
+        [(lengths, pl.BlockSpec(memory_space=pltpu.SMEM)), (residual, rows), (cot, rows),
+         (full_one, whole_spec(full_one)), (full_two, whole_spec(full_two)),
+         (full_three, whole_spec(full_three)), (full_attn, out_part),
+         (gain, whole_spec(gain)), (pre_gate, rows), (attended, rows), (queries, rows)],
+        [narrow, turned(width), turned(hidden), big, big, narrow, wide,
+         ((row_count, 2 * width), LOW, rows_spec(2 * width)), narrow,
+         ((seq_count, HD, width), WIDE, state_spec),
+         ((1, width), WIDE, pl.BlockSpec((1, width), lambda i: (0, 0)))],
+        scratch=[pltpu.VMEM((BLOCK, hidden), LOW)],
+        flops=12 * row_count * width * hidden + 2 * row_count * width * width,
     )
 
 
@@ -834,22 +1512,9 @@
 ):
     seq_count, local_length, width = tokens.shape
     row_count = seq_count * local_length
-    hidden = w_one.shape[1]
-    steps = row_count // BLOCK
-    per_seq = local_length // BLOCK
-    orders = stream_orders()
     tok = tokens.reshape(row_count, width)
     cot = cotangent.reshape(row_count, width)
-    limits = lengths - lax.axis_index("fsdp") * local_length
     gain_columns = jnp.broadcast_to(out_gain[:, None], (out_gain.shape[0], 128))
-    rows = rows_spec(width)
-    narrow = ((row_count, width), LOW, rows)
-    wide = ((row_count, width), WIDE, rows)
-    big = ((row_count, hidden), LOW, rows_spec(hidden))
-    state_spec = pl.BlockSpec((1, HD, width), lambda i: (i // per_seq, 0, 0))
-    state = ((seq_count, HD, width), WIDE, state_spec)
-    square = 2 * row_count * width * width
-
     (
         normed_low, pre_key, keys, values, pre_query, queries, pre_gate, attended, mixed,
         residual, prefix, gain, full_attn, full_one, full_two, full_three,
@@ -857,62 +1522,23 @@
         tok, seq_count, (w_key, w_value, w_query, w_gate, w_out), gain_columns, w_one, w_two, w_three
     )
 
-    def part(n):
-        return pl.BlockSpec((width, width), lambda i: (0, n), pipeline_mode=pl.Buffered(1))
-
     (
         layer_out, normed_two, glu, grad_up_one, grad_up_two, upstream_low, grad_residual,
-        grad_residual_low, grad_pre_gate, grad_attended, grad_totals, grad_gain_term,
-    ) = call(
-        lambda *refs: feed_kernel(per_seq, *refs),
-        steps,
-        [(limits, pl.BlockSpec(memory_space=pltpu.SMEM)), (residual, rows), (cot, rows),
-         (full_one, whole_spec(full_one)), (full_two, whole_spec(full_two)),
-         (full_three, whole_spec(full_three)), (full_attn, part(4)),
-         (gain, whole_spec(gain)), (pre_gate, rows), (attended, rows), (queries, rows)],
-        [narrow, narrow, big, big, big, narrow, wide, narrow, narrow, narrow, state,
-         ((1, width), WIDE, pl.BlockSpec((1, width), lambda i: (0, 0)))],
-        flops=12 * row_count * width * hidden + square,
-    )
-    outgoing = shift_sum(grad_totals, "fsdp", True)
-    grad_one = scatter_rows(dot_tn(normed_two, grad_up_one), orders[1])
-    grad_two = scatter_rows(dot_tn(normed_two, grad_up_two), orders[2])
-    grad_three = scatter_rows(dot_tn(glu, upstream_low), orders[0])
-    gain_term = jnp.broadcast_to(grad_gain_term.reshape(width, 1), (width, 128))
-    grad_out = scatter_rows(
-        jnp.concatenate([dot_tn(mixed, grad_residual_low), gain_term], axis=1), orders[1]
-    )
-    grad_gain = grad_out[:, width]
-    grad_out = grad_out[:, :width]
-
-    def back(i):
-        return (i // per_seq) * per_seq + per_seq - 1 - i % per_seq
-
-    back_rows = rows_spec(width, order=back)
-    back_narrow = ((row_count, width), LOW, back_rows)
-    grad_pre_query, grad_pre_key, grad_pre_value = call(
-        lambda *refs: attend_back_kernel(per_seq, *refs),
-        steps,
-        [(queries, back_rows), (keys, back_rows), (values, back_rows),
-         (grad_attended, back_rows), (pre_query, back_rows), (pre_key, back_rows),
-         (prefix, pl.BlockSpec((1, HD, width), lambda i: (back(i), 0, 0))),
-         (outgoing, state_spec)],
-        [back_narrow, back_narrow, back_narrow],
-        scratch=[pltpu.VMEM((HD, width), WIDE)],
-        flops=6 * square,
-    )
-    grad_query = scatter_rows(dot_tn(normed_low, grad_pre_query), orders[0])
-    grad_key = scatter_rows(dot_tn(normed_low, grad_pre_key), orders[1])
-    grad_value = scatter_rows(dot_tn(normed_low, grad_pre_value), orders[2])
-    grad_gate = scatter_rows(dot_tn(normed_low, grad_pre_gate), orders[0])
-    (input_grad,) = call(
-        input_kernel,
-        steps,
-        [(grad_pre_query, rows), (grad_pre_key, rows), (grad_pre_value, rows),
-         (grad_pre_gate, rows), (full_attn, part(2)), (full_attn, part(0)),
-         (full_attn, part(1)), (full_attn, part(3)), (tok, rows), (grad_residual, rows)],
-        [wide],
-        flops=4 * square,
+        gated, grad_attended, grad_totals, grad_gain_term,
+    ) = feed(
+        seq_count, lengths, residual, cot, full_one, full_two, full_three, full_attn, gain,
+        pre_gate, attended, queries,
+    )
+    grad_one, grad_two, grad_three, grad_three_pre = feed_back(
+        seq_count, normed_two, grad_up_one, grad_up_two, glu, upstream_low, queries, keys, values,
+        grad_attended, pre_query, pre_key, prefix, grad_totals,
+    )
+    grads, input_grad = attend_weights(
+        normed_low, mixed, gated, grad_three_pre, grad_gain_term, full_attn, tok, grad_residual
+    )
+    grad_out, grad_gain = grads[:, :width], grads[:, width]
+    grad_gate, grad_query, grad_key, grad_value = (
+        grads[:, 128 + n * width : 128 + (n + 1) * width] for n in range(1, 5)
     )
     return (
         layer_out.reshape(tokens.shape),

time: 619 us -> 457 us (0.74)
  Pallas kernels: 316 us -> 434 us
  waiting for transfers between devices: 109 us -> 0 us
  matrix products: 85 us -> 0 us
  starting transfers between devices: 42.8 us -> 0 us
  other arithmetic: 25.9 us -> 0 us
  local copies, waits for them, and re-layouts: 33.3 us -> 15.4 us
    pallas_call x1 -> x3, Pallas kernels: 150 us -> 332 us  [the longest x1 147 us: forward(): pl.pallas_call(functools.partial(forward_kernel, steps, per_seq, bits), g...]
    ppermute x41 -> x0, waiting for transfers between devices: 109 us -> none  [the longest x40 109 us: scatter_rows(): come = lax.ppermute(send, axis, perm)]
    dot_general x8 -> x0, matrix products: 85 us -> none  [dot_tn(): lax.dot_general(a, b, (((0,), (0,)), ((), ())), preferred_element_type=WIDE)]
    pallas_call x3 -> x1, Pallas kernels: 166 us -> 102 us  [call(): pl.pallas_call(kernel, grid=(steps,), in_specs=[spec for _, spec in opera...]
    ppermute x41 -> x0, starting transfers between devices: 42.8 us -> none  [the longest x40 41.5 us: scatter_rows(): come = lax.ppermute(send, axis, perm)]
    dynamic_slice x11 -> x0, local copies, waits for them, and re-layouts: 27.3 us -> none  [the longest x4 15.7 us: scatter_rows(): keep = lax.dynamic_index_in_dim(data, own, place, keepdims=False)]
    convert_element_type x35 -> x0, other arithmetic: 18.6 us -> none  [the longest x32 16 us: scatter_rows(): data = data.astype(jnp.bfloat16)]
    unnamed x42 -> x10, local copies, waits for them, and re-layouts: 1.91 us -> 10.7 us
  transfers between devices with their start and end apart: 41 -> 0, of which waited for: 24 -> 0; matrix products, arithmetic and copies ran while one was open for 18% -> 0% of each run, Pallas kernels for 10% -> 0%
where the time goes in v4:
time: 457 us; the launch traced here: 451 us
  Pallas kernels  434 us (95%)
  local copies, waits for them, and re-layouts  15.4 us (3%)
    pallas_call x1, Pallas kernels, forward(): pl.pallas_call(functools.partial(forward_kernel, steps, per_seq, bits), g...  147 us
    pallas_call x1, Pallas kernels, feed_back(): pl.pallas_call(functools.partial(feed_back_kernel, per_seq, bits), grid=(...  113 us
    pallas_call x1, Pallas kernels, call(): pl.pallas_call(kernel, grid=(steps,), in_specs=[spec for _, spec in opera...  102 us
    pallas_call x1, Pallas kernels, attend_weights(): pl.pallas_call(functools.partial(attend_weights_kernel, bits), grid=(chun...  72.4 us
    unnamed x10, local copies, waits for them, and re-layouts  10.7 us

profile of v4, /device:TPU:0, one launch (start us, length us, event | category | flops | bytes accessed | tf_op | source)
XLA Modules:
  0.0 450.7 jit_solution(6654983352069090839)
XLA Ops:
  0.6 1.3 broadcast_in_dim.2.s_gain
  2.0 146.6 %shard_map.203 = (bf16[1024,2048]{1,0:T(8,128)(2,1)}, bf16[2048,1024]{1,0:T(8,128)(2,1)}, bf16[2048,1024]{1,0:T(8,128)(2,1)}, bf16[2048,1024]{1,0:T(8,128)(2,1)}...) custom-call(bf16[2048,1024]{1,0:T(8,128)(2,1)} %bitcast.10, ...), custom_call_target="tpu_custom_call" | custom-call | flops 34359738368 | bytes 67108864 | tf_op jit(solution)/shard_map/pallas_call | solution.py:1272
  148.5 102.1 %shard_map.204 = (bf16[2048,1024]{1,0:T(8,128)(2,1)}, bf16[1024,2048]{1,0:T(8,128)(2,1)}, bf16[2816,2048]{1,0:T(8,128)(2,1)}, bf16[2048,2816]{1,0:T(8,128)(2,1)}...) custom-call(s32[2]{0:T(128)} %refs_0_.1, ...), custom_call_target="tpu_custom_call" | custom-call | flops 75161927680 | bytes 53219336 | tf_op jit(solution)/shard_map/pallas_call | solution.py:323
  250.6 113.2 %shard_map.205 = (f32[32,2816]{1,0:T(8,128)}, f32[32,2816]{1,0:T(8,128)}, f32[88,1024]{1,0:T(8,128)}, bf16[2048,3072]{1,0:T(8,128)(2,1)}) custom-call(bf16[1024,2048]{1,0:T(8,128)(2,1)} %get-tuple-element.57.normed_hbm, bf16[2048,2816]{1,0:T(8,128)(2,1)} %get-tuple-element.58.grad_one, bf16[2048,2816]{1,0:T(8,128)(2,1)} %get-tuple-element.59.grad_two, ...), custom_call_target="tpu_custom_call" | custom-call | flops 61203283968 | bytes 134217728 | tf_op jit(solution)/shard_map/pallas_call | solution.py:827
  363.8 72.4 %shard_map.206 = (f32[32,5248]{1,0:T(8,128)}, f32[2048,1024]{1,0:T(8,128)}) custom-call(bf16[1024,2048]{1,0:T(8,128)(2,1)} %get-tuple-element.54.normed_hbm, bf16[1024,2048]{1,0:T(8,128)(2,1)} %get-tuple-element.55.mixed_hbm, bf16[2048,2048]{1,0:T(8,128)(2,1)} %get-tuple-element.56.gated.rows_gate, bf16[2048,3072]{1,0:T(8,128)(2,1)} %get-tuple-element.69.grads.rows_three, ...), custom_call_target="tpu_custom_call" | custom-call | flops 38654705664 | bytes 67108864 | tf_op jit(solution)/shard_map/pallas_call | solution.py:1017
  436.2 1.3 slice_reduce_fusion
  437.5 2.0 fusion
  439.5 0.0 copy-start.2
  439.5 0.0 copy-start.1
  439.5 0.0 copy-start
  439.5 8.5 %copy.27 = f32[2,1024,1024]{2,1,0:T(8,128)} copy(f32[2,1024,1024]{2,1,0:T(8,128)} %bitcast.8) | data formatting | bytes 16777216
  448.1 0.0 copy-done.2
  448.1 0.7 copy.28
  448.8 0.0 copy-done.1
  448.8 0.7 copy.29
  449.5 0.0 copy-done
  449.6 0.7 copy.30
Async XLA Ops:
  439.5 8.5 %copy-start.2 = (f32[32,2816]{1,0:T(8,128)S(1)}, f32[32,2816]{1,0:T(8,128)}, u32[]{:S(2)}) copy-start(f32[32,2816]{1,0:T(8,128)} %get-tuple-element.101) | copy-start | bytes 1081348
  439.5 9.3 %copy-start.1 = (f32[32,2816]{1,0:T(8,128)S(1)}, f32[32,2816]{1,0:T(8,128)}, u32[]{:S(2)}) copy-start(f32[32,2816]{1,0:T(8,128)} %get-tuple-element.102) | copy-start | bytes 1081348
  439.5 10.0 %copy-start = (f32[88,1024]{1,0:T(8,128)S(1)}, f32[88,1024]{1,0:T(8,128)}, u32[]{:S(2)}) copy-start(f32[88,1024]{1,0:T(8,128)} %get-tuple-element.103) | copy-start | bytes 1081348

commit v5 on v4

--- a/solution.py
+++ b/solution.py
@@ -523,78 +523,110 @@
 
 FORWARD_PLAN = (
     (0, (
-        ("a00", 0), ("a01", 0), ("a11", 0), ("f5", 0), ("f0", 0), ("f4", 0), ("a02", 0),
-        ("a00", 1), ("a01", 1), ("a10", 0), ("a12", 0), ("a02", 1), ("a00", 2), ("a11", 1),
-        ("a01", 2), ("a12", 1), ("a02", 2), ("a11", 2), ("a20", 0), ("a12", 2), ("a21", 0),
-        ("a10", 1), ("a22", 0), ("a20", 1), ("a00", 3), ("a21", 1), ("f1", 0), ("f3", 0),
-        ("a11", 3), ("a20", 2), ("a01", 3), ("a02", 3), ("f5", 1), ("a12", 3), ("a10", 2),
-        ("f1", 1), ("a22", 1), ("f3", 1), ("a11", 4), ("a00", 4), ("a21", 2),
+        ("a00", 0), ("f5", 0), ("a02", 0), ("a02", 1), ("a01", 0), ("f3", 0), ("f0", 0),
+        ("a00", 1), ("f5", 1), ("a22", 0), ("a10", 0), ("a01", 1), ("a21", 0), ("a02", 2),
+        ("a22", 1), ("a00", 2), ("a11", 0), ("a10", 1), ("a02", 3), ("a20", 0), ("a01", 2),
+        ("a20", 1), ("a12", 0), ("f1", 0), ("a21", 1), ("a12", 1), ("f2", 0), ("a10", 2),
+        ("a00", 3), ("a22", 2), ("a20", 2), ("a11", 1), ("a02", 4), ("a12", 2), ("a01", 3),
     )),
-    (1, (("a20", 3), ("a12", 4), ("f0", 1), ("f2", 0))),
-    (2, (("f1", 2),)),
-    (3, (("f5", 2),)),
-    (4, (("a22", 2),)),
-    (5, (("f3", 2),)),
-    (6, (("a20", 4), ("f2", 1))),
+    (1, (("a22", 3), ("a21", 2),)),
+    (2, (("a11", 2),)),
+    (3, (("a12", 3), ("f0", 1),)),
+    (4, (("a20", 3),)),
+    (5, (("a22", 4), ("f2", 1),)),
+    (6, (("f1", 1), ("a20", 4),)),
     (7, (("a21", 3),)),
-    (8, (("f0", 2), ("a22", 3), ("f1", 3), ("a10", 3), ("a21", 4))),
-    (9, (("f2", 2), ("f4", 1))),
-    (10, (("f5", 3), ("f2", 3))),
-    (11, (("f3", 3), ("f1", 4))),
-    (12, (("f0", 3),)),
-    (13, (("f4", 2),)),
-    (14, (("f2", 4), ("f5", 4))),
-    (16, (("f4", 3), ("f0", 4), ("f3", 4))),
+    (8, (("a11", 3), ("f3", 1), ("a12", 4), ("f4", 0), ("a10", 3),)),
+    (9, (("f0", 2), ("f2", 2),)),
+    (11, (("f1", 2), ("f4", 1),)),
+    (12, (("f3", 2),)),
+    (13, (("f5", 2),)),
+    (14, (("f0", 3),)),
+    (15, (("f2", 3),)),
+    (16, (("f1", 3), ("f3", 3),)),
+    (17, (("f4", 2),)),
+    (23, (("f4", 3), ("f5", 3),)),
 )
 FEED_BACK_PLAN = (
-    (7, (("one0", 0), ("two0", 0))),
-    (13, (("one0", 1), ("two0", 1))),
-    (15, (("three0", 0), ("three1", 0))),
-    (16, (("one0", 2),)),
-    (17, (("two0", 2),)),
-    (18, (("one1", 0), ("two1", 0), ("two0", 3))),
-    (20, (("one0", 3), ("one2", 0))),
-    (21, (("two2", 0), ("three1", 1), ("three0", 1))),
-    (24, (("one1", 1), ("two1", 1), ("one2", 1))),
-    (25, (("three1", 2), ("two2", 1), ("three0", 2))),
-    (26, (("one1", 2), ("three0", 3), ("one2", 2))),
-    (27, (
-        ("three1", 3), ("two1", 2), ("two2", 2), ("one2", 3), ("one1", 3), ("two1", 3),
-        ("two2", 3),
-    )),
+    (11, (("three0", 0),)),
+    (12, (("three1", 0),)),
+    (13, (("one0", 0),)),
+    (16, (("two0", 0),)),
+    (17, (("three0", 1), ("one1", 0), ("one0", 1),)),
+    (18, (("two1", 0),)),
+    (20, (("three1", 1), ("two0", 1),)),
+    (22, (("one0", 2), ("one2", 0),)),
+    (23, (("one1", 1), ("two2", 0),)),
+    (25, (("three1", 2), ("two1", 1),)),
+    (28, (("one1", 2), ("one2", 1), ("two0", 2),)),
+    (29, (("two2", 1), ("three0", 2),)),
+    (30, (("one1", 3),)),
+    (31, (("two1", 2), ("one2", 2), ("three1", 3),)),
+    (32, (("two2", 2), ("two0", 3), ("one0", 3), ("three0", 3),)),
+    (33, (("two1", 3),)),
+    (34, (("one2", 3), ("two2", 3),)),
 )
 ATTEND_BACK_PLAN = (
     (4, (("p0", 0),)),
-    (6, (("p1", 0), ("p2", 0))),
-    (9, (("p3", 0), ("p0", 1), ("p2", 1), ("p4", 0))),
-    (10, (("p5", 0),)),
-    (11, (("p1", 1), ("p6", 0))),
-    (12, (("p2", 2),)),
-    (14, (("p2", 3), ("p4", 1), ("p0", 2), ("p3", 1), ("p5", 1))),
-    (15, (("p1", 2), ("p6", 1))),
-    (16, (("p4", 2), ("p0", 3), ("p3", 2), ("p5", 2))),
-    (17, (("p4", 3), ("p1", 3), ("p6", 2))),
-    (18, (("p6", 3), ("p5", 3), ("p3", 3))),
+    (5, (("p1", 0), ("p2", 0),)),
+    (7, (("p3", 0),)),
+    (9, (("p4", 0),)),
+    (10, (("p5", 0), ("p0", 1),)),
+    (11, (("p2", 1), ("p1", 1), ("p6", 0),)),
+    (12, (("p0", 2), ("p3", 1),)),
+    (13, (("p4", 1),)),
+    (14, (("p1", 2), ("p5", 1), ("p2", 2),)),
+    (15, (("p6", 1), ("p3", 2), ("p2", 3),)),
+    (16, (("p1", 3), ("p5", 2), ("p3", 3),)),
+    (17, (("p6", 2), ("p4", 2),)),
+    (18, (("p0", 3), ("p5", 3), ("p6", 3), ("p4", 3),)),
 )
 
 
+HALF = BLOCK // 2
+
+
+def causal_pair(a, firsts, seconds, later):
+    row = lax.broadcasted_iota(jnp.int32, (HALF, HEADS * HALF), 0)
+    col = lax.broadcasted_iota(jnp.int32, (HALF, HEADS * HALF), 1) % HALF
+    if later:
+        mask = (row >= col).astype(WIDE)
+        full, part = dot_nt(a, firsts), dot_nt(a[HALF:], seconds)
+        full = [(full[:HALF] * mask).astype(LOW), full[HALF:].astype(LOW)]
+    else:
+        mask = (col >= row).astype(WIDE)
+        full, part = dot_nt(a, seconds), dot_nt(a[:HALF], firsts)
+        full = [full[:HALF].astype(LOW), (full[HALF:] * mask).astype(LOW)]
+    return jnp.concatenate(full, axis=0), (part * mask).astype(LOW)
+
+
+def causal_apply(scores, firsts, seconds, later, carried):
+    full, part = scores
+    if later:
+        total = dot_nn(full, firsts) + carried
+        return jnp.concatenate([total[:HALF], total[HALF:] + dot_nn(part, seconds)], axis=0)
+    total = dot_nn(full, seconds) + carried
+    return jnp.concatenate([total[:HALF] + dot_nn(part, firsts), total[HALF:]], axis=0)
+
+
 def attend_back_step(
-    same, queries, keys, values, grad_attended, pre_query, pre_key, prefix, grads, carry,
+    same, queries, keys, values, grad_attended, pre_query, pre_key, prefix, grads, carry, middle,
 ):
     marks = head_rows()
-    causal, causal_t = causal_masks()
     width = queries.shape[1]
     for g in groups(width):
+        if g.start == width // 2:
+            middle()
         q, k, v, ga = queries[:, g], keys[:, g], values[:, g], grad_attended[:, g]
-        qs, ks, vs, gs = (split_heads(rows, marks) for rows in (q, k, v, ga))
+        qs, ks, vs, gs = (
+            (split_heads(rows[:HALF], marks), split_heads(rows[HALF:], marks))
+            for rows in (q, k, v, ga)
+        )
         state = open_state(prefix[0, :, g].astype(WIDE), same)
         grad_state = open_state(carry[:, g], same)
-        grad_scores = (dot_nt(ga, vs) * causal).astype(LOW)
-        gq = dot_nn(grad_scores, ks) + dot_nt(ga, state)
-        grad_scores = (dot_nt(v, gs) * causal_t).astype(LOW)
-        gk = dot_nn(grad_scores, qs) + dot_nt(v, grad_state)
-        scores = (dot_nt(k, qs) * causal_t).astype(LOW)
-        gv = dot_nn(scores, gs) + dot_nn(k, grad_state)
+        gq = causal_apply(causal_pair(ga, *vs, True), *ks, True, dot_nt(ga, state))
+        gk = causal_apply(causal_pair(v, *gs, False), *qs, False, dot_nt(v, grad_state))
+        gv = causal_apply(causal_pair(k, *qs, False), *gs, False, dot_nn(k, grad_state))
         gq = gq * silu_slope(pre_query[:, g].astype(WIDE))
         gk = gk * silu_slope(pre_key[:, g].astype(WIDE))
         for n, grad in enumerate((gq, gk, gv)):
@@ -607,10 +639,10 @@
 
 
 CHUNK = 256
-PAIRS = (4, 4, 3)
-PAIR_ORDERS = (("0xy1", "y0x1"), ("xy10", "x0y1"), ("yx01", "yx01"))
-THREE_ORDERS = ("01y", "y01")
-THREE_AFTER = 1
+PAIRS = (3, 4, 4)
+PAIR_ORDERS = (("x01y", "x01y"), ("y0x1", "x0y1"), ("xy10", "yx01"))
+THREE_ORDERS = ("y10", "0y1")
+THREE_AFTER = 0
 
 
 def feed_back_blocks():
@@ -701,11 +733,12 @@
         greet(bits, far=False)
         state_out[...] = totals[...].astype(LOW)
         swap_state.start()
-        load[0].wait()
-
-    @pl.when(step == three_block[0])
-    def _():
-        load[1].wait()
+
+    for first_use, copy in ((pairs[0][0], load[0]), (three_block[0], load[1])):
+
+        @pl.when(step == first_use)
+        def _():
+            copy.wait()
 
     for n in range(2, len(PAIRS)):
 
@@ -714,13 +747,17 @@
             pieces[f"one{n - 2}"].core.wait_send()
             pieces[f"two{n - 2}"].core.wait_send()
 
+    later = planned(FEED_BACK_PLAN, pieces, base, base + 16)
+    at_start = {base + (at - base) // 2: todo for at, todo in later.items() if (at - base) % 2 == 0}
+    at_middle = {base + (at - base) // 2: todo for at, todo in later.items() if (at - base) % 2}
+
     @pl.when(step < base)
     def _():
         run_events(step, planned(FEED_BACK_PLAN, pieces, 0, base))
 
     @pl.when(step >= base)
     def _():
-        run_events(step, planned(FEED_BACK_PLAN, pieces, base, base + 8))
+        run_events(step, at_start)
 
     lead = acc.shape[:-1]
     fill = (slice(None),) * len(lead)
@@ -776,12 +813,12 @@
 
         attend_back_step(
             head_square(), queries, keys, values, grad_attended, pre_query, pre_key, prefix,
-            grads, carry,
+            grads, carry, lambda: run_events(step, at_middle),
         )
 
     @pl.when(step == pl.num_programs(0) - 1)
     def _():
-        for actions in planned(FEED_BACK_PLAN, pieces, base + 8, 1000).values():
+        for actions in planned(FEED_BACK_PLAN, pieces, base + 16, 1000).values():
             for action in actions:
                 action()
         for piece, out, begin in ends:
@@ -886,8 +923,8 @@
 
 
 WIDE_CHUNK = 512
-PARTS = (2, 2, 1, 2, 1, 1, 1)
-PART_ORDERS = ("01xy", "y01x", "x0y1", "xy01", "y0x1", "yx10", "x0y1")
+PARTS = (1, 2, 1, 1, 2, 1, 2)
+PART_ORDERS = ("yx10", "yx01", "0xy1", "x0y1", "01xy", "yx01", "yx01")
 
 
 def attend_weights_kernel(
@@ -1022,7 +1059,7 @@
         out_specs=[vmem, rows(width)],
         out_shape=[
             jax.ShapeDtypeStruct((slab, columns), WIDE),
-            jax.ShapeDtypeStruct((row_count, width), WIDE),
+            jax.ShapeDtypeStruct((row_count, width), LOW),
         ],
         scratch_shapes=[
             low((width, row_count)),
@@ -1053,15 +1090,15 @@
 
 
 ATTEND_PIECES = (
-    (("a00", "10yx", 6), ("a01", "zxy", 5), ("a02", "zyx", 5)),
-    (("a10", "zyx", 9), ("a11", "x10y", 4), ("a12", "10xy", 3)),
-    (("a20", "10xy", 4), ("a21", "10yx", 2), ("a22", "zyx", 3)),
+    (("a00", "zxy", 7), ("a01", "zyx", 6), ("a02", "1yx0", 3)),
+    (("a10", "zxy", 6), ("a11", "zxy", 7), ("a12", "1xy0", 3)),
+    (("a20", "1y0x", 1), ("a21", "zyx", 7), ("a22", "y1x0", 1)),
 )
 FEED_PIECES = (
-    (("f0", "y10x", 13), ("f1", "10yx", 9)),
-    (("f2", "10yx", 7), ("f3", "1xy0", 15)),
+    (("f0", "yzx", 6), ("f1", "zyx", 16)),
+    (("f2", "zxy", 11), ("f3", "xzy", 11)),
 )
-THREE_PIECES = (("f4", "zy", 3), ("f5", "10y", 5))
+THREE_PIECES = (("f4", "zy", 4), ("f5", "yz", 4))
 FORWARD_COPIES = 128
 
 
@@ -1095,8 +1132,8 @@
     steps, per_seq, bits,
     tok, s_key, s_value, s_query, s_gate, s_out, s_gain, s_one, s_two, s_three,
     normed, pre_key, keys, values, pre_query, queries, pre_gate, attended, mixed, residual,
-    prefix, gain_row, full_attn, full_one, full_two, full_three,
-    held, all_keys, all_values, all_normed, totals, state_out, state_in, carry,
+    normed_two, up_one, up_two, glu, prefix, gain_row, full_attn, full_one, full_two, full_three,
+    held, held_one, held_two, all_keys, all_values, all_normed, totals, state_out, state_in, carry,
     three_out, three_in, three_slab, send, recv, local,
 ):
     step = pl.program_id(0)
@@ -1113,14 +1150,14 @@
             pieces[name] = Gather(held, bits, order, sems, cols)
             waves[-1].append(pieces[name])
     feed = []
-    for buf, parts in zip((full_one, full_two), FEED_PIECES):
+    for buf, parts in zip((held_one, held_two), FEED_PIECES):
         start = 0
         for name, order, tiles in parts:
             cols = slice(start, start + 128 * tiles)
             start += 128 * tiles
             pieces[name] = Gather(buf, bits, order, sems, cols)
             feed.append(pieces[name])
-    start = 0
+    start, threes = 0, []
     for n, (name, order, tiles) in enumerate(THREE_PIECES):
         cols = slice(start, start + 128 * tiles)
         start += 128 * tiles
@@ -1128,21 +1165,31 @@
         pieces[name].first_swap(
             sems, cols, three_out, three_in, three_slab, full_three.at[own[:-1]], local.at[2 + n]
         )
-        feed.append(pieces[name])
+        threes.append(pieces[name])
     swap_state = sems.copy(state_out, state_in, (SIDE,))
     keep_attn = pltpu.make_async_copy(held, full_attn, local.at[4])
+    keep_feed = [
+        pltpu.make_async_copy(held_one, full_one, local.at[0]),
+        pltpu.make_async_copy(held_two, full_two, local.at[1]),
+    ]
 
     @pl.when(step == 0)
     def _():
         place = [
-            pltpu.make_async_copy(s_one, full_one.at[own], local.at[0]),
-            pltpu.make_async_copy(s_two, full_two.at[own], local.at[1]),
+            pltpu.make_async_copy(s_one, held_one.at[own], local.at[0]),
+            pltpu.make_async_copy(s_two, held_two.at[own], local.at[1]),
         ]
         for copy in place:
             copy.start()
         for n, shard in enumerate((s_key, s_value, s_query, s_gate, s_out)):
             held[own + (slice(None), slice(n * width, (n + 1) * width))] = shard[...]
-        held[own + (slice(None), slice(5 * width, 5 * width + 128))] = s_gain[...]
+        size = s_gain.shape[1]
+        row = lax.broadcasted_iota(jnp.int32, (size, size), 0)
+        col = lax.broadcasted_iota(jnp.int32, (size, size), 1)
+        spread = jnp.broadcast_to(s_gain[...].astype(WIDE), (size, size))
+        column = jnp.sum(jnp.where(row == col, spread, 0.0), axis=1, keepdims=True)
+        column = jnp.broadcast_to(column, (size, 128)).astype(LOW)
+        held[own + (slice(None), slice(5 * width, 5 * width + 128))] = column
         three_out[...] = s_three[...].astype(WIDE)
         greet(bits)
         for copy in place:
@@ -1162,7 +1209,19 @@
         column = held[..., 5 * width : 5 * width + 128].reshape(width, 128)
         gain_row[...] = column.astype(WIDE).T[:1]
 
-    run_events(step + 1, planned(FORWARD_PLAN, pieces, 1, 2 * steps + 1))
+    for n in range(3):
+
+        @pl.when((step >= n * steps) & (step < (n + 1) * steps))
+        def _():
+            part = planned(FORWARD_PLAN, pieces, n * steps + 1, (n + 1) * steps + 1)
+            run_events(step + 1, part)
+
+    @pl.when(step == 2 * steps)
+    def _():
+        for piece in feed:
+            piece.finish()
+        for copy in keep_feed:
+            copy.start()
 
     def weight(n):
         return held[..., n * width : (n + 1) * width].reshape(width, width)
@@ -1198,7 +1257,7 @@
         state_out[...] = totals[...].astype(LOW)
         swap_state.start()
 
-    @pl.when(step >= steps)
+    @pl.when((step >= steps) & (step < 2 * steps))
     def _():
         at = step - steps
         here = pl.ds(pl.multiple_of(at * BLOCK, BLOCK), BLOCK)
@@ -1218,35 +1277,54 @@
             carry[...] = state_in[at // per_seq].astype(WIDE) * side
 
         marks = head_rows()
-        causal, _ = causal_masks()
         prefix[0] = carry[...].astype(LOW)
         for g in groups(width):
             q, k, v = queries[:, g], all_keys[here, g], all_values[here, g]
-            scores = (dot_nt(q, split_heads(k, marks)) * causal).astype(LOW)
-            out = dot_nn(scores, split_heads(v, marks))
-            out += dot_nn(q, open_state(carry[:, g], same))
+            ks, vs = (
+                (split_heads(part[:HALF], marks), split_heads(part[HALF:], marks))
+                for part in (k, v)
+            )
+            carried = dot_nn(q, open_state(carry[:, g], same))
+            out = causal_apply(causal_pair(q, *ks, True), *vs, True, carried)
             attended[:, g] = out.astype(LOW)
             carry[:, g] += pack_state(dot_tn(k, v), same)
         rows = attended[...].astype(WIDE)
         rows = rows * rms_scale(rows) * gain_row[...] * jax.nn.sigmoid(gate)
         rows = rows.astype(LOW)
         mixed[...] = rows.T
-        residual[...] = tok[...].astype(WIDE) + dot_nn(rows, weight(4))
-
-    @pl.when(step == 2 * steps - 1)
-    def _():
-        for actions in planned(FORWARD_PLAN, pieces, 2 * steps + 1, 1000).values():
+        res = tok[...].astype(WIDE) + dot_nn(rows, weight(4))
+        residual[...] = res
+        rows = (res * rms_scale(res)).astype(LOW)
+        all_normed[here, :] = rows
+        normed_two[...] = rows.T
+
+    @pl.when(step >= 2 * steps)
+    def _():
+        here = pl.ds(pl.multiple_of((step - 2 * steps) * BLOCK, BLOCK), BLOCK)
+        rows = all_normed[here, :]
+        for c in groups(up_one.shape[1]):
+            one = dot_nn(rows, held_one[..., c].reshape(width, GROUP))
+            two = dot_nn(rows, held_two[..., c].reshape(width, GROUP))
+            up_one[:, c] = one.astype(LOW)
+            up_two[:, c] = two.astype(LOW)
+            glu[c, :] = (one * two).astype(LOW).T
+
+    @pl.when(step == 3 * steps - 1)
+    def _():
+        for actions in planned(FORWARD_PLAN, pieces, 3 * steps + 1, 1000).values():
             for action in actions:
                 action()
-        for piece in feed:
+        for piece in threes:
             piece.finish()
         for piece in pieces.values():
             piece.drain()
         swap_state.wait_send()
         keep_attn.wait()
-
-
-def forward(tok, seq_count, shards_attn, gain_columns, s_one, s_two, s_three):
+        for copy in keep_feed:
+            copy.wait()
+
+
+def forward(tok, seq_count, shards_attn, gain_row, s_one, s_two, s_three):
     row_count, width = tok.shape
     hidden = s_one.shape[1]
     steps = row_count // BLOCK
@@ -1256,11 +1334,17 @@
     slab = s_one.shape[0]
     deep = s_three.shape[0]
     columns = 5 * width + 128
-    in_rows = pl.BlockSpec((BLOCK, width), lambda i: (i % steps, 0))
-    first = pl.BlockSpec((BLOCK, width), lambda i: (jnp.minimum(i, steps - 1), 0))
-    second = pl.BlockSpec((BLOCK, width), lambda i: (jnp.maximum(i - steps, 0), 0))
-    first_turned = pl.BlockSpec((width, BLOCK), lambda i: (0, jnp.minimum(i, steps - 1)))
-    second_turned = pl.BlockSpec((width, BLOCK), lambda i: (0, jnp.maximum(i - steps, 0)))
+
+    def phase(n):
+        return lambda i: clip(i - n * steps, 0, steps - 1)
+
+    in_rows = rows_spec(width, order=lambda i: jnp.where(i < steps, i, phase(1)(i)))
+    first, second = rows_spec(width, order=phase(0)), rows_spec(width, order=phase(1))
+    first_turned = pl.BlockSpec((width, BLOCK), lambda i: (0, phase(0)(i)))
+    second_turned = pl.BlockSpec((width, BLOCK), lambda i: (0, phase(1)(i)))
+    third = rows_spec(hidden, order=phase(2))
+    third_turned = pl.BlockSpec((hidden, BLOCK), lambda i: (0, phase(2)(i)))
+    big_low = jax.ShapeDtypeStruct((row_count, hidden), LOW)
     any_spec = pl.BlockSpec(memory_space=pl.ANY)
     vmem = pl.BlockSpec(memory_space=pltpu.VMEM)
 
@@ -1271,17 +1355,19 @@
     low = functools.partial(pltpu.VMEM, dtype=LOW)
     out = pl.pallas_call(
         functools.partial(forward_kernel, steps, per_seq, bits),
-        grid=(2 * steps,),
+        grid=(3 * steps,),
         in_specs=[in_rows] + [vmem] * 6 + [any_spec] * 2 + [vmem],
         out_specs=[first_turned] + [first] * 3 + [second] * 4 + [second_turned, second]
+        + [second_turned, third, third, third_turned]
         + [
-            pl.BlockSpec((1, HD, width), lambda i: (jnp.maximum(i - steps, 0), 0, 0)),
+            pl.BlockSpec((1, HD, width), lambda i: (phase(1)(i), 0, 0)),
             pl.BlockSpec((1, width), lambda i: (0, 0)),
         ]
         + [any_spec] * 4,
         out_shape=[turned_low] + [rows_low] * 7 + [turned_low]
         + [
             shape(row_count, width, dtype=WIDE),
+            turned_low, big_low, big_low, shape(hidden, row_count),
             shape(steps, HD, width),
             shape(1, width, dtype=WIDE),
             shape(*lead, slab, columns),
@@ -1291,6 +1377,8 @@
         ],
         scratch_shapes=[
             low(lead + (slab, columns)),
+            low(lead + (slab, hidden)),
+            low(lead + (slab, hidden)),
             low((row_count, width)),
             low((row_count, width)),
             low((row_count, width)),
@@ -1307,19 +1395,19 @@
         ],
         compiler_params=pltpu.CompilerParams(
             dimension_semantics=("arbitrary",),
-            vmem_limit_bytes=58 << 20,
+            vmem_limit_bytes=62 << 20,
             collective_id=1,
             has_side_effects=True,
         ),
         cost_estimate=pl.CostEstimate(
-            flops=16 * row_count * width * width, bytes_accessed=64 << 20, transcendentals=0
+            flops=28 * row_count * width * width, bytes_accessed=128 << 20, transcendentals=0
         ),
-    )(tok, *shards_attn, gain_columns, s_one, s_two, s_three)
-    return list(out[:12]) + [
-        out[12].reshape(-1, columns),
-        out[13].reshape(-1, hidden),
-        out[14].reshape(-1, hidden),
-        out[15].reshape(-1, width),
+    )(tok, *shards_attn, gain_row, s_one, s_two, s_three)
+    return list(out[:16]) + [
+        out[16].reshape(-1, columns),
+        out[17].reshape(-1, hidden),
+        out[18].reshape(-1, hidden),
+        out[19].reshape(-1, width),
     ]
 
 
@@ -1462,37 +1550,152 @@
     )
 
 
+def feed_step_kernel(
+    steps, per_seq, lengths, residual, cotangent, up_one, up_two, all_one, all_two, all_three,
+    all_attn, gain, pre_gate, attended, queries,
+    layer_out, grad_one, grad_two, upstream_low, grad_residual, gated, grad_attended,
+    totals, grad_gain, product, last_back, last_residual, last_upstream,
+    w_one, w_two, w_three, w_out, local,
+):
+    step = pl.program_id(0)
+    row_count, width = residual.shape
+
+    hidden = w_one.shape[1]
+    loads = {}
+    for n, part in enumerate((slice(0, 768), slice(768, 1792), slice(1792, hidden))):
+        loads[part.start] = pltpu.make_async_copy(
+            all_three.at[part], w_three.at[part], local.at[n]
+        )
+    later = [
+        pltpu.make_async_copy(all_one, w_one, local.at[3]),
+        pltpu.make_async_copy(all_two, w_two, local.at[4]),
+        pltpu.make_async_copy(all_attn.at[:, 4 * width : 5 * width], w_out, local.at[5]),
+    ]
+
+    def norm_part(rows):
+        res = last_residual[rows, :]
+        grad = last_upstream[rows, :].astype(WIDE)
+        grad += norm_back(res, rms_scale(res), last_back[rows, :])
+        grad_residual[rows, :] = grad
+        gated[rows, :width] = grad.astype(LOW)
+
+    def out_part():
+        last_back[...] = dot_nt(gated[:, :width], w_out[...])
+        grad_gain[...] = jnp.where(step == 1, 0.0, grad_gain[...])
+
+    def gate_part(rows):
+        grad = last_back[rows, :]
+        gate = jax.nn.sigmoid(pre_gate[rows, :].astype(WIDE))
+        att = attended[rows, :].astype(WIDE)
+        scale = rms_scale(att)
+        hat = att * scale
+        grad = grad * gate
+        grad_gain[...] += jnp.sum(grad * hat, axis=0, keepdims=True)
+        grad = grad * gain[...]
+        gated[rows, width:] = (grad * hat * (1.0 - gate)).astype(LOW)
+        grad_attended[rows, :] = norm_back(att, scale, grad).astype(LOW)
+
+    def state_part():
+        fresh = (step - 1) % per_seq == 0
+        same = head_square()
+        for g in groups(width):
+            term = pack_state(dot_tn(queries[:, g], grad_attended[:, g]), same)
+            totals[0, :, g] = jnp.where(fresh, 0.0, totals[0, :, g]) + term
+
+    def cut(count, n):
+        size = row_count // count
+        return slice(n * size, (n + 1) * size)
+
+    tail = [functools.partial(norm_part, cut(2, n)) for n in range(2)] + [out_part]
+    tail += [functools.partial(gate_part, cut(8, n)) for n in range(8)] + [state_part]
+
+    def begin(todo, loading=False):
+        spot = lax.broadcasted_iota(jnp.int32, (row_count, 1), 0) + (step % per_seq) * row_count
+        limit = lengths[step // per_seq] - lax.axis_index("fsdp") * per_seq * row_count
+        valid = (spot < limit).astype(WIDE)
+        up_low = (cotangent[...].astype(WIDE) * valid).astype(LOW)
+        upstream_low[...] = up_low
+        todo = list(todo)
+        for c in groups(hidden):
+            if loading and c.start in loads:
+                loads[c.start].wait()
+            back = dot_nt(up_low, w_three[c, :])
+            if todo:
+                todo.pop(0)()
+            one, two = up_one[:, c].astype(WIDE), up_two[:, c].astype(WIDE)
+            product[:, c] = (one * two).astype(LOW)
+            grad_one[:, c] = (back * two).astype(LOW)
+            grad_two[:, c] = (back * one).astype(LOW)
+        for part in todo:
+            part()
+        res = residual[...]
+        layer_out[...] = (valid * (res + dot_nn(product[...], w_three[...]))).astype(LOW)
+        if loading:
+            for copy in later:
+                copy.wait()
+        back = dot_nt(grad_one[...], w_one[...]) + dot_nt(grad_two[...], w_two[...])
+        last_back[...] = back
+        last_residual[...] = res
+        last_upstream[...] = up_low
+
+    @pl.when(step == 0)
+    def _():
+        for copy in list(loads.values()) + later:
+            copy.start()
+        begin([], loading=True)
+
+    @pl.when((step > 0) & (step < steps))
+    def _():
+        begin(tail)
+
+    @pl.when(step == steps)
+    def _():
+        for part in tail:
+            part()
+
+
 def feed(
-    seq_count, lengths, residual, cot, full_one, full_two, full_three, full_attn, gain, pre_gate,
-    attended, queries,
+    seq_count, lengths, residual, cot, up_one, up_two, full_one, full_two, full_three, full_attn,
+    gain, pre_gate, attended, queries,
 ):
     row_count, width = residual.shape
     hidden = full_one.shape[1]
     steps = row_count // BLOCK
     per_seq = steps // seq_count
-    rows = rows_spec(width)
+
+    def now(i):
+        return jnp.minimum(i, steps - 1)
+
+    def last(i):
+        return jnp.maximum(i - 1, 0)
+
+    rows = rows_spec(width, order=now)
+    done = rows_spec(width, order=last)
     narrow = ((row_count, width), LOW, rows)
-    wide = ((row_count, width), WIDE, rows)
-    big = ((row_count, hidden), LOW, rows_spec(hidden))
-
-    def turned(size):
-        return ((size, row_count), LOW, pl.BlockSpec((size, BLOCK), lambda i: (0, i)))
-
-    state_spec = pl.BlockSpec((1, HD, width), lambda i: (i // per_seq, 0, 0))
-    out_part = pl.BlockSpec((width, width), lambda i: (0, 4), pipeline_mode=pl.Buffered(1))
+    big = ((row_count, hidden), LOW, rows_spec(hidden, order=now))
+
+    state_spec = pl.BlockSpec((1, HD, width), lambda i: (last(i) // per_seq, 0, 0))
+    hbm = pl.BlockSpec(memory_space=pl.ANY)
     return call(
-        lambda *refs: feed_kernel(per_seq, True, *refs),
-        steps,
+        lambda *refs: feed_step_kernel(steps, per_seq, *refs),
+        steps + 1,
         [(lengths, pl.BlockSpec(memory_space=pltpu.SMEM)), (residual, rows), (cot, rows),
-         (full_one, whole_spec(full_one)), (full_two, whole_spec(full_two)),
-         (full_three, whole_spec(full_three)), (full_attn, out_part),
-         (gain, whole_spec(gain)), (pre_gate, rows), (attended, rows), (queries, rows)],
-        [narrow, turned(width), turned(hidden), big, big, narrow, wide,
-         ((row_count, 2 * width), LOW, rows_spec(2 * width)), narrow,
+         (up_one, big[2]), (up_two, big[2]),
+         (full_one, hbm), (full_two, hbm), (full_three, hbm), (full_attn, hbm),
+         (gain, whole_spec(gain)), (pre_gate, done), (attended, done), (queries, done)],
+        [narrow, big, big, narrow,
+         ((row_count, width), WIDE, done),
+         ((row_count, 2 * width), LOW, rows_spec(2 * width, order=last)),
+         ((row_count, width), LOW, done),
          ((seq_count, HD, width), WIDE, state_spec),
          ((1, width), WIDE, pl.BlockSpec((1, width), lambda i: (0, 0)))],
-        scratch=[pltpu.VMEM((BLOCK, hidden), LOW)],
-        flops=12 * row_count * width * hidden + 2 * row_count * width * width,
+        scratch=[pltpu.VMEM((BLOCK, hidden), LOW), pltpu.VMEM((BLOCK, width), WIDE),
+                 pltpu.VMEM((BLOCK, width), WIDE), pltpu.VMEM((BLOCK, width), LOW),
+                 pltpu.VMEM((width, hidden), LOW), pltpu.VMEM((width, hidden), LOW),
+                 pltpu.VMEM((hidden, width), LOW), pltpu.VMEM((width, width), LOW),
+                 pltpu.SemaphoreType.DMA((6,))],
+        flops=8 * row_count * width * hidden + 2 * row_count * width * width,
+        limit=60,
     )
 
 
@@ -1514,20 +1717,20 @@
     row_count = seq_count * local_length
     tok = tokens.reshape(row_count, width)
     cot = cotangent.reshape(row_count, width)
-    gain_columns = jnp.broadcast_to(out_gain[:, None], (out_gain.shape[0], 128))
     (
         normed_low, pre_key, keys, values, pre_query, queries, pre_gate, attended, mixed,
-        residual, prefix, gain, full_attn, full_one, full_two, full_three,
+        residual, normed_two, up_one, up_two, glu, prefix, gain, full_attn, full_one, full_two,
+        full_three,
     ) = forward(
-        tok, seq_count, (w_key, w_value, w_query, w_gate, w_out), gain_columns, w_one, w_two, w_three
+        tok, seq_count, (w_key, w_value, w_query, w_gate, w_out), out_gain[None, :], w_one, w_two, w_three
     )
 
     (
-        layer_out, normed_two, glu, grad_up_one, grad_up_two, upstream_low, grad_residual,
-        gated, grad_attended, grad_totals, grad_gain_term,
+        layer_out, grad_up_one, grad_up_two, upstream_low, grad_residual, gated,
+        grad_attended, grad_totals, grad_gain_term,
     ) = feed(
-        seq_count, lengths, residual, cot, full_one, full_two, full_three, full_attn, gain,
-        pre_gate, attended, queries,
+        seq_count, lengths, residual, cot, up_one, up_two, full_one, full_two, full_three,
+        full_attn, gain, pre_gate, attended, queries,
     )
     grad_one, grad_two, grad_three, grad_three_pre = feed_back(
         seq_count, normed_two, grad_up_one, grad_up_two, glu, upstream_low, queries, keys, values,
@@ -1542,7 +1745,7 @@
     )
     return (
         layer_out.reshape(tokens.shape),
-        input_grad.reshape(tokens.shape),
+        input_grad.astype(WIDE).reshape(tokens.shape),
         grad_query,
         grad_key,
         grad_value,

time: 457 us -> 425 us (0.930)
  Pallas kernels: 434 us -> 405 us
  local copies, waits for them, and re-layouts: 15.4 us -> 5.56 us
  other arithmetic: 0 us -> 6.72 us
    pallas_call x1, Pallas kernels: 102 us -> 73.2 us  [call(): pl.pallas_call(kernel, grid=(steps,), in_specs=[spec for _, spec in opera...]
    unnamed x10 -> x9, local copies, waits for them, and re-layouts: 10.7 us -> 2.22 us
    reshape x0 -> x1, other arithmetic: none -> 6.72 us  [fused_shards(): input_grad.astype(WIDE).reshape(tokens.shape)]
where the time goes in v5:
time: 425 us; the launch traced here: 418 us
  Pallas kernels  405 us (95%)
  other arithmetic  6.72 us (2%)
  local copies, waits for them, and re-layouts  5.56 us (1%)
    pallas_call x1, Pallas kernels, forward(): pl.pallas_call(functools.partial(forward_kernel, steps, per_seq, bits), g...  147 us
    pallas_call x1, Pallas kernels, feed_back(): pl.pallas_call(functools.partial(feed_back_kernel, per_seq, bits), grid=(...  110 us
    pallas_call x1, Pallas kernels, attend_weights(): pl.pallas_call(functools.partial(attend_weights_kernel, bits), grid=(chun...  74.3 us
    pallas_call x1, Pallas kernels, call(): pl.pallas_call(kernel, grid=(steps,), in_specs=[spec for _, spec in opera...  73.2 us

profile of v5, /device:TPU:0, one launch (start us, length us, event | category | flops | bytes accessed | tf_op | source)
XLA Modules:
  0.0 418.2 jit_solution(8654025378524246543)
XLA Ops:
  0.6 147.3 %shard_map.203 = (bf16[1024,2048]{1,0:T(8,128)(2,1)}, bf16[2048,1024]{1,0:T(8,128)(2,1)}, bf16[2048,1024]{1,0:T(8,128)(2,1)}, bf16[2048,1024]{1,0:T(8,128)(2,1)}...) custom-call(bf16[2048,1024]{1,0:T(8,128)(2,1)} %bitcast.12, ...), custom_call_target="tpu_custom_call" | custom-call | flops 60129542144 | bytes 134217728 | tf_op jit(solution)/shard_map/pallas_call | solution.py:1356
  148.0 73.2 %shard_map.204 = (bf16[2048,1024]{1,0:T(8,128)(2,1)}, bf16[2048,2816]{1,0:T(8,128)(2,1)}, bf16[2048,2816]{1,0:T(8,128)(2,1)}, bf16[2048,1024]{1,0:T(8,128)(2,1)}...) custom-call(s32[2]{0:T(128)} %refs_0_.1, ...), custom_call_target="tpu_custom_call" | custom-call | flops 51539607552 | bytes 76288008 | tf_op jit(solution)/shard_map/pallas_call | solution.py:323
  221.2 109.9 %shard_map.205 = (f32[32,2816]{1,0:T(8,128)}, f32[32,2816]{1,0:T(8,128)}, f32[88,1024]{1,0:T(8,128)}, bf16[2048,3072]{1,0:T(8,128)(2,1)}) custom-call(bf16[1024,2048]{1,0:T(8,128)(2,1)} %get-tuple-element.61.normed_hbm, bf16[2048,2816]{1,0:T(8,128)(2,1)} %get-tuple-element.62.grad_one, bf16[2048,2816]{1,0:T(8,128)(2,1)} %get-tuple-element.63.grad_two, ...), custom_call_target="tpu_custom_call" | custom-call | flops 61203283968 | bytes 134217728 | tf_op jit(solution)/shard_map/pallas_call | solution.py:864
  331.1 74.3 %shard_map.206 = (f32[32,5248]{1,0:T(8,128)}, bf16[2048,1024]{1,0:T(8,128)(2,1)}) custom-call(bf16[1024,2048]{1,0:T(8,128)(2,1)} %get-tuple-element.58.normed_hbm, bf16[1024,2048]{1,0:T(8,128)(2,1)} %get-tuple-element.59.mixed_hbm, bf16[2048,2048]{1,0:T(8,128)(2,1)} %get-tuple-element.60.gated.rows_gate, ...), custom_call_target="tpu_custom_call" | custom-call | flops 38654705664 | bytes 67108864 | tf_op jit(solution)/shard_map/pallas_call | solution.py:1054
  405.5 1.3 slice_reduce_fusion
  406.8 2.0 fusion
  408.8 0.0 copy-start.2
  408.8 0.0 copy-start.1
  408.8 0.0 copy-start
  408.8 6.7 %convert.1 = f32[2,1024,1024]{2,1,0:T(8,128)} convert(bf16[2,1024,1024]{2,1,0:T(8,128)(2,1)} %bitcast.10) | non-fusion elementwise | flops 2097152 | bytes 12582912 | tf_op jit(solution)/shard_map/reshape | solution.py:1748
  415.5 0.0 copy-done.2
  415.6 0.7 copy.26
  416.3 0.0 copy-done.1
  416.3 0.7 copy.27
  417.0 0.0 copy-done
  417.0 0.7 copy.28
Async XLA Ops:
  408.8 6.7 %copy-start.2 = (f32[32,2816]{1,0:T(8,128)S(1)}, f32[32,2816]{1,0:T(8,128)}, u32[]{:S(2)}) copy-start(f32[32,2816]{1,0:T(8,128)} %get-tuple-element.105) | copy-start | bytes 1081348
  408.8 7.5 %copy-start.1 = (f32[32,2816]{1,0:T(8,128)S(1)}, f32[32,2816]{1,0:T(8,128)}, u32[]{:S(2)}) copy-start(f32[32,2816]{1,0:T(8,128)} %get-tuple-element.106) | copy-start | bytes 1081348
  408.8 8.2 %copy-start = (f32[88,1024]{1,0:T(8,128)S(1)}, f32[88,1024]{1,0:T(8,128)}, u32[]{:S(2)}) copy-start(f32[88,1024]{1,0:T(8,128)} %get-tuple-element.107) | copy-start | bytes 1081348

commit v6 on v5

--- a/solution.py
+++ b/solution.py
@@ -445,12 +445,16 @@
 
 
 class Scatter:
-    def __init__(self, sems, bits, order, acc, send, come, recvs, columns, slots):
+    def __init__(
+        self, sems, bits, order, acc, send, come, recvs, columns, send_columns, come_columns
+    ):
         self.bits, self.order, self.acc, self.columns = bits, order, acc, columns
-        self.come, self.recvs, self.slots = come, recvs, slots
+        self.come, self.recvs, self.come_columns = come, recvs, come_columns
         rows = (slice(None),)
         full = (slice(None),) * len(bits) + rows
-        self.core = sems.copy(send.at[full + (slots,)], come.at[full + (slots,)], (CORE,))
+        self.core = sems.copy(
+            send.at[full + (send_columns,)], come.at[full + (come_columns,)], (CORE,)
+        )
         self.copies, self.done = [], []
         for k, name in enumerate(order):
             (bit,) = LINKS[name]
@@ -485,7 +489,7 @@
     def advance(self, k):
         if k == 0:
             self.core.wait_recv()
-            self.add([], self.come, self.slots)
+            self.add([], self.come, self.come_columns)
         else:
             self.copies[k - 1].wait_recv()
             self.add(self.done[k - 1] + [LINKS[self.order[k - 1]][0]], self.recvs[k - 1], self.columns)
@@ -523,63 +527,70 @@
 
 FORWARD_PLAN = (
     (0, (
-        ("a00", 0), ("f5", 0), ("a02", 0), ("a02", 1), ("a01", 0), ("f3", 0), ("f0", 0),
-        ("a00", 1), ("f5", 1), ("a22", 0), ("a10", 0), ("a01", 1), ("a21", 0), ("a02", 2),
-        ("a22", 1), ("a00", 2), ("a11", 0), ("a10", 1), ("a02", 3), ("a20", 0), ("a01", 2),
-        ("a20", 1), ("a12", 0), ("f1", 0), ("a21", 1), ("a12", 1), ("f2", 0), ("a10", 2),
-        ("a00", 3), ("a22", 2), ("a20", 2), ("a11", 1), ("a02", 4), ("a12", 2), ("a01", 3),
+        ("a00", 0), ("a02", 0), ("f5", 0), ("f4", 0), ("a01", 0), ("a00", 1), ("f5", 1),
+        ("a02", 1), ("a01", 1), ("a20", 0), ("a00", 2), ("a22", 0), ("a21", 0), ("a02", 2),
+        ("a12", 0), ("a11", 0), ("a10", 0), ("a01", 2), ("a20", 1), ("a02", 3), ("a21", 1),
+        ("a12", 1), ("a00", 3), ("a01", 3), ("a11", 1), ("a10", 1), ("a22", 1), ("a21", 2),
+        ("a20", 2), ("a12", 2), ("a02", 4), ("f2", 0), ("f0", 0), ("a11", 2), ("a10", 2),
+        ("a00", 4), ("a01", 4), ("a21", 3), ("a20", 3),
     )),
-    (1, (("a22", 3), ("a21", 2),)),
-    (2, (("a11", 2),)),
-    (3, (("a12", 3), ("f0", 1),)),
-    (4, (("a20", 3),)),
-    (5, (("a22", 4), ("f2", 1),)),
-    (6, (("f1", 1), ("a20", 4),)),
-    (7, (("a21", 3),)),
-    (8, (("a11", 3), ("f3", 1), ("a12", 4), ("f4", 0), ("a10", 3),)),
-    (9, (("f0", 2), ("f2", 2),)),
-    (11, (("f1", 2), ("f4", 1),)),
-    (12, (("f3", 2),)),
-    (13, (("f5", 2),)),
-    (14, (("f0", 3),)),
-    (15, (("f2", 3),)),
-    (16, (("f1", 3), ("f3", 3),)),
-    (17, (("f4", 2),)),
-    (23, (("f4", 3), ("f5", 3),)),
+    (1, (("a10", 3), ("f1", 0),)),
+    (2, (("a22", 2), ("a11", 3),)),
+    (3, (("f3", 0),)),
+    (4, (("a22", 3), ("a20", 4), ("f1", 1), ("a12", 3),)),
+    (5, (("a21", 4), ("f0", 1), ("f2", 1), ("f3", 1),)),
+    (7, (("a10", 4), ("f1", 2), ("a11", 4),)),
+    (8, (("a12", 4), ("f4", 1), ("a22", 4), ("f0", 2),)),
+    (10, (("f2", 2), ("f1", 3), ("f3", 2), ("f5", 2),)),
+    (11, (("f0", 3),)),
+    (13, (("f4", 2), ("f2", 3), ("f3", 3),)),
+    (14, (("f1", 4),)),
+    (16, (("f0", 4), ("f5", 3),)),
+    (18, (("f4", 3),)),
+    (21, (("f2", 4),)),
+    (22, (("f3", 4),)),
+    (29, (("f5", 4),)),
+    (30, (("f4", 4),)),
 )
 FEED_BACK_PLAN = (
-    (11, (("three0", 0),)),
-    (12, (("three1", 0),)),
-    (13, (("one0", 0),)),
-    (16, (("two0", 0),)),
-    (17, (("three0", 1), ("one1", 0), ("one0", 1),)),
-    (18, (("two1", 0),)),
-    (20, (("three1", 1), ("two0", 1),)),
-    (22, (("one0", 2), ("one2", 0),)),
-    (23, (("one1", 1), ("two2", 0),)),
-    (25, (("three1", 2), ("two1", 1),)),
-    (28, (("one1", 2), ("one2", 1), ("two0", 2),)),
-    (29, (("two2", 1), ("three0", 2),)),
-    (30, (("one1", 3),)),
-    (31, (("two1", 2), ("one2", 2), ("three1", 3),)),
-    (32, (("two2", 2), ("two0", 3), ("one0", 3), ("three0", 3),)),
+    (10, (("three0", 0),)),
+    (11, (("three1", 0),)),
+    (12, (("one0", 0),)),
+    (13, (("two0", 0),)),
+    (15, (("two1", 0), ("one1", 0),)),
+    (16, (("three0", 1),)),
+    (17, (("two0", 1), ("three1", 1),)),
+    (18, (("two2", 0),)),
+    (19, (("one2", 0), ("one0", 1), ("one1", 1), ("three0", 2),)),
+    (21, (("one3", 0),)),
+    (22, (("one0", 2),)),
+    (23, (("two2", 1), ("two0", 2), ("one1", 2), ("two3", 0),)),
+    (24, (("three1", 2),)),
+    (25, (("one2", 1), ("two0", 3),)),
+    (26, (("one3", 1),)),
+    (27, (("two1", 1), ("one0", 3), ("two2", 2),)),
+    (28, (("one1", 3), ("two3", 1),)),
+    (29, (("one2", 2), ("one3", 2),)),
+    (30, (("two2", 3), ("three0", 3),)),
+    (31, (("two1", 2), ("two3", 2), ("one2", 3),)),
+    (32, (("one3", 3), ("three1", 3),)),
     (33, (("two1", 3),)),
-    (34, (("one2", 3), ("two2", 3),)),
+    (34, (("two3", 3),)),
 )
 ATTEND_BACK_PLAN = (
     (4, (("p0", 0),)),
-    (5, (("p1", 0), ("p2", 0),)),
-    (7, (("p3", 0),)),
-    (9, (("p4", 0),)),
-    (10, (("p5", 0), ("p0", 1),)),
-    (11, (("p2", 1), ("p1", 1), ("p6", 0),)),
-    (12, (("p0", 2), ("p3", 1),)),
-    (13, (("p4", 1),)),
-    (14, (("p1", 2), ("p5", 1), ("p2", 2),)),
-    (15, (("p6", 1), ("p3", 2), ("p2", 3),)),
-    (16, (("p1", 3), ("p5", 2), ("p3", 3),)),
-    (17, (("p6", 2), ("p4", 2),)),
-    (18, (("p0", 3), ("p5", 3), ("p6", 3), ("p4", 3),)),
+    (6, (("p1", 0),)),
+    (7, (("p2", 0), ("p3", 0),)),
+    (8, (("p4", 0),)),
+    (9, (("p0", 1),)),
+    (10, (("p5", 0), ("p3", 1), ("p4", 1), ("p1", 1), ("p6", 0),)),
+    (11, (("p2", 1), ("p0", 2),)),
+    (12, (("p4", 2), ("p3", 2), ("p1", 2),)),
+    (13, (("p5", 1), ("p6", 1), ("p2", 2), ("p3", 3),)),
+    (14, (("p0", 3), ("p1", 3),)),
+    (15, (("p6", 2), ("p4", 3), ("p5", 2), ("p2", 3),)),
+    (16, (("p6", 3),)),
+    (17, (("p5", 3),)),
 )
 
 
@@ -639,9 +650,9 @@
 
 
 CHUNK = 256
-PAIRS = (3, 4, 4)
-PAIR_ORDERS = (("x01y", "x01y"), ("y0x1", "x0y1"), ("xy10", "yx01"))
-THREE_ORDERS = ("y10", "0y1")
+PAIRS = (2, 3, 3, 3)
+PAIR_ORDERS = (("xy01", "xy01"), ("xy01", "0xy1"), ("xy01", "xy01"), ("yx01", "xy01"))
+THREE_ORDERS = ("0y1", "y01")
 THREE_AFTER = 0
 
 
@@ -704,8 +715,8 @@
             begin = w * hidden + first * CHUNK
             span = count * CHUNK
             pieces[f"{name}{n}"] = Scatter(
-                sems, links, PAIR_ORDERS[n][w], acc, send.at[n % 2, w], come.at[n, w], recvs,
-                slice(begin, begin + span), slice(0, span),
+                sems, links, PAIR_ORDERS[n][w], acc, send.at[n % 2, w], come, recvs,
+                slice(begin, begin + span), slice(0, span), slice(begin, begin + span),
             )
             ends.append((pieces[f"{name}{n}"], out, first * CHUNK))
         first += count
@@ -715,7 +726,7 @@
         cols = slice(n * half, (n + 1) * half)
         piece = ThreeScatter(
             sems, links[:-1], THREE_ORDERS[n], acc3, send3, take3, (come31, come32, come33),
-            cols, cols,
+            cols, cols, cols,
         )
         piece.last_swap(sems, out_three, last_send, last_come)
         pieces[f"three{n}"] = piece
@@ -887,7 +898,7 @@
             low((2, slab, 2 * hidden)),
             low((slab, 2 * hidden)),
             low((2, 2, 2, 2, 2, 2, slab, span)),
-            low((len(PAIRS), 2, 2, 2, 2, 2, slab, span)),
+            low((2, 2, 2, 2, slab, 2 * hidden)),
             low((2, 2, 2, deep // 2, width)),
             low((2, 2, deep // 2, width)),
             low((2, deep // 2, width)),
@@ -923,8 +934,8 @@
 
 
 WIDE_CHUNK = 512
-PARTS = (1, 2, 1, 1, 2, 1, 2)
-PART_ORDERS = ("yx10", "yx01", "0xy1", "x0y1", "01xy", "yx01", "yx01")
+PARTS = (2, 1, 2, 1, 1, 2, 1)
+PART_ORDERS = ("y0x1", "0xy1", "x0y1", "0xy1", "y01x", "yx01", "x0y1")
 
 
 def attend_weights_kernel(
@@ -955,7 +966,8 @@
         cols = slice(column(first), column(first + count))
         first += count
         pieces[f"p{n}"] = Scatter(
-            sems, links, PART_ORDERS[n], acc, send, come, (come1, come2, come3, come4), cols, cols
+            sems, links, PART_ORDERS[n], acc, send, come, (come1, come2, come3, come4), cols,
+            cols, cols,
         )
         launches[first - 1] = [pieces[f"p{n}"].launch]
     load = [
@@ -1090,15 +1102,15 @@
 
 
 ATTEND_PIECES = (
-    (("a00", "zxy", 7), ("a01", "zyx", 6), ("a02", "1yx0", 3)),
-    (("a10", "zxy", 6), ("a11", "zxy", 7), ("a12", "1xy0", 3)),
-    (("a20", "1y0x", 1), ("a21", "zyx", 7), ("a22", "y1x0", 1)),
+    (("a00", "10xy", 7), ("a01", "10yx", 6), ("a02", "10yx", 3)),
+    (("a10", "10xy", 8), ("a11", "10yx", 5), ("a12", "1y0x", 3)),
+    (("a20", "1x0y", 3), ("a21", "10yx", 4), ("a22", "10xy", 2)),
 )
 FEED_PIECES = (
-    (("f0", "yzx", 6), ("f1", "zyx", 16)),
-    (("f2", "zxy", 11), ("f3", "xzy", 11)),
+    (("f0", "10yx", 11), ("f1", "10xy", 11)),
+    (("f2", "10xy", 13), ("f3", "1y0x", 9)),
 )
-THREE_PIECES = (("f4", "zy", 4), ("f5", "yz", 4))
+THREE_PIECES = (("f4", "10y", 4), ("f5", "y10", 4))
 FORWARD_COPIES = 128
 
 
@@ -1132,7 +1144,7 @@
     steps, per_seq, bits,
     tok, s_key, s_value, s_query, s_gate, s_out, s_gain, s_one, s_two, s_three,
     normed, pre_key, keys, values, pre_query, queries, pre_gate, attended, mixed, residual,
-    normed_two, up_one, up_two, glu, prefix, gain_row, full_attn, full_one, full_two, full_three,
+    normed_two, up_one, up_two, prefix, gain_row, full_attn, full_one, full_two, full_three,
     held, held_one, held_two, all_keys, all_values, all_normed, totals, state_out, state_in, carry,
     three_out, three_in, three_slab, send, recv, local,
 ):
@@ -1151,12 +1163,13 @@
             waves[-1].append(pieces[name])
     feed = []
     for buf, parts in zip((held_one, held_two), FEED_PIECES):
+        feed.append([])
         start = 0
         for name, order, tiles in parts:
             cols = slice(start, start + 128 * tiles)
             start += 128 * tiles
             pieces[name] = Gather(buf, bits, order, sems, cols)
-            feed.append(pieces[name])
+            feed[-1].append(pieces[name])
     start, threes = 0, []
     for n, (name, order, tiles) in enumerate(THREE_PIECES):
         cols = slice(start, start + 128 * tiles)
@@ -1209,19 +1222,20 @@
         column = held[..., 5 * width : 5 * width + 128].reshape(width, 128)
         gain_row[...] = column.astype(WIDE).T[:1]
 
-    for n in range(3):
+    for n in range(4):
 
         @pl.when((step >= n * steps) & (step < (n + 1) * steps))
         def _():
             part = planned(FORWARD_PLAN, pieces, n * steps + 1, (n + 1) * steps + 1)
             run_events(step + 1, part)
 
-    @pl.when(step == 2 * steps)
-    def _():
-        for piece in feed:
-            piece.finish()
-        for copy in keep_feed:
-            copy.start()
+    for n in range(2):
+
+        @pl.when(step == (2 + n) * steps)
+        def _():
+            for piece in feed[n]:
+                piece.finish()
+            keep_feed[n].start()
 
     def weight(n):
         return held[..., n * width : (n + 1) * width].reshape(width, width)
@@ -1298,20 +1312,18 @@
         all_normed[here, :] = rows
         normed_two[...] = rows.T
 
-    @pl.when(step >= 2 * steps)
-    def _():
-        here = pl.ds(pl.multiple_of((step - 2 * steps) * BLOCK, BLOCK), BLOCK)
-        rows = all_normed[here, :]
-        for c in groups(up_one.shape[1]):
-            one = dot_nn(rows, held_one[..., c].reshape(width, GROUP))
-            two = dot_nn(rows, held_two[..., c].reshape(width, GROUP))
-            up_one[:, c] = one.astype(LOW)
-            up_two[:, c] = two.astype(LOW)
-            glu[c, :] = (one * two).astype(LOW).T
-
-    @pl.when(step == 3 * steps - 1)
-    def _():
-        for actions in planned(FORWARD_PLAN, pieces, 3 * steps + 1, 1000).values():
+    for n, (weights, result) in enumerate(((held_one, up_one), (held_two, up_two))):
+
+        @pl.when((step >= (2 + n) * steps) & (step < (3 + n) * steps))
+        def _():
+            at = step - (2 + n) * steps
+            rows = all_normed[pl.ds(pl.multiple_of(at * BLOCK, BLOCK), BLOCK), :]
+            for c in groups(result.shape[1]):
+                result[:, c] = dot_nn(rows, weights[..., c].reshape(width, GROUP)).astype(LOW)
+
+    @pl.when(step == 4 * steps - 1)
+    def _():
+        for actions in planned(FORWARD_PLAN, pieces, 4 * steps + 1, 1000).values():
             for action in actions:
                 action()
         for piece in threes:
@@ -1342,8 +1354,7 @@
     first, second = rows_spec(width, order=phase(0)), rows_spec(width, order=phase(1))
     first_turned = pl.BlockSpec((width, BLOCK), lambda i: (0, phase(0)(i)))
     second_turned = pl.BlockSpec((width, BLOCK), lambda i: (0, phase(1)(i)))
-    third = rows_spec(hidden, order=phase(2))
-    third_turned = pl.BlockSpec((hidden, BLOCK), lambda i: (0, phase(2)(i)))
+    third, fourth = rows_spec(hidden, order=phase(2)), rows_spec(hidden, order=phase(3))
     big_low = jax.ShapeDtypeStruct((row_count, hidden), LOW)
     any_spec = pl.BlockSpec(memory_space=pl.ANY)
     vmem = pl.BlockSpec(memory_space=pltpu.VMEM)
@@ -1355,10 +1366,10 @@
     low = functools.partial(pltpu.VMEM, dtype=LOW)
     out = pl.pallas_call(
         functools.partial(forward_kernel, steps, per_seq, bits),
-        grid=(3 * steps,),
+        grid=(4 * steps,),
         in_specs=[in_rows] + [vmem] * 6 + [any_spec] * 2 + [vmem],
         out_specs=[first_turned] + [first] * 3 + [second] * 4 + [second_turned, second]
-        + [second_turned, third, third, third_turned]
+        + [second_turned, third, fourth]
         + [
             pl.BlockSpec((1, HD, width), lambda i: (phase(1)(i), 0, 0)),
             pl.BlockSpec((1, width), lambda i: (0, 0)),
@@ -1367,7 +1378,7 @@
         out_shape=[turned_low] + [rows_low] * 7 + [turned_low]
         + [
             shape(row_count, width, dtype=WIDE),
-            turned_low, big_low, big_low, shape(hidden, row_count),
+            turned_low, big_low, big_low,
             shape(steps, HD, width),
             shape(1, width, dtype=WIDE),
             shape(*lead, slab, columns),
@@ -1403,11 +1414,11 @@
             flops=28 * row_count * width * width, bytes_accessed=128 << 20, transcendentals=0
         ),
     )(tok, *shards_attn, gain_row, s_one, s_two, s_three)
-    return list(out[:16]) + [
-        out[16].reshape(-1, columns),
+    return list(out[:15]) + [
+        out[15].reshape(-1, columns),
+        out[16].reshape(-1, hidden),
         out[17].reshape(-1, hidden),
-        out[18].reshape(-1, hidden),
-        out[19].reshape(-1, width),
+        out[18].reshape(-1, width),
     ]
 
 
@@ -1553,7 +1564,7 @@
 def feed_step_kernel(
     steps, per_seq, lengths, residual, cotangent, up_one, up_two, all_one, all_two, all_three,
     all_attn, gain, pre_gate, attended, queries,
-    layer_out, grad_one, grad_two, upstream_low, grad_residual, gated, grad_attended,
+    layer_out, glu, grad_one, grad_two, upstream_low, grad_residual, gated, grad_attended,
     totals, grad_gain, product, last_back, last_residual, last_upstream,
     w_one, w_two, w_three, w_out, local,
 ):
@@ -1623,7 +1634,9 @@
             if todo:
                 todo.pop(0)()
             one, two = up_one[:, c].astype(WIDE), up_two[:, c].astype(WIDE)
-            product[:, c] = (one * two).astype(LOW)
+            both = (one * two).astype(LOW)
+            product[:, c] = both
+            glu[c, :] = both.T
             grad_one[:, c] = (back * two).astype(LOW)
             grad_two[:, c] = (back * one).astype(LOW)
         for part in todo:
@@ -1674,6 +1687,9 @@
     narrow = ((row_count, width), LOW, rows)
     big = ((row_count, hidden), LOW, rows_spec(hidden, order=now))
 
+    turned = (
+        (hidden, row_count), LOW, pl.BlockSpec((hidden, BLOCK), lambda i: (0, now(i)))
+    )
     state_spec = pl.BlockSpec((1, HD, width), lambda i: (last(i) // per_seq, 0, 0))
     hbm = pl.BlockSpec(memory_space=pl.ANY)
     return call(
@@ -1683,7 +1699,7 @@
          (up_one, big[2]), (up_two, big[2]),
          (full_one, hbm), (full_two, hbm), (full_three, hbm), (full_attn, hbm),
          (gain, whole_spec(gain)), (pre_gate, done), (attended, done), (queries, done)],
-        [narrow, big, big, narrow,
+        [narrow, turned, big, big, narrow,
          ((row_count, width), WIDE, done),
          ((row_count, 2 * width), LOW, rows_spec(2 * width, order=last)),
          ((row_count, width), LOW, done),
@@ -1719,14 +1735,14 @@
     cot = cotangent.reshape(row_count, width)
     (
         normed_low, pre_key, keys, values, pre_query, queries, pre_gate, attended, mixed,
-        residual, normed_two, up_one, up_two, glu, prefix, gain, full_attn, full_one, full_two,
+        residual, normed_two, up_one, up_two, prefix, gain, full_attn, full_one, full_two,
         full_three,
     ) = forward(
         tok, seq_count, (w_key, w_value, w_query, w_gate, w_out), out_gain[None, :], w_one, w_two, w_three
     )
 
     (
-        layer_out, grad_up_one, grad_up_two, upstream_low, grad_residual, gated,
+        layer_out, glu, grad_up_one, grad_up_two, upstream_low, grad_residual, gated,
         grad_attended, grad_totals, grad_gain_term,
     ) = feed(
         seq_count, lengths, residual, cot, up_one, up_two, full_one, full_two, full_three,

time: 425 us -> 417 us (0.981)
  Pallas kernels: 405 us -> 397 us
    pallas_call x1, Pallas kernels: 110 us -> 104 us  [feed_back(): pl.pallas_call(functools.partial(feed_back_kernel, per_seq, bits), grid=(...]
    pallas_call x1, Pallas kernels: 74.3 us -> 69.7 us  [attend_weights(): pl.pallas_call(functools.partial(attend_weights_kernel, bits), grid=(chun...]
where the time goes in v6:
time: 417 us; the launch traced here: 410 us
  Pallas kernels  397 us (95%)
  other arithmetic  6.72 us (2%)
  local copies, waits for them, and re-layouts  5.56 us (1%)
    pallas_call x1, Pallas kernels, forward(): pl.pallas_call(functools.partial(forward_kernel, steps, per_seq, bits), g...  148 us
    pallas_call x1, Pallas kernels, feed_back(): pl.pallas_call(functools.partial(feed_back_kernel, per_seq, bits), grid=(...  104 us
    pallas_call x1, Pallas kernels, call(): pl.pallas_call(kernel, grid=(steps,), in_specs=[spec for _, spec in opera...  74.2 us
    pallas_call x1, Pallas kernels, attend_weights(): pl.pallas_call(functools.partial(attend_weights_kernel, bits), grid=(chun...  69.7 us

profile of v6, /device:TPU:0, one launch (start us, length us, event | category | flops | bytes accessed | tf_op | source)
XLA Modules:
  0.0 410.0 jit_solution(4447712552667286754)
XLA Ops:
  0.6 148.4 %shard_map.203 = (bf16[1024,2048]{1,0:T(8,128)(2,1)}, bf16[2048,1024]{1,0:T(8,128)(2,1)}, bf16[2048,1024]{1,0:T(8,128)(2,1)}, bf16[2048,1024]{1,0:T(8,128)(2,1)}...) custom-call(bf16[2048,1024]{1,0:T(8,128)(2,1)} %bitcast.12, ...), custom_call_target="tpu_custom_call" | custom-call | flops 60129542144 | bytes 134217728 | tf_op jit(solution)/shard_map/pallas_call | solution.py:1367
  149.1 74.2 %shard_map.204 = (bf16[2048,1024]{1,0:T(8,128)(2,1)}, bf16[2816,2048]{1,0:T(8,128)(2,1)}, bf16[2048,2816]{1,0:T(8,128)(2,1)}, bf16[2048,2816]{1,0:T(8,128)(2,1)}...) custom-call(s32[2]{0:T(128)} %refs_0_.1, ...), custom_call_target="tpu_custom_call" | custom-call | flops 51539607552 | bytes 76288008 | tf_op jit(solution)/shard_map/pallas_call | solution.py:323
  223.3 104.4 %shard_map.205 = (f32[32,2816]{1,0:T(8,128)}, f32[32,2816]{1,0:T(8,128)}, f32[88,1024]{1,0:T(8,128)}, bf16[2048,3072]{1,0:T(8,128)(2,1)}) custom-call(bf16[1024,2048]{1,0:T(8,128)(2,1)} %get-tuple-element.61.normed_hbm, bf16[2048,2816]{1,0:T(8,128)(2,1)} %get-tuple-element.62.grad_one, bf16[2048,2816]{1,0:T(8,128)(2,1)} %get-tuple-element.63.grad_two, ...), custom_call_target="tpu_custom_call" | custom-call | flops 61203283968 | bytes 134217728 | tf_op jit(solution)/shard_map/pallas_call | solution.py:875
  327.7 69.7 %shard_map.206 = (f32[32,5248]{1,0:T(8,128)}, bf16[2048,1024]{1,0:T(8,128)(2,1)}) custom-call(bf16[1024,2048]{1,0:T(8,128)(2,1)} %get-tuple-element.58.normed_hbm, bf16[1024,2048]{1,0:T(8,128)(2,1)} %get-tuple-element.59.mixed_hbm, bf16[2048,2048]{1,0:T(8,128)(2,1)} %get-tuple-element.60.gated.rows_gate, ...), custom_call_target="tpu_custom_call" | custom-call | flops 38654705664 | bytes 67108864 | tf_op jit(solution)/shard_map/pallas_call | solution.py:1066
  397.4 1.3 slice_reduce_fusion
  398.8 2.0 fusion
  400.8 0.0 copy-start.2
  400.8 0.0 copy-start.1
  400.8 0.0 copy-start
  400.8 6.7 %convert.1 = f32[2,1024,1024]{2,1,0:T(8,128)} convert(bf16[2,1024,1024]{2,1,0:T(8,128)(2,1)} %bitcast.10) | non-fusion elementwise | flops 2097152 | bytes 12582912 | tf_op jit(solution)/shard_map/reshape | solution.py:1764
  407.5 0.0 copy-done.2
  407.5 0.7 copy.26
  408.3 0.0 copy-done.1
  408.3 0.7 copy.27
  409.0 0.0 copy-done
  409.0 0.7 copy.28
Async XLA Ops:
  400.8 6.7 %copy-start.2 = (f32[32,2816]{1,0:T(8,128)S(1)}, f32[32,2816]{1,0:T(8,128)}, u32[]{:S(2)}) copy-start(f32[32,2816]{1,0:T(8,128)} %get-tuple-element.105) | copy-start | bytes 1081348
  400.8 7.5 %copy-start.1 = (f32[32,2816]{1,0:T(8,128)S(1)}, f32[32,2816]{1,0:T(8,128)}, u32[]{:S(2)}) copy-start(f32[32,2816]{1,0:T(8,128)} %get-tuple-element.106) | copy-start | bytes 1081348
  400.8 8.2 %copy-start = (f32[88,1024]{1,0:T(8,128)S(1)}, f32[88,1024]{1,0:T(8,128)}, u32[]{:S(2)}) copy-start(f32[88,1024]{1,0:T(8,128)} %get-tuple-element.107) | copy-start | bytes 1081348

commit v7 on v6

--- a/solution.py
+++ b/solution.py
@@ -119,7 +119,7 @@
 
 
 def silu_slope(pre_rows):
-    logistic = jax.nn.sigmoid(pre_rows)
+    logistic = pl.reciprocal(1.0 + jnp.exp(-pre_rows), approx=True)
     return logistic * (1.0 + pre_rows * (1.0 - logistic))
 
 

time: 417 us -> 417 us (level)
  no operation moved by 1% of the time
where the time goes in v7:
time: 417 us; the launch traced here: 410 us
  Pallas kernels  397 us (95%)
  other arithmetic  6.72 us (2%)
  local copies, waits for them, and re-layouts  5.56 us (1%)
    pallas_call x1, Pallas kernels, forward(): pl.pallas_call(functools.partial(forward_kernel, steps, per_seq, bits), g...  148 us
    pallas_call x1, Pallas kernels, feed_back(): pl.pallas_call(functools.partial(feed_back_kernel, per_seq, bits), grid=(...  104 us
    pallas_call x1, Pallas kernels, call(): pl.pallas_call(kernel, grid=(steps,), in_specs=[spec for _, spec in opera...  74.2 us
    pallas_call x1, Pallas kernels, attend_weights(): pl.pallas_call(functools.partial(attend_weights_kernel, bits), grid=(chun...  69.7 us

profile of v7, /device:TPU:0, one launch (start us, length us, event | category | flops | bytes accessed | tf_op | source)
XLA Modules:
  0.0 409.9 jit_solution(11100956840019488627)
XLA Ops:
  0.6 148.4 %shard_map.203 = (bf16[1024,2048]{1,0:T(8,128)(2,1)}, bf16[2048,1024]{1,0:T(8,128)(2,1)}, bf16[2048,1024]{1,0:T(8,128)(2,1)}, bf16[2048,1024]{1,0:T(8,128)(2,1)}...) custom-call(bf16[2048,1024]{1,0:T(8,128)(2,1)} %bitcast.12, ...), custom_call_target="tpu_custom_call" | custom-call | flops 60129542144 | bytes 134217728 | tf_op jit(solution)/shard_map/pallas_call | solution.py:1367
  149.1 74.2 %shard_map.204 = (bf16[2048,1024]{1,0:T(8,128)(2,1)}, bf16[2816,2048]{1,0:T(8,128)(2,1)}, bf16[2048,2816]{1,0:T(8,128)(2,1)}, bf16[2048,2816]{1,0:T(8,128)(2,1)}...) custom-call(s32[2]{0:T(128)} %refs_0_.1, ...), custom_call_target="tpu_custom_call" | custom-call | flops 51539607552 | bytes 76288008 | tf_op jit(solution)/shard_map/pallas_call | solution.py:323
  223.3 104.4 %shard_map.205 = (f32[32,2816]{1,0:T(8,128)}, f32[32,2816]{1,0:T(8,128)}, f32[88,1024]{1,0:T(8,128)}, bf16[2048,3072]{1,0:T(8,128)(2,1)}) custom-call(bf16[1024,2048]{1,0:T(8,128)(2,1)} %get-tuple-element.61.normed_hbm, bf16[2048,2816]{1,0:T(8,128)(2,1)} %get-tuple-element.62.grad_one, bf16[2048,2816]{1,0:T(8,128)(2,1)} %get-tuple-element.63.grad_two, ...), custom_call_target="tpu_custom_call" | custom-call | flops 61203283968 | bytes 134217728 | tf_op jit(solution)/shard_map/pallas_call | solution.py:875
  327.7 69.7 %shard_map.206 = (f32[32,5248]{1,0:T(8,128)}, bf16[2048,1024]{1,0:T(8,128)(2,1)}) custom-call(bf16[1024,2048]{1,0:T(8,128)(2,1)} %get-tuple-element.58.normed_hbm, bf16[1024,2048]{1,0:T(8,128)(2,1)} %get-tuple-element.59.mixed_hbm, bf16[2048,2048]{1,0:T(8,128)(2,1)} %get-tuple-element.60.gated.rows_gate, ...), custom_call_target="tpu_custom_call" | custom-call | flops 38654705664 | bytes 67108864 | tf_op jit(solution)/shard_map/pallas_call | solution.py:1066
  397.4 1.3 slice_reduce_fusion
  398.7 2.0 fusion
  400.7 0.0 copy-start.2
  400.7 0.0 copy-start.1
  400.7 0.0 copy-start
  400.7 6.7 %convert.1 = f32[2,1024,1024]{2,1,0:T(8,128)} convert(bf16[2,1024,1024]{2,1,0:T(8,128)(2,1)} %bitcast.10) | non-fusion elementwise | flops 2097152 | bytes 12582912 | tf_op jit(solution)/shard_map/reshape | solution.py:1764
  407.4 0.0 copy-done.2
  407.4 0.7 copy.26
  408.2 0.0 copy-done.1
  408.2 0.7 copy.27
  408.9 0.0 copy-done
  408.9 0.7 copy.28
Async XLA Ops:
  400.7 6.7 %copy-start.2 = (f32[32,2816]{1,0:T(8,128)S(1)}, f32[32,2816]{1,0:T(8,128)}, u32[]{:S(2)}) copy-start(f32[32,2816]{1,0:T(8,128)} %get-tuple-element.105) | copy-start | bytes 1081348
  400.7 7.5 %copy-start.1 = (f32[32,2816]{1,0:T(8,128)S(1)}, f32[32,2816]{1,0:T(8,128)}, u32[]{:S(2)}) copy-start(f32[32,2816]{1,0:T(8,128)} %get-tuple-element.106) | copy-start | bytes 1081348
  400.7 8.2 %copy-start = (f32[88,1024]{1,0:T(8,128)S(1)}, f32[88,1024]{1,0:T(8,128)}, u32[]{:S(2)}) copy-start(f32[88,1024]{1,0:T(8,128)} %get-tuple-element.107) | copy-start | bytes 1081348
